TPU v7x, 32 devices: a whole 2x2x4 slice. The times are simulated.
32 devices in a mesh: seq: 8 (over y, x, core), dp: 4 (over z).
Axes of the slice: x: 2, y: 2, z: 4, core: 2. Of those that a mesh axis runs over, the one named last changes fastest.
Arguments:
- inputs: bfloat16 [8, 2048, 768], P('dp', 'seq'), may hold values from -6 to 6
- w_query: bfloat16 [768, 768], P(('seq', 'dp')), may hold values from -0.21875 to 0.21875
- w_keyval: bfloat16 [768, 128], P(('seq', 'dp')), may hold values from -0.21875 to 0.21875
- w_out: bfloat16 [768, 768], P(('seq', 'dp')), may hold values from -2.5 to 2.5
- w_up: bfloat16 [768, 3072], P(('seq', 'dp')), may hold values from -0.21875 to 0.21875
- w_down: bfloat16 [3072, 768], P(('seq', 'dp')), may hold values from -0.109375 to 0.109375
- norm_gain: bfloat16 [768, 2], P(('seq', 'dp')), may hold values from 0.099609375 to 1.8984375
- norm_bias: bfloat16 [768, 2], P(('seq', 'dp')), may hold values from -1.5 to 1.5
- out_cotangent: bfloat16 [8, 2048, 768], P('dp', 'seq'), may hold values from -6 to 6
- kv_cotangent: bfloat16 [8, 2048, 128], P('dp', 'seq'), may hold values from -6 to 6
Outputs:
- output: bfloat16 [8, 2048, 768], P('dp', 'seq')
- keyval: bfloat16 [8, 2048, 128], P('dp', 'seq')
- grad_inputs: float32 [8, 2048, 768], P('dp', 'seq')
- grad_query: float32 [768, 768], P(('seq', 'dp'))
- grad_keyval: float32 [768, 128], P(('seq', 'dp'))
- grad_out: float32 [768, 768], P(('seq', 'dp'))
- grad_up: float32 [768, 3072], P(('seq', 'dp'))
- grad_down: float32 [3072, 768], P(('seq', 'dp'))
- grad_gain: float32 [768, 2], P(('seq', 'dp'))
- grad_bias: float32 [768, 2], P(('seq', 'dp'))
All inputs are finite; a program needn't handle non-finite values.
Results may differ from a plain program's by a relative error of at most 0.011.
Values may be sent and summed in bfloat16 or wider, within the bound.
No kernel may reach another device: no remote copies, remote signals or barrier semaphores. Data moves between devices by JAX's collectives and lax.ppermute only.
A program may use at most 128 MiB of HBM per device.

v0:
```python
import math

import jax
import jax.numpy as jnp
from jax import lax
from jax.sharding import PartitionSpec as P

D = 768
HEADS = 12
HEAD = 64
ROT = 16


epsilon = 1e-05
negative = -1e30


def layer_norm(values, gain, shift):
    center = values - jnp.mean(values, axis=-1, keepdims=True)
    spread = jnp.mean(center * center, axis=-1, keepdims=True)
    return center * lax.rsqrt(spread + epsilon) * gain + shift


def rotate(values, positions):
    half_rot = ROT // 2
    exponent = jnp.arange(half_rot, dtype=jnp.float32) * (2.0 / ROT)
    frequency = jnp.exp(-math.log(10000.0) * exponent)
    angles = (positions.astype(jnp.float32) * 0.25)[:, None] * frequency[None, :]
    cos_table = jnp.cos(angles)[:, None, :]
    sin_table = jnp.sin(angles)[:, None, :]
    first = values[..., :half_rot]
    second = values[..., half_rot:ROT]
    return jnp.concatenate(
        [
            first * cos_table - second * sin_table,
            second * cos_table + first * sin_table,
            values[..., ROT:],
        ],
        axis=-1,
    )


def split_blocks(piece):
    count = piece.shape[0]
    block = 512
    offsets = jnp.arange(count // block, dtype=jnp.int32) * block
    return (piece.reshape(count // block, block, piece.shape[1]), offsets, block)


def matmul_t(left, right):
    return lax.dot_general(
        left, right, (((0,), (0,)), ((), ())), preferred_element_type=jnp.float32
    )


def matmul_rt(left, right):
    return lax.dot_general(
        left, right, (((1,), (1,)), ((), ())), preferred_element_type=jnp.float32
    )


def on_device(
    inputs,
    w_query,
    w_keyval,
    w_out,
    w_up,
    w_down,
    norm_gain,
    norm_bias,
    out_cotangent,
    kv_cotangent,
):
    weights = (
        lax.all_gather(w_query, ("seq", "dp"), axis=0, tiled=True),
        lax.all_gather(w_keyval, ("seq", "dp"), axis=0, tiled=True),
        lax.all_gather(w_out, ("seq", "dp"), axis=0, tiled=True),
        lax.all_gather(w_up, ("seq", "dp"), axis=0, tiled=True),
        lax.all_gather(w_down, ("seq", "dp"), axis=0, tiled=True),
        lax.all_gather(norm_gain, ("seq", "dp"), axis=0, tiled=True),
        lax.all_gather(norm_bias, ("seq", "dp"), axis=0, tiled=True),
    )
    full_query, full_keyval, full_out, full_up, full_down, full_gain, full_bias = weights
    micro_count, row_count, _ = inputs.shape
    seq_rank = lax.axis_index("seq")
    positions = seq_rank * row_count + jnp.arange(row_count, dtype=jnp.int32)
    last_query = seq_rank * row_count + row_count - 1
    scale = 1.0 / math.sqrt(HEAD)
    gain_attn = full_gain[:, 0].astype(jnp.float32)
    gain_mlp = full_gain[:, 1].astype(jnp.float32)
    bias_attn = full_bias[:, 0].astype(jnp.float32)
    bias_mlp = full_bias[:, 1].astype(jnp.float32)
    outputs = []
    keyvals = []
    saved = []
    for batch_index in range(micro_count):
        tokens = inputs[batch_index].astype(jnp.float32)
        normed_attn = layer_norm(tokens, gain_attn, bias_attn).astype(jnp.bfloat16)
        normed_mlp = layer_norm(tokens, gain_mlp, bias_mlp).astype(jnp.bfloat16)
        query_pre = jnp.dot(normed_attn, full_query, preferred_element_type=jnp.float32)
        queries = rotate(query_pre.reshape(row_count, HEADS, HEAD), positions).astype(jnp.bfloat16)
        keyval_pre = jnp.dot(normed_attn, full_keyval, preferred_element_type=jnp.float32)
        keys_rot = rotate(keyval_pre[:, None, :HEAD], positions)[:, 0, :]
        keyval = jnp.concatenate([keys_rot, keyval_pre[:, HEAD:]], axis=-1).astype(jnp.bfloat16)

        def forward_fold(carry, piece):
            blocks, offsets, block = split_blocks(piece)

            def forward_step(state, item):
                part, offset = item

                def forward_live(inner):
                    peak, total, accum = inner
                    scores = (
                        jnp.einsum(
                            "qhd,kd->hqk",
                            queries,
                            part[:, :HEAD],
                            preferred_element_type=jnp.float32,
                        )
                        * scale
                    )
                    key_pos = offset + jnp.arange(block, dtype=jnp.int32)
                    allowed = (key_pos[None, :] <= positions[:, None])[None]
                    scores = jnp.where(allowed, scores, negative)
                    new_peak = jnp.maximum(peak, jnp.max(scores, axis=-1))
                    ratio = jnp.exp(peak - new_peak)
                    probs = jnp.where(allowed, jnp.exp(scores - new_peak[..., None]), 0.0)
                    total = total * ratio + jnp.sum(probs, axis=-1)
                    accum = accum * ratio[..., None] + jnp.einsum(
                        "hqk,kd->hqd",
                        probs.astype(jnp.bfloat16),
                        part[:, HEAD:],
                        preferred_element_type=jnp.float32,
                    )
                    return (new_peak, total, accum)

                return (
                    lax.cond(offset <= last_query, forward_live, lambda inner: inner, state),
                    None,
                )

            carry, _ = lax.scan(forward_step, carry, (blocks, offsets))
            return carry

        start_state = (
            jnp.full((HEADS, row_count), negative, jnp.float32),
            jnp.zeros((HEADS, row_count), jnp.float32),
            jnp.zeros((HEADS, row_count, HEAD), jnp.float32),
        )
        peak, total, accum = forward_fold(
            start_state, lax.all_gather(keyval, "seq", axis=0, tiled=True)
        )
        context_pre = jnp.transpose(accum / total[..., None], (1, 0, 2))
        logsum = peak + jnp.log(total)
        context = context_pre.reshape(row_count, D).astype(jnp.bfloat16)
        attn_out = jnp.dot(context, full_out, preferred_element_type=jnp.float32)
        hidden_pre = jnp.dot(normed_mlp, full_up, preferred_element_type=jnp.float32)
        hidden = jax.nn.gelu(hidden_pre, approximate=False).astype(jnp.bfloat16)
        mlp_out = jnp.dot(hidden, full_down, preferred_element_type=jnp.float32)
        outputs.append((tokens + attn_out + mlp_out).astype(jnp.bfloat16))
        keyvals.append(keyval)
        saved.append(
            (
                normed_attn,
                normed_mlp,
                queries,
                keyval,
                context_pre,
                context,
                logsum,
                hidden_pre,
                hidden,
            )
        )
    back_weights = (
        lax.all_gather(w_query, ("seq", "dp"), axis=0, tiled=True),
        lax.all_gather(w_keyval, ("seq", "dp"), axis=0, tiled=True),
        lax.all_gather(w_out, ("seq", "dp"), axis=0, tiled=True),
        lax.all_gather(w_up, ("seq", "dp"), axis=0, tiled=True),
        lax.all_gather(w_down, ("seq", "dp"), axis=0, tiled=True),
        lax.all_gather(norm_gain, ("seq", "dp"), axis=0, tiled=True),
        lax.all_gather(norm_bias, ("seq", "dp"), axis=0, tiled=True),
    )
    back_query, back_keyval, back_out, back_up, back_down, back_gain, back_bias = back_weights
    gain_attn = back_gain[:, 0].astype(jnp.float32)
    gain_mlp = back_gain[:, 1].astype(jnp.float32)
    bias_attn = back_bias[:, 0].astype(jnp.float32)
    bias_mlp = back_bias[:, 1].astype(jnp.float32)

    def rotate_back(grads):
        _, pullback = jax.vjp(lambda field: rotate(field, positions), grads)
        return pullback(grads)[0]

    totals = None
    grad_rows = []
    for batch_index in range(micro_count):
        (
            normed_attn,
            normed_mlp,
            queries,
            keyval,
            context_pre,
            context,
            logsum,
            hidden_pre,
            hidden,
        ) = saved[batch_index]
        tokens = inputs[batch_index].astype(jnp.float32)
        cotangent = out_cotangent[batch_index]
        cotangent_f = cotangent.astype(jnp.float32)
        grad_down_local = matmul_t(hidden, cotangent)
        d_hidden = matmul_rt(cotangent, back_down)
        _, gelu_back = jax.vjp(lambda field: jax.nn.gelu(field, approximate=False), hidden_pre)
        d_hidden_pre = gelu_back(d_hidden)[0].astype(jnp.bfloat16)
        grad_up_local = matmul_t(normed_mlp, d_hidden_pre)
        d_normed_mlp = matmul_rt(d_hidden_pre, back_up)
        grad_out_local = matmul_t(context, cotangent)
        d_context = (
            matmul_rt(cotangent, back_out).astype(jnp.bfloat16).reshape(row_count, HEADS, HEAD)
        )
        delta = jnp.transpose(jnp.sum(d_context.astype(jnp.float32) * context_pre, axis=-1), (1, 0))
        backward_piece = lax.all_gather(keyval, "seq", axis=0, tiled=True)
        d_queries = jnp.zeros((HEADS, row_count, HEAD), jnp.float32)
        backward_blocks, backward_offsets, backward_block = split_blocks(backward_piece)

        def backward_step(acc_queries, item):
            part, offset = item
            keys = part[:, :HEAD]
            values = part[:, HEAD:]

            def backward_live(acc):
                scores = (
                    jnp.einsum("qhd,kd->hqk", queries, keys, preferred_element_type=jnp.float32)
                    * scale
                )
                key_pos = offset + jnp.arange(backward_block, dtype=jnp.int32)
                allowed = (key_pos[None, :] <= positions[:, None])[None]
                probs = jnp.where(allowed, jnp.exp(scores - logsum[..., None]), 0.0)
                d_probs = jnp.einsum(
                    "qhd,kd->hqk", d_context, values, preferred_element_type=jnp.float32
                )
                d_scores = (probs * (d_probs - delta[..., None])).astype(jnp.bfloat16)
                acc = (
                    acc
                    + jnp.einsum("hqk,kd->hqd", d_scores, keys, preferred_element_type=jnp.float32)
                    * scale
                )
                d_keys = (
                    jnp.einsum("hqk,qhd->kd", d_scores, queries, preferred_element_type=jnp.float32)
                    * scale
                )
                d_values = jnp.einsum(
                    "hqk,qhd->kd",
                    probs.astype(jnp.bfloat16),
                    d_context,
                    preferred_element_type=jnp.float32,
                )
                return (acc, jnp.concatenate([d_keys, d_values], axis=-1))

            def dead(acc):
                return (acc, jnp.zeros((backward_block, 2 * HEAD), jnp.float32))

            return lax.cond(offset <= last_query, backward_live, dead, acc_queries)

        d_queries, pieces = lax.scan(backward_step, d_queries, (backward_blocks, backward_offsets))
        count = backward_piece.shape[0]
        d_keyval = pieces.reshape(count, 2 * HEAD)
        d_queries, d_keyval_all = (d_queries, d_keyval)
        d_keyval_own = lax.psum_scatter(
            d_keyval_all.astype(jnp.bfloat16), "seq", scatter_dimension=0, tiled=True
        ).astype(jnp.float32)
        d_keyval_own = d_keyval_own + kv_cotangent[batch_index].astype(jnp.float32)
        d_query_pre = (
            rotate_back(jnp.transpose(d_queries, (1, 0, 2)))
            .reshape(row_count, D)
            .astype(jnp.bfloat16)
        )
        d_keys_pre = rotate_back(d_keyval_own[:, None, :HEAD])[:, 0, :]
        d_keyval_pre = jnp.concatenate([d_keys_pre, d_keyval_own[:, HEAD:]], axis=-1).astype(
            jnp.bfloat16
        )
        grad_query_local = matmul_t(normed_attn, d_query_pre)
        grad_keyval_local = matmul_t(normed_attn, d_keyval_pre)
        d_normed_attn = matmul_rt(d_query_pre, back_query) + matmul_rt(d_keyval_pre, back_keyval)
        _, norm_back_attn = jax.vjp(layer_norm, tokens, gain_attn, bias_attn)
        d_tokens_attn, d_gain_attn, d_bias_attn = norm_back_attn(d_normed_attn)
        _, norm_back_mlp = jax.vjp(layer_norm, tokens, gain_mlp, bias_mlp)
        d_tokens_mlp, d_gain_mlp, d_bias_mlp = norm_back_mlp(d_normed_mlp)
        grad_rows.append(cotangent_f + d_tokens_attn + d_tokens_mlp)
        local = (
            grad_query_local,
            grad_keyval_local,
            grad_out_local,
            grad_up_local,
            grad_down_local,
            jnp.stack([d_gain_attn, d_gain_mlp], axis=1),
            jnp.stack([d_bias_attn, d_bias_mlp], axis=1),
        )
        totals = local if totals is None else jax.tree.map(jnp.add, totals, local)
    totals = lax.psum_scatter(totals, ("seq", "dp"), scatter_dimension=0, tiled=True)
    grad_query, grad_keyval, grad_out, grad_up, grad_down, grad_gain, grad_bias = totals
    return (
        jnp.stack(outputs),
        jnp.stack(keyvals),
        jnp.stack(grad_rows),
        grad_query,
        grad_keyval,
        grad_out,
        grad_up,
        grad_down,
        grad_gain,
        grad_bias,
    )


def solution(mesh):
    return jax.shard_map(
        on_device,
        mesh=mesh,
        in_specs=(
            P("dp", "seq", None),
            P(("seq", "dp"), None),
            P(("seq", "dp"), None),
            P(("seq", "dp"), None),
            P(("seq", "dp"), None),
            P(("seq", "dp"), None),
            P(("seq", "dp"), None),
            P(("seq", "dp"), None),
            P("dp", "seq", None),
            P("dp", "seq", None),
        ),
        out_specs=(
            P("dp", "seq", None),
            P("dp", "seq", None),
            P("dp", "seq", None),
            P(("seq", "dp"), None),
            P(("seq", "dp"), None),
            P(("seq", "dp"), None),
            P(("seq", "dp"), None),
            P(("seq", "dp"), None),
            P(("seq", "dp"), None),
            P(("seq", "dp"), None),
        ),
        check_vma=False,
    )
```

profile of v0, /device:TPU:0, one launch (start us, length us, event | category | flops | bytes accessed | tf_op | source)
XLA Modules:
  0.0 1177.5 jit_solution(15523842783060434556)
XLA Ops:
  8.7 1.3 convert_reduce_fusion.1
  10.0 1.5 fusion.121
  11.6 69.5 %all-gather = bf16[32,24,2]{1,2,0:T(2,128)(2,1)S(1)} all-gather(bf16[1,24,2]{1,2,0:T(2,128)(2,1)} %bitcast.454), channel_id=1, replica_groups=mesh['seq'=8,'dp'=4] {'seq','dp'}, dimensions={0}, use_global_device_ids=true | all-gather | bytes 3168 | tf_op jit(solution)/shard_map/all_gather | solution.py:80
  81.2 63.2 %all-gather.1 = bf16[32,24,2]{1,2,0:T(2,128)(2,1)S(1)} all-gather(bf16[1,24,2]{1,2,0:T(2,128)(2,1)} %bitcast.455), channel_id=1, replica_groups=mesh['seq'=8,'dp'=4] {'seq','dp'}, dimensions={0}, use_global_device_ids=true | all-gather | bytes 3168 | tf_op jit(solution)/shard_map/all_gather | solution.py:81
  144.5 67.3 %all_gather.37 = bf16[768,128]{1,0:T(8,128)(2,1)S(1)} all-gather(bf16[24,128]{1,0:T(8,128)(2,1)} %param.28), channel_id=1, replica_groups=mesh['seq'=8,'dp'=4] {'seq','dp'}, dimensions={0}, use_global_device_ids=true | all-gather | bytes 202752 | tf_op jit(solution)/shard_map/all_gather | solution.py:76
  212.5 1.4 fusion.218
  215.3 9.9 all_gather.38
  226.6 11.3 all_gather.43
  238.6 1.7 copy.74
  242.2 13.7 %while.62 = (s32[]{:T(128)}, f32[12,256]{1,0:T(8,128)S(1)}, f32[12,256]{1,0:T(8,128)S(1)}, f32[12,256,64]{1,2,0:T(8,128)S(1)}, s32[4]{0:T(128)}, /*index=5*/s32[...) while((s32[]{:T(128)}, f32[12,256]{1,0:T(8,128)S(1)}, ...), condition=%wide.region_7.8_spmd.clone, body=%wide.region_2.7_spmd.clone.sunk | while | flops 423631616 | bytes 21971212 | solution.py:143
  244.1 6.2 conditional.12
  246.9 1.5 fusion.10
  248.4 1.8 fusion.14
  255.9 3.1 fusion.150
  259.0 2.5 convolution_convert_fusion.1
  261.5 1.9 copy.77
  265.5 18.0 %while.64 = (s32[]{:T(128)}, f32[12,256,64]{1,2,0:T(8,128)S(1)}, bf16[4,512,128]{1,2,0:T(8,128)(2,1)}, s32[4]{0:T(128)}, s32[]{:T(128)}, /*index=5*/bf16[4,512,1...) while((s32[]{:T(128)}, f32[12,256,64]{1,2,0:T(8,128)S(1)}, ...), condition=%wide.region_20.21_spmd.clone, body=%wide.region_17.20_spmd.clone.sunk | while | flops 1023214336 | bytes 34591512 | solution.py:266
  267.4 7.8 conditional.14
  270.1 1.9 fusion.35
  273.1 1.3 fusion.43
  284.6 1.6 multiply_add_fusion.5
  287.2 14.8 %while.63 = (s32[]{:T(128)}, f32[12,256]{1,0:T(8,128)S(1)}, f32[12,256]{1,0:T(8,128)S(1)}, f32[12,256,64]{1,2,0:T(8,128)}, s32[4]{0:T(128)}, /*index=5*/s32[]{:T...) while((s32[]{:T(128)}, f32[12,256]{1,0:T(8,128)S(1)}, ...), condition=%wide.region_15.16_spmd.clone, body=%wide.region_10.15_spmd.clone.sunk | while | flops 423631616 | bytes 21971212 | solution.py:143
  289.3 7.2 conditional.13
  291.2 1.5 fusion.23
  292.7 3.7 fusion.27
  302.1 2.5 convolution_convert_fusion
  305.8 2.0 copy.102
  307.9 1.9 fusion.132
  311.3 19.5 %while.65 = (s32[]{:T(128)}, f32[12,256,64]{1,2,0:T(8,128)S(1)}, bf16[4,512,128]{1,2,0:T(8,128)(2,1)}, s32[4]{0:T(128)}, s32[]{:T(128)}, /*index=5*/bf16[4,512,1...) while((s32[]{:T(128)}, f32[12,256,64]{1,2,0:T(8,128)S(1)}, ...), condition=%wide.region_30.31_spmd.clone, body=%wide.region_27.30_spmd.clone.sunk | while | flops 1023214336 | bytes 34693992 | solution.py:266
  313.7 7.0 conditional.15
  315.6 1.9 fusion.51
  318.7 1.3 fusion.59
  330.8 2.0 copy.103
  336.5 2.1 fusion.155
  338.5 64.1 %reduce-scatter.12.cloned.1.call-done = bf16[256,128]{0,1:T(8,128)(2,1)} async-done(((bf16[2048,128]{0,1:T(8,128)(2,1)}), bf16[256,128]{0,1:T(8,128)(2,1)}) %reduce-scatter.12.cloned.1.call-update) | async-done | bytes 65552 | tf_op jit(solution)/shard_map/reduce_scatter | solution.py:270
  403.6 44.8 %reduce-scatter.14.cloned.1.call-done = bf16[256,128]{0,1:T(8,128)(2,1)} async-done(((bf16[2048,128]{0,1:T(8,128)(2,1)}), bf16[256,128]{0,1:T(8,128)(2,1)}) %reduce-scatter.14.cloned.1.call-update) | async-done | bytes 65552 | tf_op jit(solution)/shard_map/reduce_scatter | solution.py:270
  453.0 2.1 convolution_add_fusion.3
  455.3 1.3 bitcast_convert_fusion
  457.3 1.9 convolution_add_fusion.2
  459.3 55.3 %all-gather.11.cloned.1.call-done = bf16[768,3072]{1,0:T(8,128)(2,1)} async-done(((bf16[24,3072]{1,0:T(8,128)(2,1)}), bf16[768,3072]{1,0:T(8,128)(2,1)}) %all-gather.11.cloned.1.call-update) | async-done | bytes 4718608 | tf_op jit(solution)/shard_map/all_gather | solution.py:78
  514.6 11.6 multiply_convert_fusion.1
  526.2 53.5 %all-gather.13.cloned.1.call-done = bf16[3072,768]{1,0:T(8,128)(2,1)} async-done(((bf16[96,768]{1,0:T(8,128)(2,1)}), bf16[3072,768]{1,0:T(8,128)(2,1)}) %all-gather.13.cloned.1.call-update) | async-done | bytes 4718608 | tf_op jit(solution)/shard_map/all_gather | solution.py:79
  579.6 6.1 add_convert_fusion.1
  585.8 1.6 fusion.210
  587.4 1.3 copy-done.82
  588.7 8.0 multiply_convert_fusion
  596.7 2.3 add_convert_fusion
  600.2 5.3 convolution_add_fusion.1
  605.6 2.9 fusion.141
  608.5 5.2 convolution_add_fusion
  615.5 1.4 maximum_maximum_fusion
  617.0 1.7 copy.85
  618.7 1.7 fusion.232
  621.9 3.9 fusion.234
  625.9 2.8 fusion.123
  628.7 1.4 fusion.120
  631.4 40.3 %all-reduce.15 = (f32[768,2]{0,1:T(2,128)}, f32[768,2]{0,1:T(2,128)}) all-reduce(f32[768,2]{0,1:T(2,128)} %maximum_add_fusion, f32[768,2]{0,1:T(2,128)} %maximum_add_fusion.1), channel_id=9, replica_groups=mesh['seq'=8,'dp'=4] {'seq','dp'}, use_global_device_ids=true, to_apply=%region_45.46.clone | all-reduce | flops 3072 | bytes 24576
  672.9 1.3 constant_dynamic-slice_fusion.1
  674.2 4.4 fusion.230
  679.1 3.8 fusion.231
  687.0 96.8 %reduce-scatter.16.cloned.1.call-done = f32[24,768]{1,0:T(8,128)} async-done(((f32[768,768]{1,0:T(8,128)}), f32[24,768]{1,0:T(8,128)}) %reduce-scatter.16.cloned.1.call-update) | async-done | bytes 73744 | tf_op jit(solution)/shard_map/reduce_scatter | solution.py:301
  783.7 103.9 %reduce-scatter.18.cloned.1.call-done = f32[24,768]{1,0:T(8,128)} async-done(((f32[768,768]{1,0:T(8,128)}), f32[24,768]{1,0:T(8,128)}) %reduce-scatter.18.cloned.1.call-update) | async-done | bytes 73744 | tf_op jit(solution)/shard_map/reduce_scatter | solution.py:301
  887.7 141.9 %reduce-scatter.20.cloned.1.call-done = f32[24,3072]{1,0:T(8,128)} async-done(((f32[768,3072]{1,0:T(8,128)}), f32[24,3072]{1,0:T(8,128)}) %reduce-scatter.20.cloned.1.call-update) | async-done | bytes 294928 | tf_op jit(solution)/shard_map/reduce_scatter | solution.py:301
  1029.5 141.1 %reduce-scatter.22.cloned.1.call-done = f32[96,768]{1,0:T(8,128)} async-done(((f32[3072,768]{1,0:T(8,128)}), f32[96,768]{1,0:T(8,128)}) %reduce-scatter.22.cloned.1.call-update) | async-done | bytes 294928 | tf_op jit(solution)/shard_map/reduce_scatter | solution.py:301
  (389 shorter events, 75.6 us)
Async XLA Ops:
  7.2 206.8 %copy-start = (bf16[2,256,768]{2,1,0:T(8,128)(2,1)S(1)}, bf16[2,256,768]{2,1,0:T(8,128)(2,1)}, u32[]{:S(2)}) copy-start(bf16[2,256,768]{2,1,0:T(8,128)(2,1)} %param.26) | copy-start | bytes 2359300
  7.2 231.4 %all-gather.7.cloned.1.call-start = ((), (), s32[]{:S(2)}) async-start(), calls=%async_computation.7 | async-start | bytes 1216512 | tf_op jit(solution)/shard_map/all_gather | solution.py:75
  7.9 251.1 %all-gather.9.cloned.1.call-start = ((), (), s32[]{:S(2)}) async-start(), calls=%async_computation.8 | async-start | bytes 1216512 | tf_op jit(solution)/shard_map/all_gather | solution.py:77
  8.7 394.0 %reduce-scatter.12.cloned.1.call-start = ((), (), s32[]{:S(2)}) async-start(), calls=%async_computation.11 | async-start | bytes 589824 | tf_op jit(solution)/shard_map/reduce_scatter | solution.py:270
  10.0 230.3 %copy-start.44 = (f32[256]{0:T(256)}, f32[256]{0:T(256)S(1)}, u32[]{:S(2)}) copy-start(f32[256]{0:T(256)S(1)} %get-tuple-element.917) | copy-start | bytes 3076
  11.5 132.9 %copy-start.68 = (f32[256]{0:T(256)}, f32[256]{0:T(256)S(1)}, u32[]{:S(2)}) copy-start(f32[256]{0:T(256)S(1)} %get-tuple-element.777) | copy-start | bytes 3076
  11.5 202.4 %copy-start.70 = (f32[256]{0:T(256)}, f32[256]{0:T(256)S(1)}, u32[]{:S(2)}) copy-start(f32[256]{0:T(256)S(1)} %get-tuple-element.776) | copy-start | bytes 3076
  11.6 439.9 %copy-start.48 = (f32[256]{0:T(256)}, f32[256]{0:T(256)S(1)}, u32[]{:S(2)}) copy-start(f32[256]{0:T(256)S(1)} %fusion.197) | copy-start | bytes 3076
  211.8 2.1 copy-start.19
  212.5 43.4 %copy-start.52 = (f32[768]{0:T(1024)}, f32[768]{0:T(1024)S(1)}, u32[]{:S(2)}) copy-start(f32[768]{0:T(1024)S(1)} %get-tuple-element.782) | copy-start | bytes 9220
  213.9 24.0 %copy-start.42 = (f32[256,128]{0,1:T(8,128)}, f32[256,128]{0,1:T(8,128)S(1)}, u32[]{:S(2)}) copy-start(f32[256,128]{0,1:T(8,128)S(1)} %fusion.218) | copy-start | bytes 393220
  214.0 26.4 %copy-start.54 = (f32[256]{0:T(256)}, f32[256]{0:T(256)S(1)}, u32[]{:S(2)}) copy-start(f32[256]{0:T(256)S(1)} %fusion.196) | copy-start | bytes 3076
  214.4 23.5 %copy-start.43 = (f32[256,128]{0,1:T(8,128)}, f32[256,128]{0,1:T(8,128)S(1)}, u32[]{:S(2)}) copy-start(f32[256,128]{0,1:T(8,128)S(1)} %fusion.221) | copy-start | bytes 393220
  214.4 25.9 %copy-start.72 = (f32[8]{0:T(128)}, f32[8]{0:T(128)S(1)}, u32[]{:S(2)}) copy-start(f32[8]{0:T(128)S(1)} %multiply_exponential_fusion) | copy-start | bytes 100
  214.5 27.5 %copy-start.66 = (f32[256]{0:T(256)}, f32[256]{0:T(256)S(1)}, u32[]{:S(2)}) copy-start(f32[256]{0:T(256)S(1)} %convert_multiply_fusion) | copy-start | bytes 3076
  255.9 7.6 copy-start.5
  255.9 7.6 copy-start.28
  255.9 3.1 copy-start.3
  305.8 4.6 copy-start.23
  307.8 140.5 %reduce-scatter.14.cloned.1.call-start = ((), (), s32[]{:S(2)}) async-start(), calls=%async_computation.12 | async-start | bytes 589824 | tf_op jit(solution)/shard_map/reduce_scatter | solution.py:270
  330.8 4.8 copy-start.32
  330.8 5.6 copy-start.45
  330.8 5.6 copy-start.53
  330.8 5.6 copy-start.55
  332.8 181.8 %all-gather.11.cloned.1.call-start = ((), (), s32[]{:S(2)}) async-start(), calls=%async_computation.9 | async-start | bytes 4866048 | tf_op jit(solution)/shard_map/all_gather | solution.py:78
  333.4 246.2 %all-gather.13.cloned.1.call-start = ((), (), s32[]{:S(2)}) async-start(), calls=%async_computation.10 | async-start | bytes 4866048 | tf_op jit(solution)/shard_map/all_gather | solution.py:79
  334.0 353.0 %reduce-scatter.24.cloned.1.call-start = ((), (), s32[]{:S(2)}) async-start(), calls=%async_computation.17 | async-start | bytes 405504
  335.6 113.7 %copy-start.67 = (f32[256]{0:T(256)S(1)}, f32[256]{0:T(256)}, u32[]{:S(2)}) copy-start(f32[256]{0:T(256)} %copy-done.66) | copy-start | bytes 3076
  335.6 113.7 %copy-start.73 = (f32[8]{0:T(128)S(1)}, f32[8]{0:T(128)}, u32[]{:S(2)}) copy-start(f32[8]{0:T(128)} %copy-done.72) | copy-start | bytes 100
  403.5 47.9 %copy-start.38 = (bf16[256,64]{0,1:T(8,128)(2,1)}, bf16[256,64]{0,1:T(8,128)(2,1)S(1)}, u32[]{:S(2)}) copy-start(bf16[256,64]{0,1:T(8,128)(2,1)S(1)} %slice.353) | copy-start | bytes 98308
  449.2 2.2 copy-start.40
  451.2 332.6 %reduce-scatter.16.cloned.1.call-start = ((), (), s32[]{:S(2)}) async-start(), calls=%async_computation.13 | async-start | bytes 2433024 | tf_op jit(solution)/shard_map/reduce_scatter | solution.py:301
  453.0 2.2 copy-start.6
  453.0 2.2 copy-start.29
  455.2 432.5 %reduce-scatter.18.cloned.1.call-start = ((), (), s32[]{:S(2)}) async-start(), calls=%async_computation.14 | async-start | bytes 2433024 | tf_op jit(solution)/shard_map/reduce_scatter | solution.py:301
  457.3 57.3 %copy-start.31 = (f32[768]{0:T(1024)S(1)}, f32[768]{0:T(1024)}, u32[]{:S(2)}) copy-start(f32[768]{0:T(1024)} %get-tuple-element.918) | copy-start | bytes 9220
  457.3 57.3 %copy-start.33 = (f32[768]{0:T(1024)S(1)}, f32[768]{0:T(1024)}, u32[]{:S(2)}) copy-start(f32[768]{0:T(1024)} %get-tuple-element.783) | copy-start | bytes 9220
  457.3 57.3 %copy-start.46 = (f32[256]{0:T(256)S(1)}, f32[256]{0:T(256)}, u32[]{:S(2)}) copy-start(f32[256]{0:T(256)} %copy-done.44) | copy-start | bytes 3076
  457.3 57.3 %copy-start.56 = (f32[256]{0:T(256)S(1)}, f32[256]{0:T(256)}, u32[]{:S(2)}) copy-start(f32[256]{0:T(256)} %copy-done.54) | copy-start | bytes 3076
  459.2 570.3 %reduce-scatter.20.cloned.1.call-start = ((), (), s32[]{:S(2)}) async-start(), calls=%async_computation.15 | async-start | bytes 9732096 | tf_op jit(solution)/shard_map/reduce_scatter | solution.py:301
  585.8 2.9 copy-start.82
  585.8 10.9 slice-start
  588.7 8.0 slice-start.1
  596.7 11.8 copy-start.7
  605.5 565.1 %reduce-scatter.22.cloned.1.call-start = ((), (), s32[]{:S(2)}) async-start(), calls=%async_computation.16 | async-start | bytes 9732096 | tf_op jit(solution)/shard_map/reduce_scatter | solution.py:301
  613.7 5.0 copy-start.1
  613.7 6.7 copy-start.11
  618.6 2.3 copy-start.20
  618.6 2.3 copy-start.37
  618.6 2.3 copy-start.41
  618.6 2.6 copy-start.35
  618.6 2.6 copy-start.39
  618.7 2.6 copy-start.47
  618.7 7.2 slice-start.2
  621.3 4.6 slice-start.3
  621.8 4.0 copy-start.78
  621.9 3.9 copy-start.76
  621.9 4.0 copy-start.27
  621.9 4.0 copy-start.50
  621.9 4.0 copy-start.57
  625.8 2.9 copy-start.15
  674.2 4.4 copy-start.9
  674.2 4.9 copy-start.8
  679.1 3.8 copy-start.14
  (34 other events, 53.0 us)
Sparse Core Ops, SparseCore 0:
  10.8 56.7 all-gather.6
  70.4 53.0 all-gather.8
  308.0 94.6 reduce-scatter.11
  405.9 42.4 reduce-scatter.13
  451.0 63.5 all-gather.10
  517.2 62.3 all-gather.12
  585.2 93.6 reduce-scatter.23
  685.6 98.1 reduce-scatter.15
  789.6 97.9 reduce-scatter.17
  895.0 134.5 reduce-scatter.19
  1036.0 134.5 reduce-scatter.21
where the time goes:
time: 1180 us
  waiting for transfers between devices  704 us (60%)
  blocking collectives  261 us (22%)
  matrix products  100 us (8%)
  local copies, waits for them, and re-layouts  56.3 us (5%)
  other arithmetic  27.6 us (2%)
  between operations  15.8 us (1%)
    reduce_scatter x4, waiting for transfers between devices, on_device(): lax.psum_scatter(totals, ('seq', 'dp'), scatter_dimension=0, tiled=True)  484 us
    reduce_scatter x2, waiting for transfers between devices, on_device(): lax.psum_scatter(d_keyval_all.astype(jnp.bfloat16), 'seq', scatter_dimens...  109 us
    all_gather x1, blocking collectives, on_device(): lax.all_gather(norm_gain, ('seq', 'dp'), axis=0, tiled=True)  69.5 us
    all_gather x1, blocking collectives, on_device(): lax.all_gather(w_keyval, ('seq', 'dp'), axis=0, tiled=True)  67.3 us
    all_gather x1, blocking collectives, on_device(): lax.all_gather(norm_bias, ('seq', 'dp'), axis=0, tiled=True)  63.2 us
    all_gather x1, waiting for transfers between devices, on_device(): lax.all_gather(w_up, ('seq', 'dp'), axis=0, tiled=True)  55.3 us
    all_gather x1, waiting for transfers between devices, on_device(): lax.all_gather(w_down, ('seq', 'dp'), axis=0, tiled=True)  53.5 us
    unnamed x1, blocking collectives  40.3 us
  transfers between devices with their start and end apart: 11, of which 8 were waited for; matrix products, arithmetic and copies ran while one was open for 11% of the time, Pallas kernels for 0%

commit v1 on v0

v1 whole, which is shorter than its diff:
```python
import functools
import math

import jax
import jax.numpy as jnp
from jax import lax
from jax.experimental import pallas as pl
from jax.experimental.pallas import tpu as pltpu
from jax.sharding import PartitionSpec as P

HEADS = 12
HEAD = 64
ROT = 16
TEAM = 4
MINE = HEADS // TEAM
WIDE = 2 * HEAD
EPSILON = 1e-05
BF = jnp.bfloat16
F32 = jnp.float32
SCALE = 1.0 / math.sqrt(HEAD)
MB = 1 << 20


def dot(left, right):
    return lax.dot_general(left, right, (((1,), (0,)), ((), ())), preferred_element_type=F32)


def dot_rt(left, right):
    return lax.dot_general(left, right, (((1,), (1,)), ((), ())), preferred_element_type=F32)


def dot_lt(left, right):
    return lax.dot_general(left, right, (((0,), (0,)), ((), ())), preferred_element_type=F32)


def lanes(shape):
    return lax.broadcasted_iota(jnp.int32, shape, len(shape) - 1)


def turn(values, cos_table, sin_table, sign):
    near = (lanes(values.shape) % HEAD) < ROT // 2
    swapped = jnp.where(
        near, pltpu.roll(values, WIDE - ROT // 2, 1), pltpu.roll(values, ROT // 2, 1)
    )
    return values * cos_table + (sign * swapped) * sin_table


def standardize(tokens):
    center = tokens - jnp.mean(tokens, axis=-1, keepdims=True)
    spread = jnp.mean(center * center, axis=-1, keepdims=True)
    scale = lax.rsqrt(spread + EPSILON)
    return center * scale, scale


def norm_back(hat, scale, pulled):
    return scale * (
        pulled
        - jnp.mean(pulled, axis=-1, keepdims=True)
        - hat * jnp.mean(pulled * hat, axis=-1, keepdims=True)
    )


def three_parts(column):
    high = column.astype(BF)
    rest = column - high.astype(F32)
    mid = rest.astype(BF)
    low = (rest - mid.astype(F32)).astype(BF)
    return high, mid, low


def marked(lane, base, parts):
    out = jnp.zeros(lane.shape, BF)
    for index, part in enumerate(parts):
        out = jnp.where(lane == base + index, part, out)
    return out


def prepare_kernel(x_ref, weight_ref, norm_ref, cos_ref, sin_ref, attn_ref, mlp_ref, query_ref, keyval_ref):
    tokens = x_ref[0, 0].astype(F32)
    hat, _ = standardize(tokens)
    normed = (hat * norm_ref[0:1, :] + norm_ref[2:3, :]).astype(BF)
    attn_ref[0, 0] = normed
    mlp_ref[0, 0] = (hat * norm_ref[1:2, :] + norm_ref[3:4, :]).astype(BF)
    made = dot(normed, weight_ref[...])
    cos_table = cos_ref[0]
    sin_table = sin_ref[0]
    keys_side = lanes(cos_table.shape) < HEAD
    keyval_ref[0, 0] = turn(
        made[:, :WIDE], jnp.where(keys_side, cos_table, 1.0), jnp.where(keys_side, sin_table, 0.0), 1.0
    ).astype(BF)
    for part in range(2):
        piece = made[:, WIDE * (part + 1) : WIDE * (part + 2)]
        query_ref[0, 0, :, WIDE * part : WIDE * (part + 1)] = (
            turn(piece, cos_table, sin_table, 1.0) * SCALE
        ).astype(BF)


def rank_of(own, block, top):
    return own ^ ((block % 2) * top) ^ (block // 2)


def slot_of(away, top, wide):
    return ((away // 2) % wide) * TEAM + (away // top) % 2 + 2 * (away % 2)


def forward_kernel(top, wide, own_ref, query_ref, keyval_ref, context_ref, marked_ref, low_ref, score_ref, peak_ref):
    rows = query_ref.shape[2]
    own = own_ref[0]
    rank = rank_of(own, pl.program_id(1), top)
    lane = lanes((rows, WIDE))
    first = query_ref[0, 0, :, :WIDE]
    last = query_ref[0, 0, :, WIDE:]
    heads = [first, pltpu.roll(first.astype(F32), HEAD, 1).astype(BF), last]
    for head in range(MINE):
        low_ref[head] = heads[head]
    keep = lax.broadcasted_iota(jnp.int32, (rows, rows), 1) <= lax.broadcasted_iota(
        jnp.int32, (rows, rows), 0
    )

    def keys_of(step):
        block = keyval_ref[slot_of(step ^ own, top, wide), 0]
        return block, jnp.where(lane < HEAD, block, jnp.zeros_like(block))

    def score(step, masked):
        _, keys = keys_of(step)
        for head in range(MINE):
            scores = dot_rt(low_ref[head], keys)
            if masked:
                scores = jnp.where(keep, scores, -1e30)
            score_ref[step, head] = scores
            best = jnp.maximum(scores[:, :WIDE], scores[:, WIDE:])
            peak_ref[head] = best if masked else jnp.maximum(peak_ref[head], best)

    score(rank, True)

    @pl.loop(0, rank)
    def _(step):
        score(step, False)

    for head in range(MINE):
        peak_ref[head] = jnp.broadcast_to(
            jnp.max(peak_ref[head], axis=-1, keepdims=True), (rows, WIDE)
        )

    def weigh(step, sums):
        block, _ = keys_of(step)
        block = jnp.where(lane < HEAD, jnp.ones_like(block), block)
        out = []
        for head in range(MINE):
            peak = peak_ref[head]
            weights = jnp.exp(
                score_ref[step, head] - jnp.concatenate([peak] * (rows // WIDE), axis=1)
            )
            out.append(sums[head] + dot(weights.astype(BF), block))
        return tuple(out)

    sums = lax.fori_loop(
        0, rank + 1, weigh, tuple(jnp.zeros((rows, WIDE), F32) for _ in range(MINE))
    )
    made = []
    for head in range(MINE):
        swapped = pltpu.roll(sums[head], HEAD, 1)
        total = jnp.where(lane < HEAD, sums[head], swapped)
        made.append(jnp.where(lane < HEAD, swapped, sums[head]) / total)
        logsum = peak_ref[head] + jnp.log(total)
        query = low_ref[head]
        marked_ref[0, 0, head] = jnp.where(
            lane < HEAD, query, marked(lane, HEAD, three_parts(-logsum))
        )
    context_ref[0, 0, :, :WIDE] = jnp.where(lane < HEAD, made[0], made[1]).astype(BF)
    context_ref[0, 0, :, WIDE:] = jnp.where(lane < HEAD, made[2], 0.0).astype(BF)


def context_kernel(context_ref, grad_ref, out_ref, marked_ref, total_ref):
    rows = context_ref.shape[2]
    grad = grad_ref[0, 0]
    context = context_ref[0, 0]
    lane = lanes((rows, WIDE))
    pulled = dot_rt(grad, out_ref[...]).astype(BF)
    product = pulled.astype(F32) * context.astype(F32)
    for head in range(MINE):
        column = WIDE * (head // 2)
        side = (lane < HEAD) if head % 2 == 0 else (lane >= HEAD)
        delta = jnp.sum(
            jnp.where(side, product[:, column : column + WIDE], 0.0), axis=-1, keepdims=True
        )
        piece = pulled[:, column : column + WIDE]
        if head % 2 == 0:
            piece = pltpu.roll(piece.astype(F32), HEAD, 1).astype(BF)
        marked_ref[0, 0, head] = jnp.where(
            lane >= HEAD, piece, marked(lane, 0, three_parts(jnp.broadcast_to(-delta, lane.shape)))
        )
    made = dot_lt(context, grad)
    first = (pl.program_id(0) == 0) & (pl.program_id(1) == 0)

    @pl.when(first)
    def _():
        total_ref[...] = made

    @pl.when(jnp.logical_not(first))
    def _():
        total_ref[...] += made


def backward_kernel(top, wide, own_ref, query_ref, grad_ref, keyval_ref, cos_ref, sin_ref, dquery_ref, dkeyval_ref, sum_ref):
    rows = query_ref.shape[3]
    own = own_ref[0]
    rank = rank_of(own, pl.program_id(0), top)
    lane = lanes((rows, WIDE))
    ones_low = jnp.where(lane < 3, 1.0, 0.0).astype(BF)
    ones_high = jnp.where((lane >= HEAD) & (lane < HEAD + 3), 1.0, 0.0).astype(BF)
    keep = lax.broadcasted_iota(jnp.int32, (rows, rows), 0) <= lax.broadcasted_iota(
        jnp.int32, (rows, rows), 1
    )

    @pl.when(pl.program_id(0) == 0)
    def _():
        dkeyval_ref[...] = jnp.zeros_like(dkeyval_ref)

    def visit(step, masked):
        slot = slot_of(step ^ own, top, wide)
        block = keyval_ref[slot, 0]
        keys = jnp.where(lane < HEAD, block, ones_high)
        values = jnp.where(lane < HEAD, ones_low, block)
        d_keys = jnp.zeros((rows, WIDE), F32)
        d_values = jnp.zeros((rows, WIDE), F32)
        for head in range(MINE):
            query = query_ref[0, 0, head]
            grad = grad_ref[0, 0, head]
            probs = jnp.exp(dot_rt(keys, query))
            if masked:
                probs = jnp.where(keep, probs, 0.0)
            d_scores = (probs * dot_rt(values, grad)).astype(BF)
            d_values += dot(probs.astype(BF), grad)
            d_keys += dot(d_scores, query)
            d_query = dot_lt(keys, d_scores)
            sum_ref[head] = d_query if masked else sum_ref[head] + d_query
        dkeyval_ref[slot] += jnp.where(lane < HEAD, d_keys, d_values)

    visit(rank, True)

    @pl.loop(0, rank)
    def _(step):
        visit(step, False)

    turned = [jnp.transpose(sum_ref[head]) * SCALE for head in range(MINE)]
    both = jnp.where(lane < HEAD, turned[0], pltpu.roll(turned[1], HEAD, 1))
    last = jnp.where(lane < HEAD, turned[2], 0.0)
    cos_table = cos_ref[0]
    sin_table = sin_ref[0]
    dquery_ref[0, :, :WIDE] = turn(both, cos_table, sin_table, -1.0).astype(BF)
    dquery_ref[0, :, WIDE:] = turn(last, cos_table, sin_table, -1.0).astype(BF)


def hidden_kernel(normed_ref, grad_ref, context_ref, up_ref, down_ref, out_ref, made_ref, dnormed_ref, gup_ref, gdown_ref, up_sum, down_sum):
    def flat(ref):
        return ref[0].reshape(ref.shape[1] * ref.shape[2], ref.shape[3])

    normed = flat(normed_ref)
    grad = flat(grad_ref)
    raw = dot(normed, up_ref[...])
    bell = 0.5 + 0.5 * lax.erf(raw * math.sqrt(0.5))
    slope = bell + raw * (jnp.exp(raw * raw * -0.5) * (1.0 / math.sqrt(2.0 * math.pi)))
    hidden = (raw * bell).astype(BF)
    d_raw = (dot_rt(grad, down_ref[...]) * slope).astype(BF)
    made = dot(hidden, down_ref[...]) + dot(flat(context_ref), out_ref[...])
    made_ref[0] = made.astype(BF).reshape(made_ref.shape[1:])
    dnormed_ref[0] = dot_rt(d_raw, up_ref[...]).astype(BF).reshape(dnormed_ref.shape[1:])
    step = pl.program_id(0)
    gdown = dot_lt(hidden, grad)
    gup = dot_lt(normed, d_raw)

    @pl.when(step == 0)
    def _():
        down_sum[...] = gdown
        up_sum[...] = gup

    @pl.when(step > 0)
    def _():
        down_sum[...] += gdown
        up_sum[...] += gup

    @pl.when(step == pl.num_programs(0) - 1)
    def _():
        gdown_ref[...] = down_sum[...].astype(BF)
        gup_ref[...] = up_sum[...].astype(BF)


def tokens_kernel(x_ref, normed_ref, dnormed_ref, dquery_ref, weight_ref, norm_ref, dx_ref, gquery_ref, gnorm_ref):
    hat, scale = standardize(x_ref[0, 0].astype(F32))
    d_query = dquery_ref[0, 0]
    d_attn = dot_rt(d_query, weight_ref[...])
    d_mlp = dnormed_ref[0, 0].astype(F32)
    dx_ref[0, 0] = norm_back(hat, scale, d_attn * norm_ref[0:1, :] + d_mlp * norm_ref[1:2, :]).astype(BF)
    sums = [
        jnp.sum(piece, axis=0, keepdims=True) for piece in (d_attn * hat, d_mlp * hat, d_attn, d_mlp)
    ]
    sums = jnp.concatenate(sums + [jnp.zeros_like(sums[0])] * 4, axis=0)
    gquery = dot_lt(normed_ref[0, 0], d_query)
    first = (pl.program_id(0) == 0) & (pl.program_id(1) == 0)

    @pl.when(first)
    def _():
        gquery_ref[...] = gquery
        gnorm_ref[...] = sums

    @pl.when(jnp.logical_not(first))
    def _():
        gquery_ref[...] += gquery
        gnorm_ref[...] += sums


def keyval_kernel(x_ref, normed_ref, dkeyval_ref, cotangent_ref, weight_ref, norm_ref, cos_ref, sin_ref, dx_ref, gkeyval_ref, gnorm_ref):
    hat, scale = standardize(x_ref[0].astype(F32))
    keys_side = lanes(cos_ref.shape[1:]) < HEAD
    d_keyval = dkeyval_ref[0] + cotangent_ref[0].astype(F32)
    d_pre = turn(
        d_keyval, jnp.where(keys_side, cos_ref[0], 1.0), jnp.where(keys_side, sin_ref[0], 0.0), -1.0
    ).astype(BF)
    d_attn = dot_rt(d_pre, weight_ref[...])
    dx_ref[0] = norm_back(hat, scale, d_attn * norm_ref[0:1, :])
    sums = [jnp.sum(piece, axis=0, keepdims=True) for piece in (d_attn * hat, d_attn)]
    blank = jnp.zeros_like(sums[0])
    sums = jnp.concatenate([sums[0], blank, sums[1]] + [blank] * 5, axis=0)
    gkeyval = dot_lt(normed_ref[0, 0], d_pre)
    first = pl.program_id(0) == 0

    @pl.when(first)
    def _():
        gkeyval_ref[...] = gkeyval
        gnorm_ref[...] = sums

    @pl.when(jnp.logical_not(first))
    def _():
        gkeyval_ref[...] += gkeyval
        gnorm_ref[...] += sums


def params(limit):
    return pltpu.CompilerParams(vmem_limit_bytes=limit * MB)


def cost(flops, moved, exps=0):
    return pl.CostEstimate(flops=int(flops), bytes_accessed=int(moved), transcendentals=int(exps))


def struct(shape, kind):
    return jax.ShapeDtypeStruct(shape, kind)


def whole(*shape):
    return pl.BlockSpec(shape, lambda *_: (0,) * len(shape))


def on_device(nseq, ndp, inputs, w_query, w_keyval, w_out, w_up, w_down, norm_gain, norm_bias, out_cotangent, kv_cotangent):
    count, rows, width = inputs.shape
    top = nseq // 2
    wide = nseq // TEAM
    own = lax.axis_index("seq")
    own_y, own_x, own_c = own // top, (own // 2) % wide, own % 2
    own_z = lax.axis_index("dp")
    share = w_query.shape[0]
    hidden = w_up.shape[1] // TEAM
    heads_wide = MINE * HEAD

    def flip(value, mask):
        return lax.ppermute(value, "seq", [(i, i ^ mask) for i in range(nseq)])

    def flip_z(value, mask):
        return lax.ppermute(value, "dp", [(i, i ^ mask) for i in range(ndp)])

    def in_order(bit, mine, other, axis):
        return jnp.where(
            bit == 0, jnp.stack([mine, other], axis), jnp.stack([other, mine], axis)
        )

    def pick(value, index, axis):
        return lax.dynamic_index_in_dim(value, index, axis, keepdims=False)

    def gather(value):
        value = value[None]
        mask = ndp // 2
        while mask:
            value = in_order((own_z // mask) % 2, value, flip_z(value, mask), 1)
            value = value.reshape((-1,) + value.shape[2:])
            mask //= 2
        value = value[None]
        mask = wide // 2
        while mask:
            value = in_order((own_x // mask) % 2, value, flip(value, 2 * mask), 1)
            value = value.reshape((-1,) + value.shape[2:])
            mask //= 2
        return value

    def scatter(value):
        mask = wide // 2
        while mask:
            bit = (own_x // mask) % 2
            value = value.reshape((2, -1) + value.shape[1:])
            got = flip(pick(value, 1 - bit, 0), 2 * mask)
            value = (pick(value, bit, 0).astype(F32) + got.astype(F32)).astype(BF)
            mask //= 2
        value = value.reshape(value.shape[1:])
        mask = 1
        while mask < ndp:
            bit = (own_z // mask) % 2
            value = value.reshape((-1, 2) + value.shape[1:])
            got = flip_z(pick(value, 1 - bit, 1).astype(BF), mask)
            value = pick(value, bit, 1).astype(F32) + got.astype(F32)
            mask *= 2
        return value.reshape(value.shape[1:])

    def team(value):
        value = value[None]
        value = jnp.concatenate([value, flip(value, top)], axis=0)
        return jnp.concatenate([value, flip(value, 1)], axis=0)

    norms = jnp.concatenate([norm_gain, norm_bias], axis=1)
    queries_of = w_query.reshape(share, 2, 2, heads_wide).transpose(1, 2, 0, 3)
    same = jnp.concatenate([w_keyval, norms], axis=1)
    ups = w_up.reshape(share, 2, wide, 2, hidden // wide).transpose(1, 3, 0, 2, 4)
    ups = ups.reshape(2, 2, share, hidden)
    pad = jnp.zeros((2, 2, share, 3 * WIDE - WIDE - heads_wide - norms.shape[1]), BF)
    spread = (2, 2, share)
    pack = jnp.concatenate(
        [
            jnp.broadcast_to(same[:, :WIDE], spread + (WIDE,)),
            queries_of,
            jnp.broadcast_to(same[:, WIDE:], spread + (norms.shape[1],)),
            pad,
            ups,
        ],
        axis=3,
    )
    pack = in_order(own_y, pick(pack, own_y, 0), flip(pick(pack, 1 - own_y, 0), top), 0)
    pack = in_order(own_c, pick(pack, own_c, 1), flip(pick(pack, 1 - own_c, 1), 1), 1)

    def moved(target_of):
        pairs = []
        for rank in range(nseq):
            for z in range(ndp):
                member = 2 * (rank // top) + rank % 2
                place = ((rank // 2) % wide) * ndp + z
                pairs.append((member * (nseq * ndp // TEAM) + place, rank * ndp + z))
        return [pair if target_of else pair[::-1] for pair in pairs]

    out_rows = lax.ppermute(w_out, ("seq", "dp"), moved(True))

    tokens = team(inputs)

    def rows_of(value):
        order = (2, 0, 3, 1, 4, 5)
        return value.transpose(order).reshape(-1, value.shape[-1])

    front = rows_of(gather(pack[..., : 3 * WIDE]))
    low_rows = jnp.concatenate([out_rows, w_down], axis=0)
    back = gather(low_rows)
    full_out = back[:, :, :share].reshape(heads_wide, width)
    full_out = jnp.concatenate([full_out, jnp.zeros((2 * WIDE - heads_wide, width), BF)], axis=0)
    full_down = back[:, :, share:].reshape(hidden, width)
    full_up = rows_of(gather(pack[..., 3 * WIDE :]))
    grads = team(out_cotangent)

    norm_rows = front[:, WIDE + heads_wide : WIDE + heads_wide + 4].astype(F32).T
    norm_rows = jnp.concatenate([norm_rows, jnp.zeros_like(norm_rows)], axis=0)

    lane = jnp.arange(WIDE, dtype=jnp.int32) % HEAD
    frequency = jnp.exp(
        -math.log(10000.0) * ((lane % (ROT // 2)).astype(F32) * (2.0 / ROT))
    )
    ranks = jnp.stack([rank_of(own, r, top) for r in range(TEAM)])
    positions = ranks[:, None] * rows + jnp.arange(rows, dtype=jnp.int32)[None]
    angles = (positions.astype(F32) * 0.25)[..., None] * frequency
    cos_table = jnp.where(lane < ROT, jnp.cos(angles), 1.0)
    sin_table = jnp.where(lane < ROT, jnp.sin(angles), 0.0)
    sin_table = jnp.where(lane < ROT // 2, -sin_table, sin_table)
    own_rank = own.reshape(1).astype(jnp.int32)

    total = TEAM * count * rows

    def by_rows(last):
        return pl.BlockSpec((1, 1, rows, last), lambda r, b, *_: (r, b, 0, 0))

    table = pl.BlockSpec((1, rows, WIDE), lambda r, *_: (r, 0, 0))
    normed_attn, normed_mlp, queries, keyval = pl.pallas_call(
        prepare_kernel,
        grid=(TEAM, count),
        in_specs=[by_rows(width), whole(*front.shape), whole(8, width), table, table],
        out_specs=[by_rows(width), by_rows(width), by_rows(2 * WIDE), by_rows(WIDE)],
        out_shape=[
            struct((TEAM, count, rows, width), BF),
            struct((TEAM, count, rows, width), BF),
            struct((TEAM, count, rows, 2 * WIDE), BF),
            struct((TEAM, count, rows, WIDE), BF),
        ],
        compiler_params=params(40),
        cost_estimate=cost(2 * total * width * 3 * WIDE, total * width * 6),
        name="prepare",
    )(tokens, front, norm_rows, cos_table, sin_table)

    everyone = keyval
    mask = 1
    while mask < wide:
        everyone = jnp.concatenate([everyone, flip(everyone, 2 * mask)], axis=0)
        mask *= 2
    slots = TEAM * wide
    pairs = MINE * total * (slots // 2 + 1) * rows

    by_query = pl.BlockSpec((1, 1, rows, 2 * WIDE), lambda b, r, *_: (r, b, 0, 0))
    by_heads = pl.BlockSpec((1, 1, MINE, rows, WIDE), lambda b, r, *_: (r, b, 0, 0, 0))
    context, marked_query = pl.pallas_call(
        functools.partial(forward_kernel, top, wide),
        grid_spec=pltpu.PrefetchScalarGridSpec(
            num_scalar_prefetch=1,
            grid=(count, TEAM),
            in_specs=[
                by_query,
                pl.BlockSpec((slots, 1, rows, WIDE), lambda b, r, *_: (0, b, 0, 0)),
            ],
            out_specs=[by_query, by_heads],
            scratch_shapes=[
                pltpu.VMEM((MINE, rows, WIDE), BF),
                pltpu.VMEM((slots, MINE, rows, rows), F32),
                pltpu.VMEM((MINE, rows, WIDE), F32),
            ],
        ),
        out_shape=[
            struct((TEAM, count, rows, 2 * WIDE), BF),
            struct((TEAM, count, MINE, rows, WIDE), BF),
        ],
        compiler_params=params(40),
        cost_estimate=cost(pairs * 2 * 4 * HEAD, total * WIDE * 8, pairs),
        name="attend",
    )(own_rank, queries, everyone)

    by_grad = pl.BlockSpec((1, 1, rows, width), lambda b, r, *_: (r, b, 0, 0))
    marked_grad, grad_out_local = pl.pallas_call(
        context_kernel,
        grid=(count, TEAM),
        in_specs=[by_query, by_grad, whole(*full_out.shape)],
        out_specs=[by_heads, whole(*full_out.shape)],
        out_shape=[
            struct((TEAM, count, MINE, rows, WIDE), BF),
            struct(full_out.shape, F32),
        ],
        compiler_params=params(40),
        cost_estimate=cost(4 * total * width * 2 * WIDE, total * width * 4),
        name="pull_context",
    )(context, grads, full_out)

    by_seqs = pl.BlockSpec((1, count, rows, width), lambda r: (r, 0, 0, 0))
    made, d_normed, grad_up_local, grad_down_local = pl.pallas_call(
        hidden_kernel,
        grid=(TEAM,),
        in_specs=[
            by_seqs,
            by_seqs,
            pl.BlockSpec((1, count, rows, 2 * WIDE), lambda r: (r, 0, 0, 0)),
            whole(width, hidden),
            whole(hidden, width),
            whole(*full_out.shape),
        ],
        out_specs=[by_seqs, by_seqs, whole(width, hidden), whole(hidden, width)],
        out_shape=[
            struct((TEAM, count, rows, width), BF),
            struct((TEAM, count, rows, width), BF),
            struct((width, hidden), BF),
            struct((hidden, width), BF),
        ],
        scratch_shapes=[pltpu.VMEM((width, hidden), F32), pltpu.VMEM((hidden, width), F32)],
        compiler_params=params(56),
        cost_estimate=cost(12 * total * width * hidden, total * width * 10, total * hidden * 2),
        name="hidden",
    )(normed_mlp, grads, context, full_up, full_down, full_out)

    def team_sum(value):
        got = flip(value[2:], 1)
        value = value[:2].astype(F32) + got.astype(F32)
        return value[0] + flip(value[1].astype(BF), top).astype(F32)

    output = (inputs.astype(F32) + team_sum(made)).astype(BF)

    d_queries = []
    d_keyvals = []
    for b in range(count):
        d_query, d_keyval = pl.pallas_call(
            functools.partial(backward_kernel, top, wide),
            grid_spec=pltpu.PrefetchScalarGridSpec(
                num_scalar_prefetch=1,
                grid=(TEAM,),
                in_specs=[
                    pl.BlockSpec((1, 1, MINE, rows, WIDE), lambda r, *_, b=b: (r, b, 0, 0, 0)),
                    pl.BlockSpec((1, 1, MINE, rows, WIDE), lambda r, *_, b=b: (r, b, 0, 0, 0)),
                    pl.BlockSpec((slots, 1, rows, WIDE), lambda r, *_, b=b: (0, b, 0, 0)),
                    table,
                    table,
                ],
                out_specs=[
                    pl.BlockSpec((1, rows, 2 * WIDE), lambda r, *_: (r, 0, 0)),
                    whole(slots, rows, WIDE),
                ],
                scratch_shapes=[pltpu.VMEM((MINE, WIDE, rows), F32)],
            ),
            out_shape=[
                struct((TEAM, rows, 2 * WIDE), BF),
                struct((slots, rows, WIDE), F32),
            ],
            compiler_params=params(40),
            cost_estimate=cost(pairs * 2 * 5 * HEAD, total * WIDE * 8, pairs),
            name="attend_back",
        )(own_rank, marked_query, marked_grad, everyone, cos_table, sin_table)
        d_queries.append(d_query)
        mask = wide // 2
        while mask:
            half = d_keyval.shape[0] // 2
            got = flip(d_keyval[half:].astype(BF), 2 * mask)
            d_keyval = d_keyval[:half] + got.astype(F32)
            mask //= 2
        got = flip(d_keyval[2:].astype(BF), 1)
        d_keyval = d_keyval[:2] + got.astype(F32)
        d_keyvals.append(d_keyval[0] + flip(d_keyval[1].astype(BF), top).astype(F32))
    d_queries = jnp.stack(d_queries, axis=1)
    d_keyvals = jnp.stack(d_keyvals)

    query_weight = jnp.concatenate(
        [front[:, WIDE : WIDE + heads_wide], jnp.zeros((width, 2 * WIDE - heads_wide), BF)], axis=1
    )
    d_tokens, grad_query_local, norm_sums = pl.pallas_call(
        tokens_kernel,
        grid=(TEAM, count),
        in_specs=[
            by_rows(width),
            by_rows(width),
            by_rows(width),
            by_rows(2 * WIDE),
            whole(*query_weight.shape),
            whole(8, width),
        ],
        out_specs=[by_rows(width), whole(*query_weight.shape), whole(8, width)],
        out_shape=[
            struct((TEAM, count, rows, width), BF),
            struct(query_weight.shape, F32),
            struct((8, width), F32),
        ],
        compiler_params=params(40),
        cost_estimate=cost(4 * total * width * 2 * WIDE, total * width * 8),
        name="pull_tokens",
    )(tokens, normed_attn, d_normed, d_queries, query_weight, norm_rows)

    by_own = pl.BlockSpec((1, rows, width), lambda b: (b, 0, 0))
    by_keys = pl.BlockSpec((1, rows, WIDE), lambda b: (b, 0, 0))
    own_table = pl.BlockSpec((1, rows, WIDE), lambda b: (0, 0, 0))
    d_own, grad_keyval_local, norm_sums_own = pl.pallas_call(
        keyval_kernel,
        grid=(count,),
        in_specs=[
            by_own,
            pl.BlockSpec((1, 1, rows, width), lambda b: (0, b, 0, 0)),
            by_keys,
            by_keys,
            pl.BlockSpec((width, WIDE), lambda b: (0, 0)),
            whole(8, width),
            own_table,
            own_table,
        ],
        out_specs=[by_own, whole(width, WIDE), whole(8, width)],
        out_shape=[
            struct((count, rows, width), F32),
            struct((width, WIDE), F32),
            struct((8, width), F32),
        ],
        compiler_params=params(40),
        cost_estimate=cost(4 * count * rows * width * WIDE, count * rows * width * 8),
        name="pull_keyval",
    )(inputs, normed_attn, d_keyvals, kv_cotangent, front, norm_rows, cos_table, sin_table)

    grad_inputs = out_cotangent.astype(F32) + d_own + team_sum(d_tokens)

    def grouped(value):
        value = value.reshape(2, wide, 2, ndp, share, value.shape[-1])
        return value.transpose(1, 3, 0, 2, 4, 5)

    low_grads = jnp.concatenate(
        [
            grad_out_local[:heads_wide].astype(BF).reshape(wide, ndp, share, width),
            grad_down_local.reshape(wide, ndp, hidden // (wide * ndp), width),
        ],
        axis=2,
    )
    low_grads = scatter(low_grads)
    grad_down = low_grads[share:]
    grad_out = lax.ppermute(low_grads[:share].astype(BF), ("seq", "dp"), moved(False)).astype(F32)
    up_grads = scatter(grouped(grad_up_local))
    front_local = jnp.concatenate(
        [grad_keyval_local, grad_query_local[:, :heads_wide], (norm_sums + norm_sums_own)[:4].T],
        axis=1,
    ).astype(BF)
    front_grads = scatter(grouped(front_local))

    def swap_back(value, summed):
        got = flip(pick(value, 1 - own_c, 1).astype(BF), 1).astype(F32)
        mine = pick(value, own_c, 1)
        parts = in_order(own_c, mine[..., summed:], got[..., summed:], 1)
        sums = mine[..., :summed] + got[..., :summed]
        sent = jnp.concatenate([sums, parts[:, 0], parts[:, 1]], axis=-1)
        got = flip(pick(sent, 1 - own_y, 0).astype(BF), top).astype(F32)
        mine = pick(sent, own_y, 0)
        parts = in_order(own_y, mine[..., summed:], got[..., summed:], 1)
        return mine[..., :summed] + got[..., :summed], parts

    _, grad_up = swap_back(up_grads, 0)
    grad_up = grad_up.reshape(share, 2, 2, wide, hidden // wide).transpose(0, 1, 3, 2, 4)
    grad_up = grad_up.reshape(share, TEAM * hidden)
    ends = front_grads[..., WIDE + heads_wide :]
    front_grads = jnp.concatenate([front_grads[..., :WIDE], ends, front_grads[..., WIDE : WIDE + heads_wide]], axis=-1)
    sums, grad_query = swap_back(front_grads, WIDE + ends.shape[-1])
    grad_query = grad_query.reshape(share, HEADS * HEAD)
    return (
        output,
        keyval[0],
        grad_inputs,
        grad_query,
        sums[:, :WIDE],
        grad_out,
        grad_up,
        grad_down,
        sums[:, WIDE : WIDE + 2],
        sums[:, WIDE + 2 : WIDE + 4],
    )


def solution(mesh):
    rows = P("dp", "seq", None)
    split = P(("seq", "dp"), None)
    return jax.shard_map(
        functools.partial(on_device, mesh.shape["seq"], mesh.shape["dp"]),
        mesh=mesh,
        in_specs=(rows,) + (split,) * 7 + (rows, rows),
        out_specs=(rows,) * 3 + (split,) * 7,
        check_vma=False,
    )
```

time: 1180 us -> 367 us (0.31)
  waiting for transfers between devices: 704 us -> 142 us
  blocking collectives: 261 us -> 0 us
  matrix products: 100 us -> 0 us
  Pallas kernels: 0 us -> 95.7 us
  starting transfers between devices: 0.85 us -> 66.2 us
  local copies, waits for them, and re-layouts: 56.3 us -> 30.9 us
  between operations: 15.8 us -> 1.83 us
    reduce_scatter x6 -> x0, waiting for transfers between devices: 593 us -> none  [the longest x4 484 us: on_device(): lax.psum_scatter(totals, ('seq', 'dp'), scatter_dimension=0, tiled=True)]
    all_gather x5 -> x0, blocking collectives: 221 us -> none  [the longest x1 69.5 us: on_device(): lax.all_gather(norm_gain, ('seq', 'dp'), axis=0, tiled=True)]
    ppermute x0 -> x41, waiting for transfers between devices: none -> 142 us  [the longest x27 99.6 us: flip(): return lax.ppermute(value, 'seq', [(i, i ^ mask) for i in range(nseq)])]
    all_gather x4 -> x0, waiting for transfers between devices: 109 us -> none  [the longest x1 55.3 us: on_device(): lax.all_gather(w_up, ('seq', 'dp'), axis=0, tiled=True)]
    dot_general x44 -> x0, matrix products: 100 us -> none  [the longest x10 23.1 us: matmul_t(): lax.dot_general(left, right, (((0,), (0,)), ((), ())), preferred_element_...]
    pallas_call x0 -> x8, Pallas kernels: none -> 95.7 us  [the longest x2 27.7 us: on_device(): pl.pallas_call(functools.partial(backward_kernel, top, wide), grid_spec=p...]
    ppermute x0 -> x41, starting transfers between devices: none -> 66.2 us  [the longest x27 50.5 us: flip(): return lax.ppermute(value, 'seq', [(i, i ^ mask) for i in range(nseq)])]
    unnamed x1 -> x0, blocking collectives: 40.3 us -> none
  transfers between devices with their start and end apart: 11 -> 41, of which waited for: 8 -> 23; matrix products, arithmetic and copies ran while one was open for 11% -> 12% of each run, Pallas kernels for 0% -> 5%
where the time goes in v1:
time: 367 us; the launch traced here: 366 us
  waiting for transfers between devices  142 us (39%)
  Pallas kernels  95.7 us (26%)
  starting transfers between devices  66.2 us (18%)
  local copies, waits for them, and re-layouts  30.9 us (8%)
  other arithmetic  29.8 us (8%)
    ppermute x27, waiting for transfers between devices, flip(): return lax.ppermute(value, 'seq', [(i, i ^ mask) for i in range(nseq)])  99.6 us
    ppermute x27, starting transfers between devices, flip(): return lax.ppermute(value, 'seq', [(i, i ^ mask) for i in range(nseq)])  50.5 us
    ppermute x12, waiting for transfers between devices, flip_z(): return lax.ppermute(value, 'dp', [(i, i ^ mask) for i in range(ndp)])  42 us
    pallas_call x2, Pallas kernels, on_device(): pl.pallas_call(functools.partial(backward_kernel, top, wide), grid_spec=p...  27.7 us
    pallas_call x1, Pallas kernels, on_device(): pl.pallas_call(hidden_kernel, grid=(TEAM,), in_specs=[by_seqs, by_seqs, p...  22.8 us
    pallas_call x1, Pallas kernels, on_device(): pl.pallas_call(functools.partial(forward_kernel, top, wide), grid_spec=pl...  20.9 us
    ppermute x12, starting transfers between devices, flip_z(): return lax.ppermute(value, 'dp', [(i, i ^ mask) for i in range(ndp)])  14.5 us
    unnamed x78, local copies, waits for them, and re-layouts  11.1 us
  transfers between devices with their start and end apart: 41, of which 23 were waited for; matrix products, arithmetic and copies ran while one was open for 12% of the time, Pallas kernels for 5%

profile of v1, /device:TPU:0, one launch (start us, length us, event | category | flops | bytes accessed | tf_op | source)
XLA Modules:
  0.0 366.0 jit_solution(10159746885891796890)
XLA Ops:
  4.6 3.0 collective-permute-start.2
  8.4 2.0 collective-permute-start.7
  11.6 2.2 collective-permute-start.3
  13.8 2.7 collective-permute-start.14
  17.6 2.1 collective-permute-start.4
  19.7 11.3 %collective-permute-done.14 = bf16[1,120,768]{2,1,0:T(8,128)(2,1)S(1)} collective-permute-done((bf16[1,120,768]{2,1,0:T(8,128)(2,1)S(1)}, bf16[1,120,768]{2,1,0:T(8,128)(2,1)S(1)}, u32[]{:S(2)}, u32[]{:S(2)}) %collective-permute-start.14) | collective-permute-done | bytes 184352 | tf_op jit(solution)/shard_map/ppermute | solution.py:370
  31.2 3.7 %collective-permute-done.4 = bf16[1,2,2,24,384]{4,3,2,1,0:T(8,128)(2,1)S(1)} collective-permute-done((bf16[1,2,2,24,384]{4,3,2,1,0:T(8,128)(2,1)S(1)}, bf16[1,2,2,24,384]{4,3,2,1,0:T(8,128)(2,1)S(1)}, u32[]{:S(2)}, u32[]{:S(2)}) %collective-permute-start.4) | collective-permute-done | bytes 73760 | tf_op jit(solution)/shard_map/ppermute | solution.py:370
  35.6 2.4 pad_maximum_fusion.2
  38.1 1.5 collective-permute-start.11
  39.6 6.3 %collective-permute-done.5 = bf16[2,2,2,24,384]{4,3,2,1,0:T(8,128)(2,1)S(1)} collective-permute-done((bf16[2,2,2,24,384]{4,3,2,1,0:T(8,128)(2,1)S(1)}, bf16[2,2,2,24,384]{4,3,2,1,0:T(8,128)(2,1)S(1)}, u32[]{:S(2)}, u32[]{:S(2)}) %collective-permute-start.5) | collective-permute-done | bytes 147488 | tf_op jit(solution)/shard_map/ppermute | solution.py:370
  46.0 1.8 collective-permute-start.6
  47.8 1.4 pad_maximum_fusion.3
  49.7 2.5 collective-permute-done.11
  53.1 1.7 collective-permute-start.12
  54.8 3.0 negate_select_fusion
  59.1 24.4 %collective-permute-done.12 = bf16[1,4,2,2,24,768]{5,4,3,2,1,0:T(8,128)(2,1)} collective-permute-done((bf16[1,4,2,2,24,768]{5,4,3,2,1,0:T(8,128)(2,1)}, bf16[1,4,2,2,24,768]{5,4,3,2,1,0:T(8,128)(2,1)}, u32[]{:S(2)}, u32[]{:S(2)}) %collective-permute-start.12) | collective-permute-done | bytes 589856 | tf_op jit(solution)/shard_map/ppermute | solution.py:367
  83.5 1.9 fusion.5
  86.6 1.6 maximum_select_fusion
  89.4 2.1 pad_maximum_fusion.x_ref
  91.5 6.7 %prepare.1 = (bf16[4,2,256,768]{3,2,1,0:T(8,128)(2,1)S(1)}, bf16[4,2,256,768]{3,2,1,0:T(8,128)(2,1)S(1)}, bf16[4,2,256,256]{3,2,1,0:T(8,128)(2,1)S(1)}, bf16[4,2,256,128]{3,2,1,0:T(8,128)(2,1)S(1)}) custom-call(bf16[4,2,256,768]{3,2,1,0:T(8,128)(2,1)S(1)} %pad_maximum_fusion.x_ref, bf16[768,384]{1,0:T(8,128)(2,1)S(1)} %bitcast.185, ...), custom_call_target="tpu_custom_call" | custom-call | flops 1207959552 | bytes 9437184 | tf_op jit(solution)/shard_map/prepare/pallas_call | solution.py:485
  98.1 1.7 copy-done.21
  99.9 1.7 collective-permute-start.9
  101.7 1.7 pad_maximum_fusion.1.grad_ref
  104.1 8.7 %collective-permute-done.9 = bf16[4,2,256,128]{3,2,1,0:T(8,128)(2,1)S(1)} collective-permute-done((bf16[4,2,256,128]{3,2,1,0:T(8,128)(2,1)S(1)}, bf16[4,2,256,128]{3,2,1,0:T(8,128)(2,1)S(1)}, u32[]{:S(2)}, u32[]{:S(2)}) %collective-permute-start.9) | collective-permute-done | bytes 524320 | tf_op jit(solution)/shard_map/ppermute | solution.py:367
  112.9 20.9 %attend.1 = (bf16[4,2,256,256]{3,2,1,0:T(8,128)(2,1)S(1)}, bf16[4,2,3,256,128]{4,3,2,1,0:T(8,128)(2,1)S(1)}) custom-call(s32[1]{0:T(128)} %bitcast.20.own_ref, bf16[4,2,256,256]{3,2,1,0:T(8,128)(2,1)S(1)} %get-tuple-element.33.query_ref, bf16[8,2,256,128]{3,2,1,0:T(8,128)(2,1)S(1)} %constant_dynamic-update-slice_fusion.keyval_ref), custom_call_target="tpu_custom_call" | custom-call | flops 4026531840 | bytes 2097152 | tf_op jit(solution)/shard_map/attend/pallas_call | solution.py:511
  133.8 6.7 %pull_context.1 = (bf16[4,2,3,256,128]{4,3,2,1,0:T(8,128)(2,1)S(1)}, f32[256,768]{1,0:T(8,128)S(1)}) custom-call(bf16[4,2,256,256]{3,2,1,0:T(8,128)(2,1)S(1)} %get-tuple-element.35.context_ref, bf16[4,2,256,768]{3,2,1,0:T(8,128)(2,1)S(1)} %pad_maximum_fusion.1.grad_ref, bf16[256,768]{1,0:T(8,128)(2,1)S(1)} %concatenate.154.out_ref), custom_call_target="tpu_custom_call" | custom-call | flops 1610612736 | bytes 6291456 | tf_op jit(solution)/shard_map/pull_context/pallas_call | solution.py:537
  140.6 13.9 %attend_back.2 = (bf16[4,256,256]{2,1,0:T(8,128)(2,1)S(1)}, f32[8,256,128]{2,1,0:T(8,128)S(1)}) custom-call(s32[1]{0:T(128)} %bitcast.20.own_ref, bf16[4,2,3,256,128]{4,3,2,1,0:T(8,128)(2,1)S(1)} %get-tuple-element.38.query_ref, bf16[4,2,3,256,128]{4,3,2,1,0:T(8,128)(2,1)S(1)} %get-tuple-element.39.grad_ref, ...), custom_call_target="tpu_custom_call" | custom-call | flops 5033164800 | bytes 2097152 | tf_op jit(solution)/shard_map/attend_back/pallas_call | solution.py:586
  156.3 13.8 %attend_back.3 = (bf16[4,256,256]{2,1,0:T(8,128)(2,1)S(1)}, f32[8,256,128]{2,1,0:T(8,128)S(1)}) custom-call(s32[1]{0:T(128)} %bitcast.20.own_ref, bf16[4,2,3,256,128]{4,3,2,1,0:T(8,128)(2,1)S(1)} %get-tuple-element.38.query_ref, bf16[4,2,3,256,128]{4,3,2,1,0:T(8,128)(2,1)S(1)} %get-tuple-element.39.grad_ref, ...), custom_call_target="tpu_custom_call" | custom-call | flops 5033164800 | bytes 2097152 | tf_op jit(solution)/shard_map/attend_back/pallas_call | solution.py:586
  171.9 22.8 %hidden.1 = (bf16[4,2,256,768]{3,2,1,0:T(8,128)(2,1)}, bf16[4,2,256,768]{3,2,1,0:T(8,128)(2,1)}, bf16[768,768]{1,0:T(8,128)(2,1)}, bf16[768,768]{1,0:T(8,128)(2,1)}) custom-call(bf16[4,2,256,768]{3,2,1,0:T(8,128)(2,1)} %copy-done.21, bf16[4,2,256,768]{3,2,1,0:T(8,128)(2,1)} %copy-done.3, bf16[4,2,256,256]{3,2,1,0:T(8,128)(2,1)} %copy-done.22, ...), custom_call_target="tpu_custom_call" | custom-call | flops 14495514624 | bytes 15728640 | tf_op jit(solution)/shard_map/hidden/pallas_call | solution.py:552
  194.7 2.3 constant_dynamic-slice_fusion.1
  197.8 24.7 %collective-permute-start.36 = (bf16[1,4,2,2,24,768]{5,4,3,2,1,0:T(8,128)(2,1)}, bf16[1,4,2,2,24,768]{5,4,3,2,1,0:T(8,128)(2,1)}, u32[]{:S(2)}, u32[]{:S(2)}) collective-permute-start(bf16[1,4,2,2,24,768]{5,4,3,2,1,0:T(8,128)(2,1)} %bitcast.175), channel_id=1, source_target_pairs={{0,8},{4,12},{8,0},{12,4},{16,24},{20,28},{24,16},{28,20},{1,9},{5... | collective-permute-start | bytes 1769480 | tf_op jit(solution)/shard_map/ppermute | solution.py:367
  224.8 2.0 collective-permute-start.19
  227.1 8.9 %pull_tokens.1 = (bf16[4,2,256,768]{3,2,1,0:T(8,128)(2,1)S(1)}, f32[768,256]{1,0:T(8,128)S(1)}, f32[8,768]{1,0:T(8,128)S(1)}) custom-call(bf16[4,2,256,768]{3,2,1,0:T(8,128)(2,1)S(1)} %pad_maximum_fusion.x_ref, bf16[4,2,256,768]{3,2,1,0:T(8,128)(2,1)S(1)} %get-tuple-element.37.normed_ref, bf16[4,2,256,768]{3,2,1,0:T(8,128)(2,1)} %get-tuple-element.43.dnormed_ref, ...), custom_call_target="tpu_custom_call" | custom-call | flops 1610612736 | bytes 12582912 | tf_op jit(solution)/shard_map/pull_tokens/pallas_call | solution.py:628
  236.9 1.3 slice.190
  238.4 1.4 copy-done.30
  239.7 1.2 slice.172
  241.0 17.4 %collective-permute-done.19 = bf16[4,256,128]{2,1,0:T(8,128)(2,1)S(1)} collective-permute-done((bf16[4,256,128]{2,1,0:T(8,128)(2,1)S(1)}, bf16[4,256,128]{2,1,0:T(8,128)(2,1)S(1)}, u32[]{:S(2)}, u32[]{:S(2)}) %collective-permute-start.19) | collective-permute-done | bytes 262176 | tf_op jit(solution)/shard_map/ppermute | solution.py:367
  258.5 2.9 collective-permute-done.22
  264.1 1.5 collective-permute-start.21
  265.7 2.7 collective-permute-done.21
  268.4 1.5 collective-permute-start.24
  269.9 2.7 collective-permute-done.24
  272.7 1.9 pull_keyval.1
  279.1 1.8 collective-permute-start.27
  280.9 1.3 fusion.6
  282.4 3.6 collective-permute-done.27
  286.2 1.3 add_convert_fusion
  287.5 2.1 collective-permute-start.33
  289.6 8.3 %collective-permute-done.28 = bf16[2,2,2,24,324]{4,3,2,1,0:T(8,128)(2,1)S(1)} collective-permute-done((bf16[2,2,2,24,324]{4,3,2,1,0:T(8,128)(2,1)S(1)}, bf16[2,2,2,24,324]{4,3,2,1,0:T(8,128)(2,1)S(1)}, u32[]{:S(2)}, u32[]{:S(2)}) %collective-permute-start.28) | collective-permute-done | bytes 124448 | tf_op jit(solution)/shard_map/ppermute | solution.py:370
  297.9 1.7 collective-permute-start.29
  299.7 1.4 collective-permute-start.38
  301.0 2.6 collective-permute-done.29
  305.5 1.6 collective-permute-start.31
  307.1 2.3 collective-permute-done.31
  313.6 1.6 collective-permute-start.40
  315.3 1.3 collective-permute-start.34
  316.7 1.3 collective-permute-done.40
  319.4 7.3 %collective-permute-done.34 = bf16[1,120,768]{2,1,0:T(8,128)(2,1)S(1)} collective-permute-done((bf16[1,120,768]{2,1,0:T(8,128)(2,1)S(1)}, bf16[1,120,768]{2,1,0:T(8,128)(2,1)S(1)}, u32[]{:S(2)}, u32[]{:S(2)}) %collective-permute-start.34) | collective-permute-done | bytes 184352 | tf_op jit(solution)/shard_map/ppermute | solution.py:370
  326.7 2.4 convert_add_fusion.1
  329.8 1.7 convert_add_fusion
  331.6 1.6 collective-permute-start.26
  335.2 14.5 %collective-permute-done.18 = bf16[2,256,768]{2,1,0:T(8,128)(2,1)S(1)} collective-permute-done((bf16[2,256,768]{2,1,0:T(8,128)(2,1)S(1)}, bf16[2,256,768]{2,1,0:T(8,128)(2,1)S(1)}, u32[]{:S(2)}, u32[]{:S(2)}) %collective-permute-start.18) | collective-permute-done | bytes 786464 | tf_op jit(solution)/shard_map/ppermute | solution.py:367
  351.0 13.6 %collective-permute-done.26 = bf16[2,256,768]{2,1,0:T(8,128)(2,1)S(1)} collective-permute-done((bf16[2,256,768]{2,1,0:T(8,128)(2,1)S(1)}, bf16[2,256,768]{2,1,0:T(8,128)(2,1)S(1)}, u32[]{:S(2)}, u32[]{:S(2)}) %collective-permute-start.26) | collective-permute-done | bytes 786464 | tf_op jit(solution)/shard_map/ppermute | solution.py:367
  364.6 1.4 fusion.1
  (240 shorter events, 40.8 us)
Async XLA Ops:
  0.6 7.0 %copy-start = (bf16[2,256,768]{2,1,0:T(8,128)(2,1)S(1)}, bf16[2,256,768]{2,1,0:T(8,128)(2,1)}, u32[]{:S(2)}) copy-start(bf16[2,256,768]{2,1,0:T(8,128)(2,1)} %x_ref.1) | copy-start | bytes 2359300
  0.7 7.1 %copy-start.35 = (bf16[24,768]{1,0:T(8,128)(2,1)S(1)}, bf16[24,768]{1,0:T(8,128)(2,1)}, u32[]{:S(2)}) copy-start(bf16[24,768]{1,0:T(8,128)(2,1)} %param.13) | copy-start | bytes 110596
  0.7 7.7 %copy-start.23 = (bf16[2,256,768]{2,1,0:T(8,128)(2,1)S(1)}, bf16[2,256,768]{2,1,0:T(8,128)(2,1)}, u32[]{:S(2)}) copy-start(bf16[2,256,768]{2,1,0:T(8,128)(2,1)} %param.18) | copy-start | bytes 2359300
  1.8 12.0 %copy-start.34 = (bf16[96,768]{1,0:T(8,128)(2,1)S(1)}, bf16[96,768]{1,0:T(8,128)(2,1)}, u32[]{:S(2)}) copy-start(bf16[96,768]{1,0:T(8,128)(2,1)} %param.15) | copy-start | bytes 442372
  4.6 6.9 %collective-permute-start.2 = (bf16[2,24,1152]{2,1,0:T(8,128)(2,1)S(1)}, bf16[2,24,1152]{2,1,0:T(8,128)(2,1)S(1)}, u32[]{:S(2)}, u32[]{:S(2)}) collective-permute-start(bf16[2,24,1152]{2,1,0:T(8,128)(2,1)S(1)} %get-tuple-element.95), channel_id=1, source_target_pairs={{0,16},{4,20},{8,24},{12,28},{16,0},{20,4},{24,8},{28,12},{1,17},{... | collective-permute-start | bytes 331784 | tf_op jit(solution)/shard_map/ppermute | solution.py:367
  7.6 28.0 %collective-permute-start = (bf16[1,2,256,768]{3,2,1,0:T(8,128)(2,1)S(1)}, bf16[1,2,256,768]{3,2,1,0:T(8,128)(2,1)}, u32[]{:S(2)}, u32[]{:S(2)}) collective-permute-start(bf16[1,2,256,768]{3,2,1,0:T(8,128)(2,1)S(1)} %bitcast.180), channel_id=1, source_target_pairs={{0,16},{4,20},{8,24},{12,28},{16,0},{20,4},{24,8},{28,12},{1,17},{... | collective-permute-start | bytes 2359304 | tf_op jit(solution)/shard_map/ppermute | solution.py:367
  7.7 2.9 collective-permute-start.13
  8.4 39.4 %collective-permute-start.7 = (bf16[1,2,256,768]{3,2,1,0:T(8,128)(2,1)S(1)}, bf16[1,2,256,768]{3,2,1,0:T(8,128)(2,1)S(1)}, u32[]{:S(2)}, u32[]{:S(2)}) collective-permute-start(bf16[1,2,256,768]{3,2,1,0:T(8,128)(2,1)S(1)} %bitcast.189), channel_id=1, source_target_pairs={{0,16},{4,20},{8,24},{12,28},{16,0},{20,4},{24,8},{28,12},{1,17},{... | collective-permute-start | bytes 2359304 | tf_op jit(solution)/shard_map/ppermute | solution.py:367
  11.6 4.9 %collective-permute-start.3 = (bf16[2,24,1152]{2,1,0:T(8,128)(2,1)S(1)}, bf16[2,24,1152]{2,1,0:T(8,128)(2,1)S(1)}, u32[]{:S(2)}, u32[]{:S(2)}) collective-permute-start(bf16[2,24,1152]{2,1,0:T(8,128)(2,1)S(1)} %get-tuple-element.93), channel_id=1, source_target_pairs={{0,4},{4,0},{8,12},{12,8},{16,20},{20,16},{24,28},{28,24},{1,5},{5... | collective-permute-start | bytes 331784 | tf_op jit(solution)/shard_map/ppermute | solution.py:367
  13.8 17.2 %collective-permute-start.14 = (bf16[1,120,768]{2,1,0:T(8,128)(2,1)S(1)}, bf16[1,120,768]{2,1,0:T(8,128)(2,1)S(1)}, u32[]{:S(2)}, u32[]{:S(2)}) collective-permute-start(bf16[1,120,768]{2,1,0:T(8,128)(2,1)S(1)} %bitcast.211), channel_id=1, source_target_pairs={{0,2},{1,3},{2,0},{3,1},{4,6},{5,7},{6,4},{7,5},{8,10},{9,11},{10,... | collective-permute-start | bytes 552968 | tf_op jit(solution)/shard_map/ppermute | solution.py:370
  16.6 21.5 %collective-permute-start.10 = (bf16[1,2,2,24,768]{4,3,2,1,0:T(8,128)(2,1)S(1)}, bf16[1,2,2,24,768]{4,3,2,1,0:T(8,128)(2,1)S(1)}, u32[]{:S(2)}, u32[]{:S(2)}) collective-permute-start(bf16[1,2,2,24,768]{4,3,2,1,0:T(8,128)(2,1)S(1)} %get-tuple-element.89), channel_id=1, source_target_pairs={{0,2},{1,3},{2,0},{3,1},{4,6},{5,7},{6,4},{7,5},{8,10},{9,11},{10,... | collective-permute-start | bytes 442376 | tf_op jit(solution)/shard_map/ppermute | solution.py:370
  17.6 17.4 %collective-permute-start.4 = (bf16[1,2,2,24,384]{4,3,2,1,0:T(8,128)(2,1)S(1)}, bf16[1,2,2,24,384]{4,3,2,1,0:T(8,128)(2,1)S(1)}, u32[]{:S(2)}, u32[]{:S(2)}) collective-permute-start(bf16[1,2,2,24,384]{4,3,2,1,0:T(8,128)(2,1)S(1)} %get-tuple-element.91), channel_id=1, source_target_pairs={{0,2},{1,3},{2,0},{3,1},{4,6},{5,7},{6,4},{7,5},{8,10},{9,11},{10,... | collective-permute-start | bytes 221192 | tf_op jit(solution)/shard_map/ppermute | solution.py:370
  31.0 18.2 %collective-permute-start.15 = (bf16[2,120,768]{2,1,0:T(8,128)(2,1)S(1)}, bf16[2,120,768]{2,1,0:T(8,128)(2,1)S(1)}, u32[]{:S(2)}, u32[]{:S(2)}) collective-permute-start(bf16[2,120,768]{2,1,0:T(8,128)(2,1)S(1)} %maximum_select_fusion.6), channel_id=1, source_target_pairs={{0,1},{1,0},{2,3},{3,2},{4,5},{5,4},{6,7},{7,6},{8,9},{9,8},{10,11... | collective-permute-start | bytes 1105928 | tf_op jit(solution)/shard_map/ppermute | solution.py:370
  34.9 11.0 %collective-permute-start.5 = (bf16[2,2,2,24,384]{4,3,2,1,0:T(8,128)(2,1)S(1)}, bf16[2,2,2,24,384]{4,3,2,1,0:T(8,128)(2,1)S(1)}, u32[]{:S(2)}, u32[]{:S(2)}) collective-permute-start(bf16[2,2,2,24,384]{4,3,2,1,0:T(8,128)(2,1)S(1)} %maximum_select_fusion.15), channel_id=1, source_target_pairs={{0,1},{1,0},{2,3},{3,2},{4,5},{5,4},{6,7},{7,6},{8,9},{9,8},{10,11... | collective-permute-start | bytes 442376 | tf_op jit(solution)/shard_map/ppermute | solution.py:370
  38.1 51.3 %collective-permute-start.1 = (bf16[2,2,256,768]{3,2,1,0:T(8,128)(2,1)}, bf16[2,2,256,768]{3,2,1,0:T(8,128)(2,1)}, u32[]{:S(2)}, u32[]{:S(2)}) collective-permute-start(bf16[2,2,256,768]{3,2,1,0:T(8,128)(2,1)} %pad_maximum_fusion.2), channel_id=1, source_target_pairs={{0,4},{4,0},{8,12},{12,8},{16,20},{20,16},{24,28},{28,24},{1,5},{5... | collective-permute-start | bytes 4718600 | tf_op jit(solution)/shard_map/ppermute | solution.py:367
  38.1 14.1 %collective-permute-start.11 = (bf16[2,2,2,24,768]{4,3,2,1,0:T(8,128)(2,1)S(1)}, bf16[2,2,2,24,768]{4,3,2,1,0:T(8,128)(2,1)S(1)}, u32[]{:S(2)}, u32[]{:S(2)}) collective-permute-start(bf16[2,2,2,24,768]{4,3,2,1,0:T(8,128)(2,1)S(1)} %maximum_select_fusion.9), channel_id=1, source_target_pairs={{0,1},{1,0},{2,3},{3,2},{4,5},{5,4},{6,7},{7,6},{8,9},{9,8},{10,11... | collective-permute-start | bytes 884744 | tf_op jit(solution)/shard_map/ppermute | solution.py:370
  46.0 11.8 %collective-permute-start.6 = (bf16[1,4,2,2,24,384]{5,4,1,3,0,2:T(8,128)(2,1)S(1)}, bf16[1,4,2,2,24,384]{5,4,1,3,0,2:T(8,128)(2,1)S(1)}, u32[]{:S(2)}, u32[]{:S(2)}) collective-permute-start(bf16[1,4,2,2,24,384]{5,4,1,3,0,2:T(8,128)(2,1)S(1)} %copy.54), channel_id=1, source_target_pairs={{0,8},{4,12},{8,0},{12,4},{16,24},{20,28},{24,16},{28,20},{1,9},{5... | collective-permute-start | bytes 884744 | tf_op jit(solution)/shard_map/ppermute | solution.py:367
  49.2 52.4 %collective-permute-start.8 = (bf16[2,2,256,768]{3,2,1,0:T(8,128)(2,1)}, bf16[2,2,256,768]{3,2,1,0:T(8,128)(2,1)}, u32[]{:S(2)}, u32[]{:S(2)}) collective-permute-start(bf16[2,2,256,768]{3,2,1,0:T(8,128)(2,1)} %pad_maximum_fusion.3), channel_id=1, source_target_pairs={{0,4},{4,0},{8,12},{12,8},{16,20},{20,16},{24,28},{28,24},{1,5},{5... | collective-permute-start | bytes 4718600 | tf_op jit(solution)/shard_map/ppermute | solution.py:367
  49.3 37.3 %collective-permute-start.16 = (bf16[1,4,120,768]{3,2,1,0:T(8,128)(2,1)S(1)}, bf16[1,4,120,768]{3,2,1,0:T(8,128)(2,1)}, u32[]{:S(2)}, u32[]{:S(2)}) collective-permute-start(bf16[1,4,120,768]{3,2,1,0:T(8,128)(2,1)S(1)} %bitcast.196), channel_id=1, source_target_pairs={{0,8},{4,12},{8,0},{12,4},{16,24},{20,28},{24,16},{28,20},{1,9},{5... | collective-permute-start | bytes 2211848 | tf_op jit(solution)/shard_map/ppermute | solution.py:367
  53.1 30.3 %collective-permute-start.12 = (bf16[1,4,2,2,24,768]{5,4,3,2,1,0:T(8,128)(2,1)}, bf16[1,4,2,2,24,768]{5,4,3,2,1,0:T(8,128)(2,1)}, u32[]{:S(2)}, u32[]{:S(2)}) collective-permute-start(bf16[1,4,2,2,24,768]{5,4,3,2,1,0:T(8,128)(2,1)} %bitcast.29), channel_id=1, source_target_pairs={{0,8},{4,12},{8,0},{12,4},{16,24},{20,28},{24,16},{28,20},{1,9},{5... | collective-permute-start | bytes 1769480 | tf_op jit(solution)/shard_map/ppermute | solution.py:367
  89.3 44.5 %copy-start.17 = (bf16[256,768]{1,0:T(8,128)(2,1)}, bf16[256,768]{1,0:T(8,128)(2,1)S(1)}, u32[]{:S(2)}) copy-start(bf16[256,768]{1,0:T(8,128)(2,1)S(1)} %concatenate.154.out_ref) | copy-start | bytes 1179652
  91.4 10.2 %copy-start.29 = (bf16[1,2,256,768]{3,2,1,0:T(8,128)(2,1)S(1)}, bf16[1,2,256,768]{3,2,1,0:T(8,128)(2,1)}, u32[]{:S(2)}) copy-start(bf16[1,2,256,768]{3,2,1,0:T(8,128)(2,1)} %copy-done.28) | copy-start | bytes 2359300
  99.9 12.9 %collective-permute-start.9 = (bf16[4,2,256,128]{3,2,1,0:T(8,128)(2,1)S(1)}, bf16[4,2,256,128]{3,2,1,0:T(8,128)(2,1)S(1)}, u32[]{:S(2)}, u32[]{:S(2)}) collective-permute-start(bf16[4,2,256,128]{3,2,1,0:T(8,128)(2,1)S(1)} %get-tuple-element.34), channel_id=1, source_target_pairs={{0,8},{4,12},{8,0},{12,4},{16,24},{20,28},{24,16},{28,20},{1,9},{5... | collective-permute-start | bytes 1572872 | tf_op jit(solution)/shard_map/ppermute | solution.py:367
  103.4 30.4 %copy-start.3 = (bf16[4,2,256,768]{3,2,1,0:T(8,128)(2,1)}, bf16[4,2,256,768]{3,2,1,0:T(8,128)(2,1)S(1)}, u32[]{:S(2)}) copy-start(bf16[4,2,256,768]{3,2,1,0:T(8,128)(2,1)S(1)} %pad_maximum_fusion.1.grad_ref) | copy-start | bytes 9437188
  133.8 6.8 %copy-start.22 = (bf16[4,2,256,256]{3,2,1,0:T(8,128)(2,1)}, bf16[4,2,256,256]{3,2,1,0:T(8,128)(2,1)S(1)}, u32[]{:S(2)}) copy-start(bf16[4,2,256,256]{3,2,1,0:T(8,128)(2,1)S(1)} %get-tuple-element.35.context_ref) | copy-start | bytes 3145732
  140.6 13.9 %copy-start.20 = (f32[256,768]{1,0:T(8,128)}, f32[256,768]{1,0:T(8,128)S(1)}, u32[]{:S(2)}) copy-start(f32[256,768]{1,0:T(8,128)S(1)} %get-tuple-element.51) | copy-start | bytes 2359300
  194.7 29.1 %copy-start.26 = (bf16[768,768]{1,0:T(8,128)(2,1)S(1)}, bf16[768,768]{1,0:T(8,128)(2,1)}, u32[]{:S(2)}) copy-start(bf16[768,768]{1,0:T(8,128)(2,1)} %get-tuple-element.52) | copy-start | bytes 3538948
  197.8 27.0 %copy-start.12 = (f32[8,256,128]{2,1,0:T(8,128)S(1)}, f32[8,256,128]{2,1,0:T(8,128)}, u32[]{:S(2)}) copy-start(f32[8,256,128]{2,1,0:T(8,128)} %copy-done.11) | copy-start | bytes 3145732
  197.8 83.1 %collective-permute-start.36 = (bf16[1,4,2,2,24,768]{5,4,3,2,1,0:T(8,128)(2,1)}, bf16[1,4,2,2,24,768]{5,4,3,2,1,0:T(8,128)(2,1)}, u32[]{:S(2)}, u32[]{:S(2)}) collective-permute-start(bf16[1,4,2,2,24,768]{5,4,3,2,1,0:T(8,128)(2,1)} %bitcast.175), channel_id=1, source_target_pairs={{0,8},{4,12},{8,0},{12,4},{16,24},{20,28},{24,16},{28,20},{1,9},{5... | collective-permute-start | bytes 1769480 | tf_op jit(solution)/shard_map/ppermute | solution.py:367
  222.5 4.3 %copy-start.10 = (f32[8,256,128]{2,1,0:T(8,128)S(1)}, f32[8,256,128]{2,1,0:T(8,128)}, u32[]{:S(2)}) copy-start(f32[8,256,128]{2,1,0:T(8,128)} %copy-done.9) | copy-start | bytes 3145732
  223.7 3.1 copy-start.31
  223.7 3.3 copy-start.14
  223.8 3.3 copy-start.16
  224.7 61.5 %collective-permute-start.32 = (bf16[1,4,120,768]{3,2,1,0:T(8,128)(2,1)}, bf16[1,4,120,768]{3,2,1,0:T(8,128)(2,1)}, u32[]{:S(2)}, u32[]{:S(2)}) collective-permute-start(bf16[1,4,120,768]{3,2,1,0:T(8,128)(2,1)} %fusion.9), channel_id=1, source_target_pairs={{0,8},{4,12},{8,0},{12,4},{16,24},{20,28},{24,16},{28,20},{1,9},{5... | collective-permute-start | bytes 2211848 | tf_op jit(solution)/shard_map/ppermute | solution.py:367
  224.8 33.6 %collective-permute-start.19 = (bf16[4,256,128]{2,1,0:T(8,128)(2,1)S(1)}, bf16[4,256,128]{2,1,0:T(8,128)(2,1)S(1)}, u32[]{:S(2)}, u32[]{:S(2)}) collective-permute-start(bf16[4,256,128]{2,1,0:T(8,128)(2,1)S(1)} %slice.339), channel_id=1, source_target_pairs={{0,8},{4,12},{8,0},{12,4},{16,24},{20,28},{24,16},{28,20},{1,9},{5... | collective-permute-start | bytes 786440 | tf_op jit(solution)/shard_map/ppermute | solution.py:367
  226.9 34.5 %collective-permute-start.22 = (bf16[4,256,128]{2,1,0:T(8,128)(2,1)S(1)}, bf16[4,256,128]{2,1,0:T(8,128)(2,1)S(1)}, u32[]{:S(2)}, u32[]{:S(2)}) collective-permute-start(bf16[4,256,128]{2,1,0:T(8,128)(2,1)S(1)} %slice.338), channel_id=1, source_target_pairs={{0,8},{4,12},{8,0},{12,4},{16,24},{20,28},{24,16},{28,20},{1,9},{5... | collective-permute-start | bytes 786440 | tf_op jit(solution)/shard_map/ppermute | solution.py:367
  238.4 91.4 %collective-permute-start.25 = (bf16[2,2,256,768]{3,2,1,0:T(8,128)(2,1)}, bf16[2,2,256,768]{3,2,1,0:T(8,128)(2,1)}, u32[]{:S(2)}, u32[]{:S(2)}) collective-permute-start(bf16[2,2,256,768]{3,2,1,0:T(8,128)(2,1)} %slice.190), channel_id=1, source_target_pairs={{0,4},{4,0},{8,12},{12,8},{16,20},{20,16},{24,28},{28,24},{1,5},{5... | collective-permute-start | bytes 4718600 | tf_op jit(solution)/shard_map/ppermute | solution.py:367
  258.4 68.3 %collective-permute-start.17 = (bf16[2,2,256,768]{3,2,1,0:T(8,128)(2,1)}, bf16[2,2,256,768]{3,2,1,0:T(8,128)(2,1)}, u32[]{:S(2)}, u32[]{:S(2)}) collective-permute-start(bf16[2,2,256,768]{3,2,1,0:T(8,128)(2,1)} %slice.172), channel_id=1, source_target_pairs={{0,4},{4,0},{8,12},{12,8},{16,20},{20,16},{24,28},{28,24},{1,5},{5... | collective-permute-start | bytes 4718600 | tf_op jit(solution)/shard_map/ppermute | solution.py:367
  261.4 1.3 collective-permute-start.20
  261.5 11.2 %copy-start.2 = (f32[4,256,128]{2,1,0:T(8,128)S(1)}, f32[4,256,128]{2,1,0:T(8,128)}, u32[]{:S(2)}) copy-start(f32[4,256,128]{2,1,0:T(8,128)} %get-tuple-element.101.cos_ref) | copy-start | bytes 1572868
  261.5 11.2 %copy-start.19 = (bf16[2,256,128]{2,1,0:T(8,128)(2,1)S(1)}, bf16[2,256,128]{2,1,0:T(8,128)(2,1)}, u32[]{:S(2)}) copy-start(bf16[2,256,128]{2,1,0:T(8,128)(2,1)} %cotangent_ref.1) | copy-start | bytes 393220
  262.7 1.3 collective-permute-start.23
  264.1 4.3 %collective-permute-start.21 = (bf16[256,128]{1,0:T(8,128)(2,1)S(1)}, bf16[256,128]{1,0:T(8,128)(2,1)S(1)}, u32[]{:S(2)}, u32[]{:S(2)}) collective-permute-start(bf16[256,128]{1,0:T(8,128)(2,1)S(1)} %fusion.25), channel_id=1, source_target_pairs={{0,16},{4,20},{8,24},{12,28},{16,0},{20,4},{24,8},{28,12},{1,17},{... | collective-permute-start | bytes 196616 | tf_op jit(solution)/shard_map/ppermute | solution.py:367
  268.4 4.3 %collective-permute-start.24 = (bf16[256,128]{1,0:T(8,128)(2,1)S(1)}, bf16[256,128]{1,0:T(8,128)(2,1)S(1)}, u32[]{:S(2)}, u32[]{:S(2)}) collective-permute-start(bf16[256,128]{1,0:T(8,128)(2,1)S(1)} %fusion.26), channel_id=1, source_target_pairs={{0,16},{4,20},{8,24},{12,28},{16,0},{20,4},{24,8},{28,12},{1,17},{... | collective-permute-start | bytes 196616 | tf_op jit(solution)/shard_map/ppermute | solution.py:367
  276.5 4.4 %copy-start.33 = (bf16[2,1,2,4,24,768]{5,4,3,2,1,0:T(8,128)(2,1)S(1)}, bf16[2,1,2,4,24,768]{5,4,3,2,1,0:T(8,128)(2,1)}, u32[]{:S(2)}) copy-start(bf16[2,1,2,4,24,768]{5,4,3,2,1,0:T(8,128)(2,1)} %get-tuple-element.84) | copy-start | bytes 1769476
  279.1 6.8 %collective-permute-start.27 = (bf16[1,4,2,2,24,324]{5,4,3,2,1,0:T(8,128)(2,1)S(1)}, bf16[1,4,2,2,24,324]{5,4,3,2,1,0:T(8,128)(2,1)S(1)}, u32[]{:S(2)}, u32[]{:S(2)}) collective-permute-start(bf16[1,4,2,2,24,324]{5,4,3,2,1,0:T(8,128)(2,1)S(1)} %dynamic-slice_bitcast_fusion.2), channel_id=1, source_target_pairs={{0,8},{4,12},{8,0},{12,4},{16,24},{20,28},{24,16},{28,20},{1,9},{5... | collective-permute-start | bytes 746504 | tf_op jit(solution)/shard_map/ppermute | solution.py:367
  280.9 5.2 %copy-start.27 = (bf16[768,768]{1,0:T(8,128)(2,1)S(1)}, bf16[768,768]{1,0:T(8,128)(2,1)}, u32[]{:S(2)}) copy-start(bf16[768,768]{1,0:T(8,128)(2,1)} %get-tuple-element.52) | copy-start | bytes 3538948
  280.9 5.2 %copy-start.32 = (bf16[192,768]{1,0:T(8,128)(2,1)S(1)}, bf16[192,768]{1,0:T(8,128)(2,1)}, u32[]{:S(2)}) copy-start(bf16[192,768]{1,0:T(8,128)(2,1)} %copy-done.31) | copy-start | bytes 884740
  282.3 17.3 %collective-permute-start.37 = (bf16[2,2,2,24,768]{4,3,2,1,0:T(8,128)(2,1)S(1)}, bf16[2,2,2,24,768]{4,3,2,1,0:T(8,128)(2,1)S(1)}, u32[]{:S(2)}, u32[]{:S(2)}) collective-permute-start(bf16[2,2,2,24,768]{4,3,2,1,0:T(8,128)(2,1)S(1)} %dynamic-slice_bitcast_fusion.1), channel_id=1, source_target_pairs={{0,1},{1,0},{2,3},{3,2},{4,5},{5,4},{6,7},{7,6},{8,9},{9,8},{10,11... | collective-permute-start | bytes 884744 | tf_op jit(solution)/shard_map/ppermute | solution.py:370
  286.1 11.8 %collective-permute-start.28 = (bf16[2,2,2,24,324]{4,3,2,1,0:T(8,128)(2,1)S(1)}, bf16[2,2,2,24,324]{4,3,2,1,0:T(8,128)(2,1)S(1)}, u32[]{:S(2)}, u32[]{:S(2)}) collective-permute-start(bf16[2,2,2,24,324]{4,3,2,1,0:T(8,128)(2,1)S(1)} %dynamic-slice_bitcast_fusion.4), channel_id=1, source_target_pairs={{0,1},{1,0},{2,3},{3,2},{4,5},{5,4},{6,7},{7,6},{8,9},{9,8},{10,11... | collective-permute-start | bytes 373256 | tf_op jit(solution)/shard_map/ppermute | solution.py:370
  287.5 27.7 %collective-permute-start.33 = (bf16[2,120,768]{2,1,0:T(8,128)(2,1)S(1)}, bf16[2,120,768]{2,1,0:T(8,128)(2,1)S(1)}, u32[]{:S(2)}, u32[]{:S(2)}) collective-permute-start(bf16[2,120,768]{2,1,0:T(8,128)(2,1)S(1)} %dynamic-slice_bitcast_fusion), channel_id=1, source_target_pairs={{0,1},{1,0},{2,3},{3,2},{4,5},{5,4},{6,7},{7,6},{8,9},{9,8},{10,11... | collective-permute-start | bytes 1105928 | tf_op jit(solution)/shard_map/ppermute | solution.py:370
  297.9 5.7 %collective-permute-start.29 = (bf16[1,2,2,24,324]{4,3,2,1,0:T(8,128)(2,1)S(1)}, bf16[1,2,2,24,324]{4,3,2,1,0:T(8,128)(2,1)S(1)}, u32[]{:S(2)}, u32[]{:S(2)}) collective-permute-start(bf16[1,2,2,24,324]{4,3,2,1,0:T(8,128)(2,1)S(1)} %dynamic-slice_convert_fusion.3), channel_id=1, source_target_pairs={{0,2},{1,3},{2,0},{3,1},{4,6},{5,7},{6,4},{7,5},{8,10},{9,11},{10,... | collective-permute-start | bytes 186632 | tf_op jit(solution)/shard_map/ppermute | solution.py:370
  299.7 12.4 %collective-permute-start.38 = (bf16[1,2,2,24,768]{4,3,2,1,0:T(8,128)(2,1)S(1)}, bf16[1,2,2,24,768]{4,3,2,1,0:T(8,128)(2,1)S(1)}, u32[]{:S(2)}, u32[]{:S(2)}) collective-permute-start(bf16[1,2,2,24,768]{4,3,2,1,0:T(8,128)(2,1)S(1)} %dynamic-slice_convert_fusion.1), channel_id=1, source_target_pairs={{0,2},{1,3},{2,0},{3,1},{4,6},{5,7},{6,4},{7,5},{8,10},{9,11},{10,... | collective-permute-start | bytes 442376 | tf_op jit(solution)/shard_map/ppermute | solution.py:370
  303.9 1.3 collective-permute-start.30
  305.5 4.0 %collective-permute-start.31 = (bf16[24,516]{1,0:T(8,128)(2,1)S(1)}, bf16[24,516]{1,0:T(8,128)(2,1)S(1)}, u32[]{:S(2)}, u32[]{:S(2)}) collective-permute-start(bf16[24,516]{1,0:T(8,128)(2,1)S(1)} %fusion.29), channel_id=1, source_target_pairs={{0,16},{4,20},{8,24},{12,28},{16,0},{20,4},{24,8},{28,12},{1,17},{... | collective-permute-start | bytes 74312 | tf_op jit(solution)/shard_map/ppermute | solution.py:367
  312.2 1.3 collective-permute-start.39
  313.6 4.4 %collective-permute-start.40 = (bf16[24,1536]{1,0:T(8,128)(2,1)S(1)}, bf16[24,1536]{1,0:T(8,128)(2,1)S(1)}, u32[]{:S(2)}, u32[]{:S(2)}) collective-permute-start(bf16[24,1536]{1,0:T(8,128)(2,1)S(1)} %fusion.23), channel_id=1, source_target_pairs={{0,16},{4,20},{8,24},{12,28},{16,0},{20,4},{24,8},{28,12},{1,17},{... | collective-permute-start | bytes 221192 | tf_op jit(solution)/shard_map/ppermute | solution.py:367
  315.3 11.3 %collective-permute-start.34 = (bf16[1,120,768]{2,1,0:T(8,128)(2,1)S(1)}, bf16[1,120,768]{2,1,0:T(8,128)(2,1)S(1)}, u32[]{:S(2)}, u32[]{:S(2)}) collective-permute-start(bf16[1,120,768]{2,1,0:T(8,128)(2,1)S(1)} %dynamic-slice_convert_fusion), channel_id=1, source_target_pairs={{0,2},{1,3},{2,0},{3,1},{4,6},{5,7},{6,4},{7,5},{8,10},{9,11},{10,... | collective-permute-start | bytes 552968 | tf_op jit(solution)/shard_map/ppermute | solution.py:370
  326.7 3.0 copy-start.5
  329.2 20.5 %collective-permute-start.18 = (bf16[2,256,768]{2,1,0:T(8,128)(2,1)S(1)}, bf16[2,256,768]{2,1,0:T(8,128)(2,1)S(1)}, u32[]{:S(2)}, u32[]{:S(2)}) collective-permute-start(bf16[2,256,768]{2,1,0:T(8,128)(2,1)S(1)} %fusion.7), channel_id=1, source_target_pairs={{0,16},{4,20},{8,24},{12,28},{16,0},{20,4},{24,8},{28,12},{1,17},{... | collective-permute-start | bytes 2359304 | tf_op jit(solution)/shard_map/ppermute | solution.py:367
  331.6 33.0 %collective-permute-start.26 = (bf16[2,256,768]{2,1,0:T(8,128)(2,1)S(1)}, bf16[2,256,768]{2,1,0:T(8,128)(2,1)S(1)}, u32[]{:S(2)}, u32[]{:S(2)}) collective-permute-start(bf16[2,256,768]{2,1,0:T(8,128)(2,1)S(1)} %fusion.8), channel_id=1, source_target_pairs={{0,16},{4,20},{8,24},{12,28},{16,0},{20,4},{24,8},{28,12},{1,17},{... | collective-permute-start | bytes 2359304 | tf_op jit(solution)/shard_map/ppermute | solution.py:367
  333.2 1.4 collective-permute-start.35
  335.2 29.3 %copy-start.8 = (f32[2,256,768]{2,1,0:T(8,128)S(1)}, f32[2,256,768]{2,1,0:T(8,128)}, u32[]{:S(2)}) copy-start(f32[2,256,768]{2,1,0:T(8,128)} %copy-done.7) | copy-start | bytes 4718596
  335.2 29.3 %copy-start.25 = (bf16[2,256,768]{2,1,0:T(8,128)(2,1)S(1)}, bf16[2,256,768]{2,1,0:T(8,128)(2,1)}, u32[]{:S(2)}) copy-start(bf16[2,256,768]{2,1,0:T(8,128)(2,1)} %param.18) | copy-start | bytes 2359300
  (13 other events, 19.9 us)

commit v2 on v1

v2 whole, which is shorter than its diff:
```python
import functools
import math

import jax
import jax.numpy as jnp
from jax import lax
from jax.experimental import pallas as pl
from jax.experimental.pallas import tpu as pltpu
from jax.sharding import PartitionSpec as P

HEADS = 12
HEAD = 64
ROT = 16
TEAM = 4
MINE = HEADS // TEAM
WIDE = 2 * HEAD
EPSILON = 1e-05
BF = jnp.bfloat16
F32 = jnp.float32
SCALE = 1.0 / math.sqrt(HEAD)
MB = 1 << 20


def dot(left, right):
    return lax.dot_general(left, right, (((1,), (0,)), ((), ())), preferred_element_type=F32)


def dot_rt(left, right):
    return lax.dot_general(left, right, (((1,), (1,)), ((), ())), preferred_element_type=F32)


def dot_lt(left, right):
    return lax.dot_general(left, right, (((0,), (0,)), ((), ())), preferred_element_type=F32)


def lanes(shape):
    return lax.broadcasted_iota(jnp.int32, shape, len(shape) - 1)


def turn(values, cos_table, sin_table, sign):
    near = (lanes(values.shape) % HEAD) < ROT // 2
    swapped = jnp.where(
        near, pltpu.roll(values, WIDE - ROT // 2, 1), pltpu.roll(values, ROT // 2, 1)
    )
    return values * cos_table + (sign * swapped) * sin_table


def standardize(tokens):
    center = tokens - jnp.mean(tokens, axis=-1, keepdims=True)
    spread = jnp.mean(center * center, axis=-1, keepdims=True)
    scale = lax.rsqrt(spread + EPSILON)
    return center * scale, scale


def norm_back(hat, scale, pulled):
    return scale * (
        pulled
        - jnp.mean(pulled, axis=-1, keepdims=True)
        - hat * jnp.mean(pulled * hat, axis=-1, keepdims=True)
    )


def three_parts(column):
    high = column.astype(BF)
    rest = column - high.astype(F32)
    mid = rest.astype(BF)
    low = (rest - mid.astype(F32)).astype(BF)
    return high, mid, low


def marked(lane, base, parts):
    out = jnp.zeros(lane.shape, BF)
    for index, part in enumerate(parts):
        out = jnp.where(lane == base + index, part, out)
    return out


def choose(r, refs, held):
    for index, ref in enumerate(refs):

        @pl.when(r == index)
        def _(ref=ref):
            held[...] = ref[...].reshape(held.shape)


def put(r, near_ref, far_ref, value):
    @pl.when(r < 2)
    def _():
        near_ref[0] = value

    @pl.when(r >= 2)
    def _():
        far_ref[0] = value


def assemble(own_x, refs, groups, held):
    wide = sum(ref.shape[0] for ref in refs)
    relative = 0
    for ref in refs:
        block = ref.shape[2]
        for index in range(ref.shape[0]):
            x = own_x ^ relative
            for group in range(groups):
                place = (group // 2 * wide + x) * 2 + group % 2 if groups > 1 else x
                start = pl.multiple_of(place * block, block)
                held[pl.ds(start, block), :] = ref[index, group]
            relative += 1


def prepare_kernel(parts, first, own_ref, *refs):
    x_refs, refs = refs[:4], refs[4:]
    front_refs, refs = refs[:parts], refs[parts:]
    cos_ref, sin_ref, attn_ref, mlp_ref, query_ref, keyval_ref, *refs = refs
    if first:
        front_ref, norm_ref, held = refs

        @pl.when(pl.program_id(0) == 0)
        def _():
            assemble(own_ref[0], front_refs, TEAM, front_ref)
            tail = front_ref[:, 2 * WIDE :].astype(F32)
            norm_ref[...] = jnp.transpose(tail)[HEAD : HEAD + 8]
    else:
        (held,) = refs
        front_ref, norm_ref = front_refs
    choose(pl.program_id(0), x_refs, held)
    hat, _ = standardize(held[...].astype(F32))
    normed = (hat * norm_ref[0:1, :] + norm_ref[2:3, :]).astype(BF)
    attn_ref[0] = normed
    mlp_ref[0] = (hat * norm_ref[1:2, :] + norm_ref[3:4, :]).astype(BF)
    made = dot(normed, front_ref[...])
    cos_table = cos_ref[0]
    sin_table = sin_ref[0]
    keys_side = lanes(cos_table.shape) < HEAD
    keyval_ref[0] = turn(
        made[:, :WIDE], jnp.where(keys_side, cos_table, 1.0), jnp.where(keys_side, sin_table, 0.0), 1.0
    ).astype(BF)
    for part in range(2):
        piece = made[:, WIDE * (part + 1) : WIDE * (part + 2)]
        query_ref[0, :, WIDE * part : WIDE * (part + 1)] = (
            turn(piece, cos_table, sin_table, 1.0) * SCALE
        ).astype(BF)


def rank_of(own, block, top):
    return own ^ ((block % 2) * top) ^ (block // 2)


def slot_of(away, top, wide):
    return ((away // 2) % wide) * TEAM + (away // top) % 2 + 2 * (away % 2)


def load_keyval(refs, keys_ref, values_ref, base):
    start = 0
    for ref in refs:
        count, rows, _ = ref.shape
        lane = lanes((rows, WIDE))
        for index in range(count):
            block = ref[index]
            keys_ref[start + index] = jnp.where(lane < HEAD, block, base[1])
            values_ref[start + index] = jnp.where(lane < HEAD, base[0], block)
        start += count


def forward_kernel(top, wide, own_ref, query_ref, *refs):
    kv_refs, (context_ref, marked_ref, low_ref, score_ref, peak_ref, keys_ref, values_ref) = refs[:-7], refs[-7:]
    rows = query_ref.shape[1]
    own = own_ref[0]
    rank = rank_of(own, pl.program_id(0), top)
    lane = lanes((rows, WIDE))
    one = jnp.ones((rows, WIDE), BF)

    @pl.when(pl.program_id(0) == 0)
    def _():
        load_keyval(kv_refs, keys_ref, values_ref, (one, jnp.zeros_like(one)))

    first = query_ref[0, :, :WIDE]
    low_ref[:rows] = first
    low_ref[rows : 2 * rows] = pltpu.roll(first.astype(F32), HEAD, 1).astype(BF)
    low_ref[2 * rows :] = query_ref[0, :, WIDE:]
    keep = lax.broadcasted_iota(jnp.int32, (rows, rows), 1) <= lax.broadcasted_iota(
        jnp.int32, (rows, rows), 0
    )
    keep = jnp.concatenate([keep] * MINE, axis=0)

    def score(step, masked):
        scores = dot_rt(low_ref[...], keys_ref[slot_of(step ^ own, top, wide)])
        if masked:
            scores = jnp.where(keep, scores, -1e30)
        score_ref[step] = scores
        best = jnp.maximum(scores[:, :WIDE], scores[:, WIDE:])
        peak_ref[...] = best if masked else jnp.maximum(peak_ref[...], best)

    score(rank, True)

    @pl.loop(0, rank)
    def _(step):
        score(step, False)

    peak_ref[...] = jnp.broadcast_to(jnp.max(peak_ref[...], axis=-1, keepdims=True), peak_ref.shape)

    def weigh(step, sums):
        peak = peak_ref[...]
        weights = jnp.exp(score_ref[step] - jnp.concatenate([peak] * (rows // WIDE), axis=1))
        return sums + dot(weights.astype(BF), values_ref[slot_of(step ^ own, top, wide)])

    sums = lax.fori_loop(0, rank + 1, weigh, jnp.zeros((MINE * rows, WIDE), F32))
    made = []
    for head in range(MINE):
        at = slice(head * rows, (head + 1) * rows)
        part = sums[at]
        swapped = pltpu.roll(part, HEAD, 1)
        total = jnp.where(lane < HEAD, part, swapped)
        made.append(jnp.where(lane < HEAD, swapped, part) / total)
        logsum = peak_ref[at] + jnp.log(total)
        marked_ref[0, head] = jnp.where(
            lane < HEAD, low_ref[at], marked(lane, HEAD, three_parts(-logsum))
        )
    context_ref[0, :, :WIDE] = jnp.where(lane < HEAD, made[0], made[1]).astype(BF)
    context_ref[0, :, WIDE:] = jnp.where(lane < HEAD, made[2], 0.0).astype(BF)


def backward_kernel(top, wide, own_ref, query_ref, grad_ref, cos_ref, sin_ref, *refs):
    kv_refs, (dquery_ref, keep_ref, send_ref, sum_ref, keys_ref, values_ref, dkeyval_ref) = refs[:-7], refs[-7:]
    rows = query_ref.shape[2]
    own = own_ref[0]
    rank = rank_of(own, pl.program_id(0), top)
    lane = lanes((rows, WIDE))
    keep = lax.broadcasted_iota(jnp.int32, (rows, rows), 0) <= lax.broadcasted_iota(
        jnp.int32, (rows, rows), 1
    )

    @pl.when(pl.program_id(0) == 0)
    def _():
        dkeyval_ref[...] = jnp.zeros_like(dkeyval_ref)
        ones_low = jnp.where(lane < 3, 1.0, 0.0).astype(BF)
        ones_high = jnp.where((lane >= HEAD) & (lane < HEAD + 3), 1.0, 0.0).astype(BF)
        load_keyval(kv_refs, keys_ref, values_ref, (ones_low, ones_high))

    def visit(step, masked):
        slot = slot_of(step ^ own, top, wide)
        keys = keys_ref[slot]
        values = values_ref[slot]
        d_keys = jnp.zeros((rows, WIDE), F32)
        d_values = jnp.zeros((rows, WIDE), F32)
        for head in range(MINE):
            query = query_ref[0, head]
            grad = grad_ref[0, head]
            probs = jnp.exp(dot_rt(keys, query))
            if masked:
                probs = jnp.where(keep, probs, 0.0)
            d_scores = (probs * dot_rt(values, grad)).astype(BF)
            d_values += dot(probs.astype(BF), grad)
            d_keys += dot(d_scores, query)
            d_query = dot_lt(keys, d_scores)
            sum_ref[head] = d_query if masked else sum_ref[head] + d_query
        dkeyval_ref[slot] += jnp.where(lane < HEAD, d_keys, d_values)

    visit(rank, True)

    @pl.loop(0, rank)
    def _(step):
        visit(step, False)

    turned = [jnp.transpose(sum_ref[head]) * SCALE for head in range(MINE)]
    both = jnp.where(lane < HEAD, turned[0], pltpu.roll(turned[1], HEAD, 1))
    last = jnp.where(lane < HEAD, turned[2], 0.0)
    cos_table = cos_ref[0]
    sin_table = sin_ref[0]
    dquery_ref[0, :, :WIDE] = turn(both, cos_table, sin_table, -1.0).astype(BF)
    dquery_ref[0, :, WIDE:] = turn(last, cos_table, sin_table, -1.0).astype(BF)

    @pl.when(pl.program_id(0) == pl.num_programs(0) - 1)
    def _():
        half = send_ref.shape[0]
        keep_ref[...] = dkeyval_ref[:half]
        send_ref[...] = dkeyval_ref[half:].astype(BF)


def split_rows(own_x, groups, total, keep_ref, send_ref):
    wide = 2 * keep_ref.shape[0]
    block = keep_ref.shape[2]
    for side, ref in enumerate((keep_ref, send_ref)):
        half = own_x // (wide // 2) ^ side
        for index in range(wide // 2):
            x = half * (wide // 2) + index
            for group in range(groups):
                place = (group // 2 * wide + x) * 2 + group % 2 if groups > 1 else x
                start = pl.multiple_of(place * block, block)
                ref[index, group] = total[pl.ds(start, block), :].astype(ref.dtype)


def hidden_kernel(count, parts, own_ref, *refs):
    grad_refs, refs = refs[:4], refs[4:]
    normed_refs, refs = refs[:count], refs[count:]
    context_refs, refs = refs[:count], refs[count:]
    more_refs, refs = refs[:parts], refs[parts:]
    down_refs, refs = refs[:parts], refs[parts:]
    (made_ref, made_far_ref, dnormed_ref, marked_ref, more_keep, more_send, down_keep, down_send, *refs) = refs
    (up_sum, down_sum, out_sum, held, up_ref, down_ref, out_ref) = refs
    step = pl.program_id(0)
    own_x = own_ref[0]

    @pl.when(step == 0)
    def _():
        out_ref[...] = jnp.zeros_like(out_ref)
        assemble(own_x, more_refs, TEAM, up_ref)
        assemble(own_x, [ref.at[:, TEAM:] for ref in more_refs], 1, out_ref)
        assemble(own_x, down_refs, 1, down_ref)

    rows = normed_refs[0].shape[1]
    normed = jnp.concatenate([ref[0] for ref in normed_refs], axis=0)
    context = jnp.concatenate([ref[0] for ref in context_refs], axis=0)
    choose(step, grad_refs, held)
    grad = held[...]
    raw = dot(normed, up_ref[...])
    bell = 0.5 + 0.5 * lax.erf(raw * math.sqrt(0.5))
    slope = bell + raw * (jnp.exp(raw * raw * -0.5) * (1.0 / math.sqrt(2.0 * math.pi)))
    hidden = (raw * bell).astype(BF)
    d_raw = (dot_rt(grad, down_ref[...]) * slope).astype(BF)
    made = dot(hidden, down_ref[...]) + dot(context, out_ref[...])
    put(step, made_ref, made_far_ref, made.astype(BF).reshape(made_ref.shape[1:]))
    dnormed_ref[0] = dot_rt(d_raw, up_ref[...]).astype(BF).reshape(dnormed_ref.shape[1:])
    gdown = dot_lt(hidden, grad)
    gup = dot_lt(normed, d_raw)
    gout = dot_lt(context, grad)

    pulled = dot_rt(grad, out_ref[...]).astype(BF)
    product = pulled.astype(F32) * context.astype(F32)
    lane = lanes((count * rows, WIDE))
    for head in range(MINE):
        column = WIDE * (head // 2)
        side = (lane < HEAD) if head % 2 == 0 else (lane >= HEAD)
        delta = jnp.sum(
            jnp.where(side, product[:, column : column + WIDE], 0.0), axis=-1, keepdims=True
        )
        piece = pulled[:, column : column + WIDE]
        if head % 2 == 0:
            piece = pltpu.roll(piece.astype(F32), HEAD, 1).astype(BF)
        piece = jnp.where(
            lane >= HEAD, piece, marked(lane, 0, three_parts(jnp.broadcast_to(-delta, lane.shape)))
        )
        marked_ref[0, :, head] = piece.reshape(count, rows, WIDE)

    @pl.when(step == 0)
    def _():
        down_sum[...] = gdown
        up_sum[...] = gup
        out_sum[...] = gout

    @pl.when(step > 0)
    def _():
        down_sum[...] += gdown
        up_sum[...] += gup
        out_sum[...] += gout

    @pl.when(step == pl.num_programs(0) - 1)
    def _():
        split_rows(own_x, TEAM, up_sum, more_keep, more_send)
        split_rows(own_x, 1, out_sum, more_keep.at[:, TEAM:], more_send.at[:, TEAM:])
        split_rows(own_x, 1, down_sum, down_keep, down_send)


def tokens_kernel(last, own_ref, x0_ref, x1_ref, x2_ref, x3_ref, normed_ref, dnormed_ref, dquery_ref, dkeyval_ref, cotangent_ref, weight_ref, norm_ref, cos_ref, sin_ref, *refs):
    if last:
        start_ref, nstart_ref, dx_ref, dx_far_ref, keep_ref, send_ref, gfront_ref, gnorm_ref, held = refs
    else:
        dx_ref, dx_far_ref, gfront_ref, gnorm_ref, held = refs
    step = pl.program_id(0)
    choose(step, (x0_ref, x1_ref, x2_ref, x3_ref), held)
    hat, scale = standardize(held[...].astype(F32))
    cos_table = cos_ref[0]
    keys_side = lanes(cos_table.shape) < HEAD
    d_keyval = dkeyval_ref[0] + jnp.where(step == 0, cotangent_ref[0].astype(F32), 0.0)
    d_keyval = turn(
        d_keyval, jnp.where(keys_side, cos_table, 1.0), jnp.where(keys_side, sin_ref[0], 0.0), -1.0
    ).astype(BF)
    d_front = jnp.concatenate([d_keyval, dquery_ref[0]], axis=1)
    d_attn = dot_rt(d_front, weight_ref[...])
    d_mlp = dnormed_ref[0, 0].astype(F32)
    d_tokens = norm_back(hat, scale, d_attn * norm_ref[0:1, :] + d_mlp * norm_ref[1:2, :])
    put(step, dx_ref, dx_far_ref, d_tokens.astype(BF))
    sums = [
        jnp.sum(piece, axis=0, keepdims=True) for piece in (d_attn * hat, d_mlp * hat, d_attn, d_mlp)
    ]
    sums = jnp.concatenate(sums + [jnp.zeros_like(sums[0])] * 4, axis=0)
    gfront = dot_lt(normed_ref[0], d_front)

    @pl.when(step == 0)
    def _():
        gfront_ref[...] = start_ref[...] + gfront if last else gfront
        gnorm_ref[...] = nstart_ref[...] + sums if last else sums

    @pl.when(step > 0)
    def _():
        gfront_ref[...] += gfront
        gnorm_ref[...] += sums

    if last:

        @pl.when(step == pl.num_programs(0) - 1)
        def _():
            width = gnorm_ref.shape[1]
            sums = jnp.concatenate(
                [jnp.zeros((HEAD, width), F32), gnorm_ref[...], jnp.zeros((HEAD - 8, width), F32)], axis=0
            )
            gfront_ref[:, 2 * WIDE :] += jnp.transpose(sums)
            split_rows(own_ref[0], TEAM, gfront_ref, keep_ref, send_ref)


def params(limit):
    return pltpu.CompilerParams(vmem_limit_bytes=limit * MB)


def cost(micros):
    return pl.CostEstimate(flops=int(micros * 1.1e9), bytes_accessed=0, transcendentals=0)


def struct(shape, kind):
    return jax.ShapeDtypeStruct(shape, kind)


def whole(*shape):
    return pl.BlockSpec(shape, lambda *_: (0,) * len(shape))


def on_device(nseq, ndp, inputs, w_query, w_keyval, w_out, w_up, w_down, norm_gain, norm_bias, out_cotangent, kv_cotangent):
    count, rows, width = inputs.shape
    top = nseq // 2
    wide = nseq // TEAM
    own = lax.axis_index("seq")
    own_y, own_x, own_c = own // top, (own // 2) % wide, own % 2
    own_z = lax.axis_index("dp")
    share = w_query.shape[0]
    down_share = w_down.shape[0]
    hidden = w_up.shape[1] // TEAM
    heads_wide = MINE * HEAD
    front_wide = 3 * WIDE
    slots = TEAM * wide

    def flip(value, mask, what):
        with jax.named_scope("swap_" + what):
            return lax.ppermute(value, "seq", [(i, i ^ mask) for i in range(nseq)])

    def flip_z(value, mask, what):
        with jax.named_scope("swap_" + what):
            return lax.ppermute(value, "dp", [(i, i ^ mask) for i in range(ndp)])

    def hold(*values):
        return lax.optimization_barrier(values)

    def after(value, *others):
        return hold(value, *others)[0]

    def in_order(bit, mine, other, axis):
        return jnp.where(
            bit == 0, jnp.stack([mine, other], axis), jnp.stack([other, mine], axis)
        )

    def merge(value, axis):
        return value.reshape(value.shape[:axis] + (-1,) + value.shape[axis + 2 :])

    def pick(value, index, axis):
        return lax.dynamic_index_in_dim(value, index, axis, keepdims=False)

    def swap_z(value, mask, axis, what):
        other = flip_z(value, mask, f"{what}_z{mask}")

        def join(other):
            return merge(in_order((own_z // mask) % 2, value, other, axis + 1), axis)

        return other, join

    def gather_z(value, axis, what, step=None):
        masks = [ndp >> (index + 1) for index in range(ndp.bit_length() - 1)]
        for mask in masks if step is None else masks[step]:
            other, join = swap_z(value, mask, axis, what)
            value = join(other)
        return value

    def gather_x(value, what):
        parts = [value[None]]
        mask = 1
        while mask < wide:
            sent = jnp.concatenate(parts) if mask > 1 else parts[0]
            parts.append(flip(sent, 2 * mask, f"{what}_x{mask}"))
            mask *= 2
        return parts

    def flip_x(send, what):
        return flip(send, wide, f"{what}_x{wide // 2}")

    def scatter_x(keep, got, what):
        mask = wide // 2
        while True:
            value = keep.astype(F32) + got.astype(F32)
            mask //= 2
            if mask == 0:
                return value[0]
            bit = (own_x // mask) % 2
            value = value.reshape((2, -1) + value.shape[1:])
            keep = pick(value, bit, 0)
            got = flip(pick(value, 1 - bit, 0).astype(BF), 2 * mask, f"{what}_x{mask}")

    def halve_z(value, axis, what, mask):
        bit = (own_z // mask) % 2
        value = value.reshape(value.shape[:axis] + (-1, 2) + value.shape[axis + 1 :])
        got = flip_z(pick(value, 1 - bit, axis + 1).astype(BF), mask, f"{what}_z{mask}")
        return pick(value, bit, axis + 1), got

    def add_z(pair):
        return pair[0].astype(F32) + pair[1].astype(F32)

    def finish_z(value, axis, what):
        mask = 2
        while mask < ndp:
            value = add_z(halve_z(value, axis, what, mask))
            mask *= 2
        return jnp.squeeze(value, axis)

    def moved(onward):
        pairs = []
        for rank in range(nseq):
            for z in range(ndp):
                member = 2 * (rank // top) + rank % 2
                place = ((rank // 2) % wide) * ndp + z
                pairs.append((member * (nseq * ndp // TEAM) + place, rank * ndp + z))
        return [pair if onward else pair[::-1] for pair in pairs]

    def team(value, what, first, second):
        across = flip(after(value, first), top, what + "_y")
        return [value, across, flip(value, 1, what + "_c"), flip(after(across, second), 1, what + "_yc")]

    norms = jnp.concatenate([norm_gain, norm_bias], axis=1)
    queries_of = w_query.reshape(share, 2, 2, heads_wide).transpose(1, 2, 0, 3)
    same = jnp.concatenate([w_keyval, norms], axis=1)
    ups = w_up.reshape(share, 2, wide, 2, hidden // wide).transpose(1, 3, 0, 2, 4)
    ups = ups.reshape(2, 2, share, hidden)
    pad = jnp.zeros((2, 2, share, 2 * WIDE - heads_wide - norms.shape[1]), BF)
    spread = (2, 2, share)
    pack = jnp.concatenate(
        [
            jnp.broadcast_to(same[:, :WIDE], spread + (WIDE,)),
            queries_of,
            jnp.broadcast_to(same[:, WIDE:], spread + (norms.shape[1],)),
            pad,
            ups,
        ],
        axis=3,
    )
    masks = [ndp >> (index + 1) for index in range(ndp.bit_length() - 1)]
    near_masks, far_masks = masks[-1:], masks[:-1]

    def spread_z(value, axis, what, some):
        for mask in some:
            other, join = swap_z(value, mask, axis, what)
            value = join(other)
        return value

    def begin_z(value, axis, what, some):
        if not some:
            return value, lambda value: value
        return swap_z(spread_z(value, axis, what, some[:-1]), some[-1], axis, what)

    pack_y = flip(pick(pack, 1 - own_y, 0), top, "pack_y")
    with jax.named_scope("swap_out_moved"):
        out_rows = lax.ppermute(w_out, ("seq", "dp"), moved(True))
    sequences = [inputs[b : b + 1] for b in range(count)]
    across = []
    before = pack_y
    for b in range(count):
        across.append(flip(after(sequences[b], before), top, f"tokens{b}_y"))
        before = across[b]
    tokens_c = [flip(sequences[b], 1, f"tokens{b}_c") for b in range(count)]
    pack = in_order(own_y, pick(pack, own_y, 0), pack_y, 0)
    pack_c = flip(pick(pack, 1 - own_c, 1), 1, "pack_c")
    pack, pack_c, out_rows = hold(pack, pack_c, out_rows)
    pack = in_order(own_c, pick(pack, own_c, 1), pack_c, 1)

    front_z = pack[..., :front_wide].reshape(TEAM, 1, share, front_wide)
    front_z = spread_z(front_z, 1, "front", far_masks)
    front_z = spread_z(front_z, 1, "front", near_masks)
    front_z, pack, across[0], down_z = hold(front_z, pack, across[0], w_down[None])
    down_got, join_down = begin_z(down_z, 0, "down", far_masks)
    tokens = [[sequences[0], across[0], tokens_c[0], flip(across[0], 1, "tokens0_yc")]]
    front_parts = gather_x(front_z.reshape(TEAM, ndp * share, front_wide), "front")
    front_parts, tokens[0], pack, down_got = hold(front_parts, tokens[0], pack, down_got)

    lane = jnp.arange(WIDE, dtype=jnp.int32) % HEAD
    frequency = jnp.exp(
        -math.log(10000.0) * ((lane % (ROT // 2)).astype(F32) * (2.0 / ROT))
    )
    ranks = jnp.stack([rank_of(own, r, top) for r in range(TEAM)])
    positions = ranks[:, None] * rows + jnp.arange(rows, dtype=jnp.int32)[None]
    angles = (positions.astype(F32) * 0.25)[..., None] * frequency
    cos_table = jnp.where(lane < ROT, jnp.cos(angles), 1.0)
    sin_table = jnp.where(lane < ROT, jnp.sin(angles), 0.0)
    sin_table = jnp.where(lane < ROT // 2, -sin_table, sin_table)
    own_rank = own.reshape(1).astype(jnp.int32)
    own_place = own_x.reshape(1).astype(jnp.int32)

    def by_r(*last):
        return pl.BlockSpec((1,) + last, lambda r, *_: (r,) + (0,) * len(last))

    one_sequence = [pl.BlockSpec((1, rows, width), lambda r, *_: (0, 0, 0)) for _ in range(TEAM)]

    def near(*last):
        return pl.BlockSpec((1,) + last, lambda r, *_: (jnp.minimum(r, 1),) + (0,) * len(last))

    def far(*last):
        return pl.BlockSpec((1,) + last, lambda r, *_: (jnp.maximum(r - 2, 0),) + (0,) * len(last))

    def call(kernel, scalar, inputs, in_specs, out_specs, out_shape, scratch, limit, micros, name):
        return pl.pallas_call(
            kernel,
            grid_spec=pltpu.PrefetchScalarGridSpec(
                num_scalar_prefetch=1,
                grid=(TEAM,),
                in_specs=in_specs,
                out_specs=out_specs,
                scratch_shapes=scratch,
            ),
            out_shape=out_shape,
            compiler_params=params(limit),
            cost_estimate=cost(micros),
            name=name,
        )(scalar, *inputs)

    table = by_r(rows, WIDE)
    block = pltpu.VMEM((rows, width), BF)

    def prepare(b, weights):
        first = b == 0
        more_out = [struct((width, front_wide), BF), struct((8, width), F32)] if first else []
        return call(
            functools.partial(prepare_kernel, len(weights), first),
            own_place,
            [*tokens[b], *weights, cos_table, sin_table],
            one_sequence + [whole(*part.shape) for part in weights] + [table, table],
            [by_r(rows, width), by_r(rows, width), by_r(rows, 2 * WIDE), by_r(rows, WIDE)]
            + [whole(*out.shape) for out in more_out],
            [
                struct((TEAM, rows, width), BF),
                struct((TEAM, rows, width), BF),
                struct((TEAM, rows, 2 * WIDE), BF),
                struct((TEAM, rows, WIDE), BF),
            ]
            + more_out,
            [block],
            56,
            4,
            "prepare",
        )

    more = jnp.concatenate(
        [pack[..., front_wide:].reshape(TEAM, share, hidden), out_rows.reshape(1, share, width)]
    )
    down_got, join_near = begin_z(join_down(down_got), 0, "down", near_masks)

    *made_first, front, norm_rows = prepare(0, front_parts)
    prepared = [made_first]
    prepared[0], front, across[1:], more = hold(prepared[0], front, across[1:], more)
    for b in range(1, count):
        tokens.append([sequences[b], across[b], tokens_c[b], flip(across[b], 1, f"tokens{b}_yc")])
    more_got, join_more = begin_z(more[:, None], 1, "more", far_masks)
    prepared += [prepare(b, [front, norm_rows]) for b in range(1, count)]
    normed_attn, normed_mlp, queries, keyvals = [list(part) for part in zip(*prepared)]

    def keys_of_all(value, what):
        parts = [value]
        mask = 1
        while mask < wide:
            sent = jnp.concatenate(parts) if mask > 1 else parts[0]
            parts.append(flip(sent, 2 * mask, f"{what}_x{mask}"))
            mask *= 2
        return parts

    everyone = [keys_of_all(keyvals[b], f"keyval{b}") for b in range(count)]
    kv_specs = [whole(*part.shape) for part in everyone[0]]
    kv_scratch = [pltpu.VMEM((slots, rows, WIDE), BF)] * 2

    grads_y = flip(after(out_cotangent, tokens[-1][1]), top, "grads_y")
    grads_c = flip(out_cotangent, 1, "grads_c")
    everyone[0], queries, keyvals, more_got, down_got = hold(
        everyone[0], queries, keyvals, more_got, down_got
    )
    down_z = join_near(down_got)
    more_z = join_more(more_got)
    down_parts = gather_x(down_z.reshape(1, ndp * down_share, width), "down")
    more_got, join_more = begin_z(more_z, 1, "more", near_masks)

    contexts = []
    marked_queries = []
    for b in range(count):
        context, marked_query = call(
            functools.partial(forward_kernel, top, wide),
            own_rank,
            [queries[b], *everyone[b]],
            [by_r(rows, 2 * WIDE)] + kv_specs,
            [by_r(rows, 2 * WIDE), by_r(MINE, rows, WIDE)],
            [struct((TEAM, rows, 2 * WIDE), BF), struct((TEAM, MINE, rows, WIDE), BF)],
            [
                pltpu.VMEM((MINE * rows, WIDE), BF),
                pltpu.VMEM((slots, MINE * rows, rows), F32),
                pltpu.VMEM((MINE * rows, WIDE), F32),
            ]
            + kv_scratch,
            24,
            15,
            "attend",
        )
        contexts.append(context)
        marked_queries.append(marked_query)
        if b == 0:
            contexts[0], everyone[1:], queries, more_got, grads_y = hold(
                contexts[0], everyone[1:], queries, more_got, grads_y
            )
            more_z = join_more(more_got)
            grads = [out_cotangent, grads_y, grads_c, flip(grads_y, 1, "grads_yc")]
            more_parts = gather_x(more_z.reshape(TEAM + 1, ndp * share, width), "more")
    contexts, grads, more_parts, down_parts = hold(contexts, grads, more_parts, down_parts)

    half = max(wide // 2, 1)
    more_half = (half, TEAM + 1, ndp * share, width)
    down_half = (half, 1, ndp * down_share, width)
    both = pl.BlockSpec((count, rows, width), lambda r, *_: (0, 0, 0))
    made, made_far, d_normed, marked_grad, more_keep, more_send, down_keep, down_send = call(
        functools.partial(hidden_kernel, count, len(more_parts)),
        own_place,
        [*grads, *normed_mlp, *contexts, *more_parts, *down_parts],
        [both] * TEAM
        + [by_r(rows, width)] * count
        + [by_r(rows, 2 * WIDE)] * count
        + [whole(*part.shape) for part in more_parts + down_parts],
        [
            near(count, rows, width),
            far(count, rows, width),
            by_r(count, rows, width),
            by_r(count, MINE, rows, WIDE),
            whole(*more_half),
            whole(*more_half),
            whole(*down_half),
            whole(*down_half),
        ],
        [
            struct((2, count, rows, width), BF),
            struct((2, count, rows, width), BF),
            struct((TEAM, count, rows, width), BF),
            struct((TEAM, count, MINE, rows, WIDE), BF),
            struct(more_half, BF),
            struct(more_half, BF),
            struct(down_half, BF),
            struct(down_half, BF),
        ],
        [
            pltpu.VMEM((width, hidden), F32),
            pltpu.VMEM((hidden, width), F32),
            pltpu.VMEM((2 * WIDE, width), F32),
            pltpu.VMEM((count * rows, width), BF),
            pltpu.VMEM((width, hidden), BF),
            pltpu.VMEM((hidden, width), BF),
            pltpu.VMEM((2 * WIDE, width), BF),
        ],
        52,
        27,
        "hidden",
    )

    def sum_c(value, what, *others):
        return value[0].astype(F32) + after(flip(value[1], 1, what + "_c"), *others).astype(F32)

    def sum_y(value, what, *others):
        got = flip(value[1].astype(BF), top, what + "_y")
        return value[0] + after(got, *others).astype(F32)

    d_queries = []
    kept = []
    sent = []
    key_half = (slots // 2, rows, WIDE)
    for b in range(count):
        d_query, keep, send = call(
            functools.partial(backward_kernel, top, wide),
            own_rank,
            [marked_queries[b], marked_grad, cos_table, sin_table, *everyone[b]],
            [
                by_r(MINE, rows, WIDE),
                pl.BlockSpec((1, None, MINE, rows, WIDE), lambda r, *_, b=b: (r, b, 0, 0, 0)),
                table,
                table,
            ]
            + kv_specs,
            [by_r(rows, 2 * WIDE), whole(*key_half), whole(*key_half)],
            [struct((TEAM, rows, 2 * WIDE), BF), struct(key_half, F32), struct(key_half, BF)],
            [pltpu.VMEM((MINE, WIDE, rows), F32)] + kv_scratch + [pltpu.VMEM((slots, rows, WIDE), F32)],
            16,
            20,
            "attend_back",
        )
        d_queries.append(d_query)
        kept.append(keep)
        sent.append(send)
        if b == 0:
            got_c = flip(made_far, 1, "made_c")
            got_x = flip_x(more_send, "gmore")
            (d_queries, kept, sent, marked_grad, made, got_c, more_keep, got_x, down_send) = hold(
                d_queries, kept, sent, marked_grad, made, got_c, more_keep, got_x, down_send
            )
            made = made.astype(F32) + got_c.astype(F32)
            more_grads = scatter_x(more_keep, got_x, "gmore").reshape(TEAM + 1, ndp, share, width)
            got_y = flip(made[1].astype(BF), top, "made_y")
            more_z = halve_z(more_grads, 1, "gmore", 1)
            keys_got = flip_x(sent[0], "gkeyval0")
            got_x = flip_x(down_send, "gdown")
    (d_queries, kept, sent, made, got_y, more_z, keys_got, down_keep, got_x) = hold(
        d_queries, kept, sent, made, got_y, more_z, keys_got, down_keep, got_x
    )
    output = (inputs.astype(F32) + made[0] + got_y.astype(F32)).astype(BF)
    more_grads = add_z(more_z)
    down_grads = scatter_x(down_keep, got_x, "gdown").reshape(ndp, down_share, width)
    keys_gots = [keys_got] + [flip_x(sent[b], f"gkeyval{b}") for b in range(1, count)]

    def keys_back(b):
        keep, got = kept[b], keys_gots[b]
        mask = wide // 2
        while True:
            value = keep + got.astype(F32)
            mask //= 2
            if mask == 0:
                return value
            keep = value[: value.shape[0] // 2]
            got = flip(value[value.shape[0] // 2 :].astype(BF), 2 * mask, f"gkeyval{b}_x{mask}")

    def join_c(value, got):
        mine = pick(value.reshape((2, 2) + value.shape[1:]), own_c, 1)
        got = got.astype(F32)
        return jnp.where(own_c == 0, mine, got), jnp.where(own_c == 0, got, mine)

    def join_y(value, got):
        mine = pick(value, own_y, 0)
        got = got.astype(F32)
        return jnp.where(own_y == 0, mine, got), jnp.where(own_y == 0, got, mine)

    pulled = []
    carried = []
    front_half = (half, TEAM, ndp * share, front_wide)
    for b in range(count):
        last = b == count - 1
        outs = [struct((2, rows, width), BF), struct((2, rows, width), BF)]
        out_specs = [near(rows, width), far(rows, width)]
        sums = [struct((width, front_wide), F32), struct((8, width), F32)]
        if last:
            outs += [struct(front_half, F32), struct(front_half, BF)]
        else:
            outs += sums
        d_tokens, d_tokens_far, *carried = call(
            functools.partial(tokens_kernel, last),
            own_place,
            [
                *tokens[b],
                normed_attn[b],
                d_normed,
                d_queries[b],
                keys_back(b),
                kv_cotangent,
                front,
                norm_rows,
                cos_table,
                sin_table,
                *carried,
            ],
            one_sequence
            + [
                by_r(rows, width),
                pl.BlockSpec((1, 1, rows, width), lambda r, *_, b=b: (r, b, 0, 0)),
                by_r(rows, 2 * WIDE),
                table,
                pl.BlockSpec((1, rows, WIDE), lambda r, *_, b=b: (b, 0, 0)),
                whole(width, front_wide),
                whole(8, width),
                table,
                table,
            ]
            + [whole(*part.shape) for part in carried],
            out_specs + [whole(*out.shape) for out in outs[2:]],
            outs,
            ([pltpu.VMEM(out.shape, F32) for out in sums] if last else []) + [block],
            14,
            7,
            "pull_tokens",
        )
        pulled.append((d_tokens, d_tokens_far))
        if b == 0:
            mask = 2
            while mask < ndp:
                more_z = halve_z(more_grads, 1, "gmore", mask)
                more_grads = add_z(more_z)
                mask *= 2
            down_z = halve_z(down_grads, 0, "gdown", 1)
            (carried, pulled, more_grads, keys_gots, kept, d_queries) = hold(
                carried, pulled, more_grads, keys_gots, kept, d_queries
            )
            more_grads = jnp.squeeze(more_grads, 1)
            got_c = flip(pulled[0][1], 1, "dtokens0_c")
            ups_c = flip(
                pick(more_grads[:TEAM].reshape(2, 2, share, hidden), 1 - own_c, 1).astype(BF), 1, "gup_c"
            )
    front_keep, front_send = carried
    front_keep, front_send, pulled, got_c, ups_c, down_z, more_grads = hold(
        front_keep, front_send, pulled, got_c, ups_c, down_z, more_grads
    )
    down_grads = finish_z(add_z(down_z), 0, "gdown")

    def add_c(pair, got):
        return pair[0].astype(F32) + got.astype(F32)

    front_got = flip_x(front_send, "gfront")
    halves = [add_c(pulled[0], got_c)]
    got_y = flip(halves[0][1].astype(BF), top, "dtokens0_y")
    gots_c = [flip(pulled[b][1], 1, f"dtokens{b}_c") for b in range(1, count)]
    ups = jnp.concatenate(join_c(more_grads[:TEAM], ups_c), axis=-1)
    ups_y = flip(pick(ups, 1 - own_y, 0).astype(BF), top, "gup_y")
    front_keep, front_got, gots_c, more_grads = hold(front_keep, front_got, gots_c, more_grads)
    halves += [add_c(pulled[b], gots_c[b - 1]) for b in range(1, count)]
    with jax.named_scope("swap_gout_moved"):
        grad_out = lax.ppermute(more_grads[TEAM].astype(BF), ("seq", "dp"), moved(False)).astype(F32)
    front_grads = scatter_x(front_keep, front_got, "gfront").reshape(TEAM, ndp, share, front_wide)
    front_z = halve_z(front_grads, 1, "gfront", 1)
    gots_y = [got_y] + [
        flip(halves[b][1].astype(BF), top, f"dtokens{b}_y") for b in range(1, count)
    ]
    front_z, gots_y[0], halves, ups, ups_y = hold(front_z, gots_y[0], halves, ups, ups_y)
    front_grads = finish_z(add_z(front_z), 1, "gfront")

    piece = hidden // wide
    ups = join_y(ups, ups_y)
    grad_up = jnp.concatenate(
        [
            ups[y][:, hidden * c + piece * x : hidden * c + piece * (x + 1)]
            for y in range(2)
            for x in range(wide)
            for c in range(2)
        ],
        axis=-1,
    )
    front_grads, gots_y, grad_up, grad_out, down_grads = hold(
        front_grads, gots_y, grad_up, grad_out, down_grads
    )
    d_rows = [halves[b][0] + gots_y[b].astype(F32) for b in range(count)]
    grad_inputs = out_cotangent.astype(F32) + jnp.stack(d_rows)
    got_c = flip(pick(front_grads.reshape(2, 2, share, front_wide), 1 - own_c, 1).astype(BF), 1, "gfront_c")
    front_grads, got_c, grad_inputs = hold(front_grads, got_c, grad_inputs)

    low, high = join_c(front_grads, got_c)
    query = slice(WIDE, WIDE + heads_wide)
    ends = slice(WIDE + heads_wide, WIDE + heads_wide + 4)
    front_grads = (
        jnp.concatenate(
            [low[..., :WIDE] + high[..., :WIDE], low[..., query], high[..., query], low[..., ends] + high[..., ends]],
            axis=-1,
        )
    )
    got_y = flip(pick(front_grads, 1 - own_y, 0).astype(BF), top, "gfront_y")
    fronts = join_y(front_grads, got_y)
    both_heads = slice(WIDE, WIDE + 2 * heads_wide)
    grad_query = jnp.concatenate([part[:, both_heads] for part in fronts], axis=-1)
    grad_keyval = fronts[0][:, :WIDE] + fronts[1][:, :WIDE]
    norm_grads = (fronts[0] + fronts[1])[:, WIDE + 2 * heads_wide :]
    return (
        output,
        jnp.stack([part[0] for part in keyvals]),
        grad_inputs,
        grad_query,
        grad_keyval,
        grad_out,
        grad_up,
        down_grads,
        norm_grads[:, :2],
        norm_grads[:, 2:],
    )


def solution(mesh):
    rows = P("dp", "seq", None)
    split = P(("seq", "dp"), None)
    return jax.shard_map(
        functools.partial(on_device, mesh.shape["seq"], mesh.shape["dp"]),
        mesh=mesh,
        in_specs=(rows,) + (split,) * 7 + (rows, rows),
        out_specs=(rows,) * 3 + (split,) * 7,
        check_vma=False,
    )
```

time: 367 us -> 234 us (0.64)
  waiting for transfers between devices: 142 us -> 45.8 us
  local copies, waits for them, and re-layouts: 30.9 us -> 11.3 us
  other arithmetic: 29.8 us -> 14.1 us
  starting transfers between devices: 66.2 us -> 55.6 us
  Pallas kernels: 95.7 us -> 105 us
    ppermute x27 -> x31, waiting for transfers between devices: 99.6 us -> 17.5 us  [flip(): return lax.ppermute(value, 'seq', [(i, i ^ mask) for i in range(nseq)])]
    ppermute x12, waiting for transfers between devices: 42 us -> 28.2 us  [flip_z(): return lax.ppermute(value, 'dp', [(i, i ^ mask) for i in range(ndp)])]
    ppermute x27 -> x31, starting transfers between devices: 50.5 us -> 39.3 us  [flip(): return lax.ppermute(value, 'seq', [(i, i ^ mask) for i in range(nseq)])]
    concatenate x10 -> x4, other arithmetic: 9.89 us -> 0.76 us  [the longest x1 0.64 us: on_device(): jnp.concatenate([part[:, both_heads] for part in fronts], axis=-1)]
    pallas_call x8 -> x9, Pallas kernels: 95.7 us -> 105 us  [call(): pl.pallas_call(kernel, grid_spec=pltpu.PrefetchScalarGridSpec(num_scalar_...]
    slice x18 -> x12, local copies, waits for them, and re-layouts: 7.48 us -> 0.22 us  [the longest x1 0.07 us: on_device(): norm_grads[:, 2:]]
    unnamed x78 -> x103, local copies, waits for them, and re-layouts: 11.1 us -> 6.65 us
  transfers between devices with their start and end apart: 41 -> 45, of which waited for: 23 -> 14; matrix products, arithmetic and copies ran while one was open for 12% -> 5% of each run, Pallas kernels for 5% -> 32%
where the time goes in v2:
time: 234 us; the launch traced here: 233 us
  Pallas kernels  105 us (45%)
  starting transfers between devices  55.6 us (24%)
  waiting for transfers between devices  45.8 us (20%)
  other arithmetic  14.1 us (6%)
  local copies, waits for them, and re-layouts  11.3 us (5%)
    pallas_call x9, Pallas kernels, call(): pl.pallas_call(kernel, grid_spec=pltpu.PrefetchScalarGridSpec(num_scalar_...  105 us
    ppermute x31, starting transfers between devices, flip(): return lax.ppermute(value, 'seq', [(i, i ^ mask) for i in range(nseq)])  39.3 us
    ppermute x12, waiting for transfers between devices, flip_z(): return lax.ppermute(value, 'dp', [(i, i ^ mask) for i in range(ndp)])  28.2 us
    ppermute x31, waiting for transfers between devices, flip(): return lax.ppermute(value, 'seq', [(i, i ^ mask) for i in range(nseq)])  17.5 us
    ppermute x12, starting transfers between devices, flip_z(): return lax.ppermute(value, 'dp', [(i, i ^ mask) for i in range(ndp)])  14.9 us
    unnamed x103, local copies, waits for them, and re-layouts  6.65 us
  transfers between devices with their start and end apart: 45, of which 14 were waited for; matrix products, arithmetic and copies ran while one was open for 5% of the time, Pallas kernels for 32%

profile of v2, /device:TPU:0, one launch (start us, length us, event | category | flops | bytes accessed | tf_op | source)
XLA Modules:
  0.0 233.2 jit_solution(3134959013733534046)
XLA Ops:
  0.7 0.9 reshape.457
  1.6 0.7 pad_maximum_fusion.7
  2.4 1.0 reshape.458
  3.7 0.7 broadcast_in_dim.37
  4.5 3.0 %collective-permute-start = (bf16[2,24,1152]{2,1,0:T(8,128)(2,1)S(1)}, bf16[2,24,1152]{2,1,0:T(8,128)(2,1)S(1)}, u32[]{:S(2)}, u32[]{:S(2)}) collective-permute-start(bf16[2,24,1152]{2,1,0:T(8,128)(2,1)S(1)} %get-tuple-element.340), channel_id=1, source_target_pairs={{0,16},{4,20},{8,24},{12,28},{16,0},{20,4},{24,8},{28,12},{1,17},{... | collective-permute-start | bytes 331784 | tf_op jit(solution)/shard_map/swap_pack_y/ppermute | solution.py:442
  8.3 2.4 %collective-permute-done = bf16[2,24,1152]{2,1,0:T(8,128)(2,1)S(1)} collective-permute-done((bf16[2,24,1152]{2,1,0:T(8,128)(2,1)S(1)}, bf16[2,24,1152]{2,1,0:T(8,128)(2,1)S(1)}, u32[]{:S(2)}, u32[]{:S(2)}) %collective-permute-start) | collective-permute-done | bytes 110624 | tf_op jit(solution)/shard_map/swap_pack_y/ppermute | solution.py:442
  12.3 2.7 %collective-permute-start.3 = (bf16[4,1,24,384]{3,2,0,1:T(8,128)(2,1)S(1)}, bf16[4,1,24,384]{3,2,0,1:T(8,128)(2,1)S(1)}, u32[]{:S(2)}, u32[]{:S(2)}) collective-permute-start(bf16[4,1,24,384]{3,2,0,1:T(8,128)(2,1)S(1)} %bitcast.130), channel_id=1, source_target_pairs={{0,2},{1,3},{2,0},{3,1},{4,6},{5,7},{6,4},{7,5},{8,10},{9,11},{10,... | collective-permute-start | bytes 221192 | tf_op jit(solution)/shard_map/swap_front_z2/ppermute | solution.py:446
  15.1 1.5 collective-permute-start.5
  16.6 2.9 %collective-permute-done.3 = bf16[4,1,24,384]{3,2,0,1:T(8,128)(2,1)S(1)} collective-permute-done((bf16[4,1,24,384]{3,2,0,1:T(8,128)(2,1)S(1)}, bf16[4,1,24,384]{3,2,0,1:T(8,128)(2,1)S(1)}, u32[]{:S(2)}, u32[]{:S(2)}) %collective-permute-start.3) | collective-permute-done | bytes 73760 | tf_op jit(solution)/shard_map/swap_front_z2/ppermute | solution.py:446
  19.6 0.8 collective-permute-start.4
  20.4 4.7 %collective-permute-done.4 = bf16[4,2,24,384]{3,2,0,1:T(8,128)(2,1)S(1)} collective-permute-done((bf16[4,2,24,384]{3,2,0,1:T(8,128)(2,1)S(1)}, bf16[4,2,24,384]{3,2,0,1:T(8,128)(2,1)S(1)}, u32[]{:S(2)}, u32[]{:S(2)}) %collective-permute-start.4) | collective-permute-done | bytes 147488 | tf_op jit(solution)/shard_map/swap_front_z1/ppermute | solution.py:446
  25.1 0.7 copy.57
  26.3 1.3 collective-permute-start.6
  27.6 1.7 collective-permute-start.9
  29.3 3.1 %negate_select_fusion = (f32[4,256,128]{2,1,0:T(8,128)}, f32[4,256,128]{2,1,0:T(8,128)}) fusion(f32[128]{0:T(128)S(1)} %fusion.21, f32[4,256]{1,0:T(4,128)S(1)} %convert_multiply_fusion, pred[128]{0:T(512)(128)(4,1)S(1)} %get-tuple-element.347, pred[128]{0:T(512)(128)(4,1)S(1)} %get-tuple-element.348), kind=kLoop, calls=%fused_computation.17 | loop fusion | flops 655360 | bytes 1053440 | tf_op jit(solution)/shard_map/jit(_where)/select_n | solution.py:597
  32.4 2.2 collective-permute-start.10
  34.6 3.0 %collective-permute-done.9 = bf16[1,96,768]{2,1,0:T(8,128)(2,1)S(1)} collective-permute-done((bf16[1,96,768]{2,1,0:T(8,128)(2,1)S(1)}, bf16[1,96,768]{2,1,0:T(8,128)(2,1)S(1)}, u32[]{:S(2)}, u32[]{:S(2)}) %collective-permute-start.9) | collective-permute-done | bytes 147488 | tf_op jit(solution)/shard_map/swap_down_z2/ppermute | solution.py:446
  37.6 0.7 copy-done.39
  38.4 0.7 copy-done.14
  39.1 6.6 %prepare.2 = (bf16[4,256,768]{2,1,0:T(8,128)(2,1)}, bf16[4,256,768]{2,1,0:T(8,128)(2,1)}, bf16[4,256,256]{2,1,0:T(8,128)(2,1)}, bf16[4,256,128]{2,1,0:T(8,128)(2...) custom-call(s32[1]{0:T(128)} %bitcast.1.own_ref, bf16[1,256,768]{2,1,0:T(8,128)(2,1)} %copy-done.4, ...), custom_call_target="tpu_custom_call" | custom-call | flops 4400000000 | tf_op jit(solution)/shard_map/prepare/pallas_call | solution.py:613
  46.3 0.8 collective-permute-start.11
  47.1 1.0 maximum_select_fusion.4
  48.1 1.0 maximum_select_fusion.5
  49.2 3.8 %collective-permute-start.15 = (bf16[2,96,768]{2,1,0:T(8,128)(2,1)S(1)}, bf16[2,96,768]{2,1,0:T(8,128)(2,1)S(1)}, u32[]{:S(2)}, u32[]{:S(2)}) collective-permute-start(bf16[2,96,768]{2,1,0:T(8,128)(2,1)S(1)} %maximum_select_fusion.4), channel_id=1, source_target_pairs={{0,1},{1,0},{2,3},{3,2},{4,5},{5,4},{6,7},{7,6},{8,9},{9,8},{10,11... | collective-permute-start | bytes 884744 | tf_op jit(solution)/shard_map/swap_down_z1/ppermute | solution.py:446
  53.0 1.2 collective-permute-start.18
  54.2 6.2 %prepare.3 = (bf16[4,256,768]{2,1,0:T(8,128)(2,1)}, bf16[4,256,768]{2,1,0:T(8,128)(2,1)}, bf16[4,256,256]{2,1,0:T(8,128)(2,1)}, bf16[4,256,128]{2,1,0:T(8,128)(2,1)}) custom-call(s32[1]{0:T(128)} %bitcast.1.own_ref, bf16[1,256,768]{2,1,0:T(8,128)(2,1)} %copy-done.2, bf16[1,256,768]{2,1,0:T(8,128)(2,1)} %copy-done.16, bf16[1,256,768]{2,1,0:T(8,128)(2,1)} %copy-done.8, ...), custom_call_target="tpu_custom_call" | custom-call | flops 4400000000 | tf_op jit(solution)/shard_map/prepare/pallas_call | solution.py:613
  60.4 1.6 collective-permute-start.16
  62.0 1.0 collective-permute-done.15
  63.2 1.1 collective-permute-start.22
  64.3 10.7 %attend.2 = (bf16[4,256,256]{2,1,0:T(8,128)(2,1)S(1)}, bf16[4,3,256,128]{3,2,1,0:T(8,128)(2,1)S(1)}) custom-call(s32[1]{0:T(128)} %bitcast.own_ref, bf16[4,256,256]{2,1,0:T(8,128)(2,1)S(1)} %copy-done.26, bf16[4,256,128]{2,1,0:T(8,128)(2,1)S(1)} %copy-done.6, bf16[4,256,128]{2,1,0:T(8,128)(2,1)S(1)} %collective-permute-done.11.refs_1_), custom_call_target="tpu_custom_call" | custom-call | flops 16499999744 | tf_op jit(solution)/shard_map/attend/pallas_call | solution.py:613
  75.1 0.7 pad_maximum_fusion.4
  76.0 5.6 %collective-permute-start.21 = (bf16[1,5,96,768]{3,2,1,0:T(8,128)(2,1)S(1)}, bf16[1,5,96,768]{3,2,1,0:T(8,128)(2,1)S(1)}, u32[]{:S(2)}, u32[]{:S(2)}) collective-permute-start(bf16[1,5,96,768]{3,2,1,0:T(8,128)(2,1)S(1)} %bitcast.126), channel_id=1, source_target_pairs={{0,8},{4,12},{8,0},{12,4},{16,24},{20,28},{24,16},{28,20},{1,9},{5... | collective-permute-start | bytes 2211848 | tf_op jit(solution)/shard_map/swap_more_x1/ppermute | solution.py:442
  81.7 10.7 %attend.3 = (bf16[4,256,256]{2,1,0:T(8,128)(2,1)S(1)}, bf16[4,3,256,128]{3,2,1,0:T(8,128)(2,1)S(1)}) custom-call(s32[1]{0:T(128)} %bitcast.own_ref, bf16[4,256,256]{2,1,0:T(8,128)(2,1)S(1)} %copy-done.25, bf16[4,256,128]{2,1,0:T(8,128)(2,1)S(1)} %copy-done.7, bf16[4,256,128]{2,1,0:T(8,128)(2,1)S(1)} %collective-permute-done.16.refs_1_), custom_call_target="tpu_custom_call" | custom-call | flops 16499999744 | tf_op jit(solution)/shard_map/attend/pallas_call | solution.py:613
  92.4 6.4 %collective-permute-done.21.refs_9_ = bf16[1,5,96,768]{3,2,1,0:T(8,128)(2,1)S(1)} collective-permute-done((bf16[1,5,96,768]{3,2,1,0:T(8,128)(2,1)S(1)}, bf16[1,5,96,768]{3,2,1,0:T(8,128)(2,1)S(1)}, u32[]{:S(2)}, u32[]{:S(2)}) %collective-permute-start.21) | collective-permute-done | bytes 737312 | tf_op jit(solution)/shard_map/swap_more_x1/ppermute | solution.py:442
  98.8 0.9 copy-done.43
  100.0 30.0 %hidden.1 = (bf16[2,2,256,768]{3,2,1,0:T(8,128)(2,1)}, bf16[2,2,256,768]{3,2,1,0:T(8,128)(2,1)}, bf16[4,2,256,768]{3,2,1,0:T(8,128)(2,1)}, bf16[4,2,3,256,128]{4...) custom-call(s32[1]{0:T(128)} %bitcast.1.own_ref, ...), custom_call_target="tpu_custom_call" | custom-call | flops 29699999744 | tf_op jit(solution)/shard_map/hidden/pallas_call | solution.py:613
  130.1 1.8 collective-permute-start.24
  131.9 1.4 copy-done.27
  133.3 13.9 %attend_back.2 = (bf16[4,256,256]{2,1,0:T(8,128)(2,1)S(1)}, f32[4,256,128]{2,1,0:T(8,128)S(1)}, bf16[4,256,128]{2,1,0:T(8,128)(2,1)S(1)}) custom-call(s32[1]{0:T(128)} %bitcast.own_ref, bf16[4,3,256,128]{3,2,1,0:T(8,128)(2,1)S(1)} %get-tuple-element.187.query_ref, bf16[4,2,3,256,128]{4,3,2,1,0:T(8,128)(2,1)S(1)} %copy-done.27, f32[4,256,128]{2,1,0:T(8,128)S(1)} %copy-done.1, ...), custom_call_target="tpu_custom_call" | custom-call | flops 22000001024 | tf_op jit(solution)/shard_map/attend_back/pallas_call | solution.py:613
  147.2 2.0 collective-permute-done.24
  149.7 1.3 collective-permute-start.25
  151.2 2.1 collective-permute-start.26
  153.3 5.2 %collective-permute-start.27 = (bf16[4,256,128]{2,1,0:T(8,128)(2,1)S(1)}, bf16[4,256,128]{2,1,0:T(8,128)(2,1)S(1)}, u32[]{:S(2)}, u32[]{:S(2)}) collective-permute-start(bf16[4,256,128]{2,1,0:T(8,128)(2,1)S(1)} %get-tuple-element.227), channel_id=1, source_target_pairs={{0,8},{4,12},{8,0},{12,4},{16,24},{20,28},{24,16},{28,20},{1,9},{5... | collective-permute-start | bytes 786440 | tf_op jit(solution)/shard_map/swap_gkeyval0_x1/ppermute | solution.py:442
  158.5 14.1 %attend_back.3 = (bf16[4,256,256]{2,1,0:T(8,128)(2,1)S(1)}, f32[4,256,128]{2,1,0:T(8,128)S(1)}, bf16[4,256,128]{2,1,0:T(8,128)(2,1)S(1)}) custom-call(s32[1]{0:T(128)} %bitcast.own_ref, bf16[4,3,256,128]{3,2,1,0:T(8,128)(2,1)S(1)} %get-tuple-element.222.query_ref, bf16[4,2,3,256,128]{4,3,2,1,0:T(8,128)(2,1)S(1)} %copy-done.28, f32[4,256,128]{2,1,0:T(8,128)S(1)} %copy-done.1, ...), custom_call_target="tpu_custom_call" | custom-call | flops 22000001024 | tf_op jit(solution)/shard_map/attend_back/pallas_call | solution.py:613
  172.7 4.4 %collective-permute-done.28 = bf16[1,1,384,768]{3,2,1,0:T(8,128)(2,1)S(1)} collective-permute-done((bf16[1,1,384,768]{3,2,1,0:T(8,128)(2,1)S(1)}, bf16[1,1,384,768]{3,2,1,0:T(8,128)(2,1)S(1)}, u32[]{:S(2)}, u32[]{:S(2)}) %collective-permute-start.28) | collective-permute-done | bytes 589856 | tf_op jit(solution)/shard_map/swap_gdown_x1/ppermute | solution.py:442
  177.6 0.9 collective-permute-start.29
  178.6 4.1 %collective-permute-start.30 = (bf16[4,256,128]{2,1,0:T(8,128)(2,1)S(1)}, bf16[4,256,128]{2,1,0:T(8,128)(2,1)S(1)}, u32[]{:S(2)}, u32[]{:S(2)}) collective-permute-start(bf16[4,256,128]{2,1,0:T(8,128)(2,1)S(1)} %get-tuple-element.251), channel_id=1, source_target_pairs={{0,8},{4,12},{8,0},{12,4},{16,24},{20,28},{24,16},{28,20},{1,9},{5... | collective-permute-start | bytes 786440 | tf_op jit(solution)/shard_map/swap_gkeyval1_x1/ppermute | solution.py:442
  182.7 1.9 collective-permute-start.33
  184.8 6.0 %pull_tokens.2 = (bf16[2,256,768]{2,1,0:T(8,128)(2,1)S(1)}, bf16[2,256,768]{2,1,0:T(8,128)(2,1)S(1)}, f32[768,384]{1,0:T(8,128)S(1)}, f32[8,768]{1,0:T(8,128)S(1)}) custom-call(s32[1]{0:T(128)} %bitcast.1.own_ref, bf16[1,256,768]{2,1,0:T(8,128)(2,1)S(1)} %copy-done.5, bf16[1,256,768]{2,1,0:T(8,128)(2,1)S(1)} %copy-done.13, ...), custom_call_target="tpu_custom_call" | custom-call | flops 7699999744 | tf_op jit(solution)/shard_map/pull_tokens/pallas_call | solution.py:613
  192.2 6.3 %pull_tokens.3 = (bf16[2,256,768]{2,1,0:T(8,128)(2,1)S(1)}, bf16[2,256,768]{2,1,0:T(8,128)(2,1)S(1)}, f32[1,4,96,384]{3,2,1,0:T(8,128)S(1)}, bf16[1,4,96,384]{3,2,1,0:T(8,128)(2,1)S(1)}) custom-call(s32[1]{0:T(128)} %bitcast.1.own_ref, bf16[1,256,768]{2,1,0:T(8,128)(2,1)S(1)} %copy-done.3, bf16[1,256,768]{2,1,0:T(8,128)(2,1)S(1)} %copy-done.17, ...), custom_call_target="tpu_custom_call" | custom-call | flops 7699999744 | tf_op jit(solution)/shard_map/pull_tokens/pallas_call | solution.py:613
  198.5 1.3 collective-permute-start.34
  200.3 1.3 collective-permute-start.37
  201.6 0.8 collective-permute-start.38
  202.4 7.2 %collective-permute-done.42 = bf16[1,96,768]{2,1,0:T(8,128)(2,1)S(1)} collective-permute-done((bf16[1,96,768]{2,1,0:T(8,128)(2,1)S(1)}, bf16[1,96,768]{2,1,0:T(8,128)(2,1)S(1)}, u32[]{:S(2)}, u32[]{:S(2)}) %collective-permute-start.42) | collective-permute-done | bytes 147488 | tf_op jit(solution)/shard_map/swap_gdown_z2/ppermute | solution.py:446
  209.6 0.7 add_bitcast_fusion
  211.5 1.3 collective-permute-start.40
  213.5 2.9 %collective-permute-done.36 = bf16[4,2,24,384]{3,2,0,1:T(8,128)(2,1)S(1)} collective-permute-done((bf16[4,2,24,384]{3,2,0,1:T(8,128)(2,1)S(1)}, bf16[4,2,24,384]{3,2,0,1:T(8,128)(2,1)S(1)}, u32[]{:S(2)}, u32[]{:S(2)}) %collective-permute-start.36) | collective-permute-done | bytes 147488 | tf_op jit(solution)/shard_map/swap_gfront_z1/ppermute | solution.py:446
  216.4 0.7 collective-permute-start.39
  217.3 6.5 %collective-permute-done.39 = bf16[4,1,24,384]{3,2,0,1:T(8,128)(2,1)S(1)} collective-permute-done((bf16[4,1,24,384]{3,2,0,1:T(8,128)(2,1)S(1)}, bf16[4,1,24,384]{3,2,0,1:T(8,128)(2,1)S(1)}, u32[]{:S(2)}, u32[]{:S(2)}) %collective-permute-start.39) | collective-permute-done | bytes 73760 | tf_op jit(solution)/shard_map/swap_gfront_z2/ppermute | solution.py:446
  224.3 0.8 copy-done.34
  225.0 1.3 maximum_add_fusion
  226.6 1.3 collective-permute-start.44
  227.9 1.2 fusion.1
  229.1 1.5 collective-permute-done.44
  (231 shorter events, 12.9 us)
Async XLA Ops:
  0.7 10.6 %copy-start.30 = (bf16[2,256,768]{2,1,0:T(8,128)(2,1)S(1)}, bf16[2,256,768]{2,1,0:T(8,128)(2,1)}, u32[]{:S(2)}) copy-start(bf16[2,256,768]{2,1,0:T(8,128)(2,1)} %param.10) | copy-start | bytes 2359300
  4.5 6.1 %collective-permute-start = (bf16[2,24,1152]{2,1,0:T(8,128)(2,1)S(1)}, bf16[2,24,1152]{2,1,0:T(8,128)(2,1)S(1)}, u32[]{:S(2)}, u32[]{:S(2)}) collective-permute-start(bf16[2,24,1152]{2,1,0:T(8,128)(2,1)S(1)} %get-tuple-element.340), channel_id=1, source_target_pairs={{0,16},{4,20},{8,24},{12,28},{16,0},{20,4},{24,8},{28,12},{1,17},{... | collective-permute-start | bytes 331784 | tf_op jit(solution)/shard_map/swap_pack_y/ppermute | solution.py:442
  7.6 4.3 %collective-permute-start.2 = (bf16[24,768]{1,0:T(8,128)(2,1)S(1)}, bf16[24,768]{1,0:T(8,128)(2,1)S(1)}, u32[]{:S(2)}, u32[]{:S(2)}) collective-permute-start(bf16[24,768]{1,0:T(8,128)(2,1)S(1)} %copy-done.46), channel_id=1, source_target_pairs={{0,0},{1,1},{2,2},{3,3},{8,4},{9,5},{10,6},{11,7},{4,8},{5,9},{6,1... | collective-permute-start | bytes 110600 | tf_op jit(solution)/shard_map/swap_out_moved/ppermute | solution.py:566
  10.7 1.5 collective-permute-start.1
  11.3 21.1 %copy-start.4 = (bf16[1,256,768]{2,1,0:T(8,128)(2,1)}, bf16[1,256,768]{2,1,0:T(8,128)(2,1)S(1)}, u32[]{:S(2)}) copy-start(bf16[1,256,768]{2,1,0:T(8,128)(2,1)S(1)} %get-tuple-element.161.refs_0_.x0_ref) | copy-start | bytes 1179652
  11.3 21.0 %copy-start.2 = (bf16[1,256,768]{2,1,0:T(8,128)(2,1)}, bf16[1,256,768]{2,1,0:T(8,128)(2,1)S(1)}, u32[]{:S(2)}) copy-start(bf16[1,256,768]{2,1,0:T(8,128)(2,1)S(1)} %get-tuple-element.172.refs_0_.x0_ref) | copy-start | bytes 1179652
  11.3 16.3 %copy-start.38 = (bf16[96,768]{1,0:T(8,128)(2,1)S(1)}, bf16[96,768]{1,0:T(8,128)(2,1)}, u32[]{:S(2)}) copy-start(bf16[96,768]{1,0:T(8,128)(2,1)} %param.15) | copy-start | bytes 442372
  11.3 21.0 %collective-permute-start.7 = (bf16[1,256,768]{2,1,0:T(8,128)(2,1)S(1)}, bf16[1,256,768]{2,1,0:T(8,128)(2,1)S(1)}, u32[]{:S(2)}, u32[]{:S(2)}) collective-permute-start(bf16[1,256,768]{2,1,0:T(8,128)(2,1)S(1)} %get-tuple-element.161.refs_0_.x0_ref), channel_id=1, source_target_pairs={{0,4},{4,0},{8,12},{12,8},{16,20},{20,16},{24,28},{28,24},{1,5},{5... | collective-permute-start | bytes 1179656 | tf_op jit(solution)/shard_map/swap_tokens0_c/ppermute | solution.py:442
  11.4 37.7 %collective-permute-start.12 = (bf16[1,256,768]{2,1,0:T(8,128)(2,1)S(1)}, bf16[1,256,768]{2,1,0:T(8,128)(2,1)S(1)}, u32[]{:S(2)}, u32[]{:S(2)}) collective-permute-start(bf16[1,256,768]{2,1,0:T(8,128)(2,1)S(1)} %get-tuple-element.172.refs_0_.x0_ref), channel_id=1, source_target_pairs={{0,4},{4,0},{8,12},{12,8},{16,20},{20,16},{24,28},{28,24},{1,5},{5... | collective-permute-start | bytes 1179656 | tf_op jit(solution)/shard_map/swap_tokens1_c/ppermute | solution.py:442
  12.3 7.2 %collective-permute-start.3 = (bf16[4,1,24,384]{3,2,0,1:T(8,128)(2,1)S(1)}, bf16[4,1,24,384]{3,2,0,1:T(8,128)(2,1)S(1)}, u32[]{:S(2)}, u32[]{:S(2)}) collective-permute-start(bf16[4,1,24,384]{3,2,0,1:T(8,128)(2,1)S(1)} %bitcast.130), channel_id=1, source_target_pairs={{0,2},{1,3},{2,0},{3,1},{4,6},{5,7},{6,4},{7,5},{8,10},{9,11},{10,... | collective-permute-start | bytes 221192 | tf_op jit(solution)/shard_map/swap_front_z2/ppermute | solution.py:446
  15.1 11.2 %collective-permute-start.5 = (bf16[1,256,768]{2,1,0:T(8,128)(2,1)S(1)}, bf16[1,256,768]{2,1,0:T(8,128)(2,1)S(1)}, u32[]{:S(2)}, u32[]{:S(2)}) collective-permute-start(bf16[1,256,768]{2,1,0:T(8,128)(2,1)S(1)} %get-tuple-element.161.refs_0_.x0_ref), channel_id=1, source_target_pairs={{0,16},{4,20},{8,24},{12,28},{16,0},{20,4},{24,8},{28,12},{1,17},{... | collective-permute-start | bytes 1179656 | tf_op jit(solution)/shard_map/swap_tokens0_y/ppermute | solution.py:442
  19.6 5.5 %collective-permute-start.4 = (bf16[4,2,24,384]{3,2,0,1:T(8,128)(2,1)S(1)}, bf16[4,2,24,384]{3,2,0,1:T(8,128)(2,1)S(1)}, u32[]{:S(2)}, u32[]{:S(2)}) collective-permute-start(bf16[4,2,24,384]{3,2,0,1:T(8,128)(2,1)S(1)} %maximum_select_fusion.9), channel_id=1, source_target_pairs={{0,1},{1,0},{2,3},{3,2},{4,5},{5,4},{6,7},{7,6},{8,9},{9,8},{10,11... | collective-permute-start | bytes 442376 | tf_op jit(solution)/shard_map/swap_front_z1/ppermute | solution.py:446
  26.3 12.1 %copy-start.12 = (bf16[1,256,768]{2,1,0:T(8,128)(2,1)}, bf16[1,256,768]{2,1,0:T(8,128)(2,1)S(1)}, u32[]{:S(2)}) copy-start(bf16[1,256,768]{2,1,0:T(8,128)(2,1)S(1)} %collective-permute-done.5.refs_1_.x1_ref) | copy-start | bytes 1179652
  26.3 12.0 %collective-permute-start.8 = (bf16[1,256,768]{2,1,0:T(8,128)(2,1)S(1)}, bf16[1,256,768]{2,1,0:T(8,128)(2,1)S(1)}, u32[]{:S(2)}, u32[]{:S(2)}) collective-permute-start(bf16[1,256,768]{2,1,0:T(8,128)(2,1)S(1)} %collective-permute-done.5.refs_1_.x1_ref), channel_id=1, source_target_pairs={{0,4},{4,0},{8,12},{12,8},{16,20},{20,16},{24,28},{28,24},{1,5},{5... | collective-permute-start | bytes 1179656 | tf_op jit(solution)/shard_map/swap_tokens0_yc/ppermute | solution.py:442
  26.3 11.3 %collective-permute-start.6 = (bf16[1,4,96,384]{3,2,1,0:T(8,128)(2,1)}, bf16[1,4,96,384]{3,2,1,0:T(8,128)(2,1)}, u32[]{:S(2)}, u32[]{:S(2)}) collective-permute-start(bf16[1,4,96,384]{3,2,1,0:T(8,128)(2,1)} %bitcast.16.refs_4_), channel_id=1, source_target_pairs={{0,8},{4,12},{8,0},{12,4},{16,24},{20,28},{24,16},{28,20},{1,9},{5... | collective-permute-start | bytes 884744 | tf_op jit(solution)/shard_map/swap_front_x1/ppermute | solution.py:442
  27.6 10.0 %collective-permute-start.9 = (bf16[1,96,768]{2,1,0:T(8,128)(2,1)S(1)}, bf16[1,96,768]{2,1,0:T(8,128)(2,1)S(1)}, u32[]{:S(2)}, u32[]{:S(2)}) collective-permute-start(bf16[1,96,768]{2,1,0:T(8,128)(2,1)S(1)} %bitcast.137), channel_id=1, source_target_pairs={{0,2},{1,3},{2,0},{3,1},{4,6},{5,7},{6,4},{7,5},{8,10},{9,11},{10,... | collective-permute-start | bytes 442376 | tf_op jit(solution)/shard_map/swap_down_z2/ppermute | solution.py:446
  32.4 13.3 %collective-permute-start.10 = (bf16[1,256,768]{2,1,0:T(8,128)(2,1)S(1)}, bf16[1,256,768]{2,1,0:T(8,128)(2,1)S(1)}, u32[]{:S(2)}, u32[]{:S(2)}) collective-permute-start(bf16[1,256,768]{2,1,0:T(8,128)(2,1)S(1)} %get-tuple-element.172.refs_0_.x0_ref), channel_id=1, source_target_pairs={{0,16},{4,20},{8,24},{12,28},{16,0},{20,4},{24,8},{28,12},{1,17},{... | collective-permute-start | bytes 1179656 | tf_op jit(solution)/shard_map/swap_tokens1_y/ppermute | solution.py:442
  45.7 8.5 %copy-start.16 = (bf16[1,256,768]{2,1,0:T(8,128)(2,1)}, bf16[1,256,768]{2,1,0:T(8,128)(2,1)S(1)}, u32[]{:S(2)}) copy-start(bf16[1,256,768]{2,1,0:T(8,128)(2,1)S(1)} %collective-permute-done.10.refs_1_.x1_ref) | copy-start | bytes 1179652
  45.7 7.3 %collective-permute-start.13 = (bf16[1,256,768]{2,1,0:T(8,128)(2,1)S(1)}, bf16[1,256,768]{2,1,0:T(8,128)(2,1)S(1)}, u32[]{:S(2)}, u32[]{:S(2)}) collective-permute-start(bf16[1,256,768]{2,1,0:T(8,128)(2,1)S(1)} %collective-permute-done.10.refs_1_.x1_ref), channel_id=1, source_target_pairs={{0,4},{4,0},{8,12},{12,8},{16,20},{20,16},{24,28},{28,24},{1,5},{5... | collective-permute-start | bytes 1179656 | tf_op jit(solution)/shard_map/swap_tokens1_yc/ppermute | solution.py:442
  45.8 46.6 %collective-permute-start.19 = (bf16[2,256,768]{2,1,0:T(8,128)(2,1)S(1)}, bf16[2,256,768]{2,1,0:T(8,128)(2,1)}, u32[]{:S(2)}, u32[]{:S(2)}) collective-permute-start(bf16[2,256,768]{2,1,0:T(8,128)(2,1)S(1)} %copy-done.33), channel_id=1, source_target_pairs={{0,4},{4,0},{8,12},{12,8},{16,20},{20,16},{24,28},{28,24},{1,5},{5... | collective-permute-start | bytes 2359304 | tf_op jit(solution)/shard_map/swap_grads_c/ppermute | solution.py:442
  46.3 15.7 %collective-permute-start.11 = (bf16[4,256,128]{2,1,0:T(8,128)(2,1)}, bf16[4,256,128]{2,1,0:T(8,128)(2,1)S(1)}, u32[]{:S(2)}, u32[]{:S(2)}) collective-permute-start(bf16[4,256,128]{2,1,0:T(8,128)(2,1)} %get-tuple-element.237.refs_0_), channel_id=1, source_target_pairs={{0,8},{4,12},{8,0},{12,4},{16,24},{20,28},{24,16},{28,20},{1,9},{5... | collective-permute-start | bytes 786440 | tf_op jit(solution)/shard_map/swap_keyval0_x1/ppermute | solution.py:442
  47.1 13.3 %collective-permute-start.14 = (bf16[5,1,24,768]{3,2,1,0:T(8,128)(2,1)S(1)}, bf16[5,1,24,768]{3,2,1,0:T(8,128)(2,1)S(1)}, u32[]{:S(2)}, u32[]{:S(2)}) collective-permute-start(bf16[5,1,24,768]{3,2,1,0:T(8,128)(2,1)S(1)} %bitcast.123), channel_id=1, source_target_pairs={{0,2},{1,3},{2,0},{3,1},{4,6},{5,7},{6,4},{7,5},{8,10},{9,11},{10,... | collective-permute-start | bytes 552968 | tf_op jit(solution)/shard_map/swap_more_z2/ppermute | solution.py:446
  49.2 13.8 %collective-permute-start.15 = (bf16[2,96,768]{2,1,0:T(8,128)(2,1)S(1)}, bf16[2,96,768]{2,1,0:T(8,128)(2,1)S(1)}, u32[]{:S(2)}, u32[]{:S(2)}) collective-permute-start(bf16[2,96,768]{2,1,0:T(8,128)(2,1)S(1)} %maximum_select_fusion.4), channel_id=1, source_target_pairs={{0,1},{1,0},{2,3},{3,2},{4,5},{5,4},{6,7},{7,6},{8,9},{9,8},{10,11... | collective-permute-start | bytes 884744 | tf_op jit(solution)/shard_map/swap_down_z1/ppermute | solution.py:446
  53.0 22.9 %collective-permute-start.18 = (bf16[2,256,768]{2,1,0:T(8,128)(2,1)S(1)}, bf16[2,256,768]{2,1,0:T(8,128)(2,1)S(1)}, u32[]{:S(2)}, u32[]{:S(2)}) collective-permute-start(bf16[2,256,768]{2,1,0:T(8,128)(2,1)S(1)} %copy-done.33), channel_id=1, source_target_pairs={{0,16},{4,20},{8,24},{12,28},{16,0},{20,4},{24,8},{28,12},{1,17},{... | collective-permute-start | bytes 2359304 | tf_op jit(solution)/shard_map/swap_grads_y/ppermute | solution.py:442
  60.4 15.4 %collective-permute-start.16 = (bf16[4,256,128]{2,1,0:T(8,128)(2,1)}, bf16[4,256,128]{2,1,0:T(8,128)(2,1)S(1)}, u32[]{:S(2)}, u32[]{:S(2)}) collective-permute-start(bf16[4,256,128]{2,1,0:T(8,128)(2,1)} %get-tuple-element.238.refs_0_), channel_id=1, source_target_pairs={{0,8},{4,12},{8,0},{12,4},{16,24},{20,28},{24,16},{28,20},{1,9},{5... | collective-permute-start | bytes 786440 | tf_op jit(solution)/shard_map/swap_keyval1_x1/ppermute | solution.py:442
  63.0 12.8 %collective-permute-start.17 = (bf16[5,2,24,768]{3,2,1,0:T(8,128)(2,1)S(1)}, bf16[5,2,24,768]{3,2,1,0:T(8,128)(2,1)S(1)}, u32[]{:S(2)}, u32[]{:S(2)}) collective-permute-start(bf16[5,2,24,768]{3,2,1,0:T(8,128)(2,1)S(1)} %maximum_select_fusion.2), channel_id=1, source_target_pairs={{0,1},{1,0},{2,3},{3,2},{4,5},{5,4},{6,7},{7,6},{8,9},{9,8},{10,11... | collective-permute-start | bytes 1105928 | tf_op jit(solution)/shard_map/swap_more_z1/ppermute | solution.py:446
  63.2 11.8 %copy-start.37 = (bf16[2,2,96,768]{3,2,1,0:T(8,128)(2,1)}, bf16[2,2,96,768]{3,2,1,0:T(8,128)(2,1)S(1)}, u32[]{:S(2)}) copy-start(bf16[2,2,96,768]{3,2,1,0:T(8,128)(2,1)S(1)} %maximum_select_fusion.1) | copy-start | bytes 1769476
  63.2 11.9 %copy-start.7 = (bf16[4,256,128]{2,1,0:T(8,128)(2,1)S(1)}, bf16[4,256,128]{2,1,0:T(8,128)(2,1)}, u32[]{:S(2)}) copy-start(bf16[4,256,128]{2,1,0:T(8,128)(2,1)} %get-tuple-element.238.refs_0_) | copy-start | bytes 786436
  63.2 29.2 %collective-permute-start.22 = (bf16[1,1,384,768]{3,2,1,0:T(8,128)(2,1)S(1)}, bf16[1,1,384,768]{3,2,1,0:T(8,128)(2,1)S(1)}, u32[]{:S(2)}, u32[]{:S(2)}) collective-permute-start(bf16[1,1,384,768]{3,2,1,0:T(8,128)(2,1)S(1)} %bitcast.133), channel_id=1, source_target_pairs={{0,8},{4,12},{8,0},{12,4},{16,24},{20,28},{24,16},{28,20},{1,9},{5... | collective-permute-start | bytes 1769480 | tf_op jit(solution)/shard_map/swap_down_x1/ppermute | solution.py:442
  75.9 16.5 %copy-start.41 = (bf16[2,256,768]{2,1,0:T(8,128)(2,1)}, bf16[2,256,768]{2,1,0:T(8,128)(2,1)S(1)}, u32[]{:S(2)}) copy-start(bf16[2,256,768]{2,1,0:T(8,128)(2,1)S(1)} %collective-permute-done.18.refs_1_) | copy-start | bytes 2359300
  75.9 23.0 %collective-permute-start.20 = (bf16[2,256,768]{2,1,0:T(8,128)(2,1)S(1)}, bf16[2,256,768]{2,1,0:T(8,128)(2,1)S(1)}, u32[]{:S(2)}, u32[]{:S(2)}) collective-permute-start(bf16[2,256,768]{2,1,0:T(8,128)(2,1)S(1)} %collective-permute-done.18.refs_1_), channel_id=1, source_target_pairs={{0,4},{4,0},{8,12},{12,8},{16,20},{20,16},{24,28},{28,24},{1,5},{5... | collective-permute-start | bytes 2359304 | tf_op jit(solution)/shard_map/swap_grads_yc/ppermute | solution.py:442
  76.0 16.4 %copy-start.36 = (bf16[5,2,2,24,768]{4,3,2,1,0:T(8,128)(2,1)}, bf16[5,2,2,24,768]{4,3,2,1,0:T(8,128)(2,1)S(1)}, u32[]{:S(2)}) copy-start(bf16[5,2,2,24,768]{4,3,2,1,0:T(8,128)(2,1)S(1)} %maximum_select_fusion) | copy-start | bytes 2211844
  76.0 22.8 %collective-permute-start.21 = (bf16[1,5,96,768]{3,2,1,0:T(8,128)(2,1)S(1)}, bf16[1,5,96,768]{3,2,1,0:T(8,128)(2,1)S(1)}, u32[]{:S(2)}, u32[]{:S(2)}) collective-permute-start(bf16[1,5,96,768]{3,2,1,0:T(8,128)(2,1)S(1)} %bitcast.126), channel_id=1, source_target_pairs={{0,8},{4,12},{8,0},{12,4},{16,24},{20,28},{24,16},{28,20},{1,9},{5... | collective-permute-start | bytes 2211848 | tf_op jit(solution)/shard_map/swap_more_x1/ppermute | solution.py:442
  100.0 31.9 %copy-start = (f32[4,256,128]{2,1,0:T(8,128)S(1)}, f32[4,256,128]{2,1,0:T(8,128)}, u32[]{:S(2)}) copy-start(f32[4,256,128]{2,1,0:T(8,128)} %get-tuple-element.345.refs_7_.sin_ref) | copy-start | bytes 1572868
  100.0 31.9 %copy-start.1 = (f32[4,256,128]{2,1,0:T(8,128)S(1)}, f32[4,256,128]{2,1,0:T(8,128)}, u32[]{:S(2)}) copy-start(f32[4,256,128]{2,1,0:T(8,128)} %get-tuple-element.346.refs_6_.cos_ref) | copy-start | bytes 1572868
  130.0 19.2 %collective-permute-start.23 = (bf16[2,2,256,768]{3,2,1,0:T(8,128)(2,1)}, bf16[2,2,256,768]{3,2,1,0:T(8,128)(2,1)S(1)}, u32[]{:S(2)}, u32[]{:S(2)}) collective-permute-start(bf16[2,2,256,768]{3,2,1,0:T(8,128)(2,1)} %get-tuple-element.217), channel_id=1, source_target_pairs={{0,4},{4,0},{8,12},{12,8},{16,20},{20,16},{24,28},{28,24},{1,5},{5... | collective-permute-start | bytes 4718600 | tf_op jit(solution)/shard_map/swap_made_c/ppermute | solution.py:442
  130.1 19.1 %collective-permute-start.24 = (bf16[1,5,96,768]{3,2,1,0:T(8,128)(2,1)}, bf16[1,5,96,768]{3,2,1,0:T(8,128)(2,1)S(1)}, u32[]{:S(2)}, u32[]{:S(2)}) collective-permute-start(bf16[1,5,96,768]{3,2,1,0:T(8,128)(2,1)} %get-tuple-element.219), channel_id=1, source_target_pairs={{0,8},{4,12},{8,0},{12,4},{16,24},{20,28},{24,16},{28,20},{1,9},{5... | collective-permute-start | bytes 2211848 | tf_op jit(solution)/shard_map/swap_gmore_x1/ppermute | solution.py:442
  133.3 15.9 %copy-start.32 = (bf16[2,2,256,768]{3,2,1,0:T(8,128)(2,1)S(1)}, bf16[2,2,256,768]{3,2,1,0:T(8,128)(2,1)}, u32[]{:S(2)}) copy-start(bf16[2,2,256,768]{3,2,1,0:T(8,128)(2,1)} %get-tuple-element.229) | copy-start | bytes 4718596
  149.6 8.8 %copy-start.44 = (bf16[1,1,384,768]{3,2,1,0:T(8,128)(2,1)S(1)}, bf16[1,1,384,768]{3,2,1,0:T(8,128)(2,1)}, u32[]{:S(2)}) copy-start(bf16[1,1,384,768]{3,2,1,0:T(8,128)(2,1)} %get-tuple-element.234) | copy-start | bytes 1769476
  149.7 8.8 %copy-start.28 = (bf16[4,2,3,256,128]{4,3,2,1,0:T(8,128)(2,1)S(1)}, bf16[4,2,3,256,128]{4,3,2,1,0:T(8,128)(2,1)}, u32[]{:S(2)}) copy-start(bf16[4,2,3,256,128]{4,3,2,1,0:T(8,128)(2,1)} %get-tuple-element.223.grad_ref) | copy-start | bytes 4718596
  149.7 27.5 %collective-permute-start.25 = (bf16[2,256,768]{2,1,0:T(8,128)(2,1)S(1)}, bf16[2,256,768]{2,1,0:T(8,128)(2,1)S(1)}, u32[]{:S(2)}, u32[]{:S(2)}) collective-permute-start(bf16[2,256,768]{2,1,0:T(8,128)(2,1)S(1)} %fusion.2), channel_id=1, source_target_pairs={{0,16},{4,20},{8,24},{12,28},{16,0},{20,4},{24,8},{28,12},{1,17},{... | collective-permute-start | bytes 2359304 | tf_op jit(solution)/shard_map/swap_made_y/ppermute | solution.py:442
  151.2 21.6 %collective-permute-start.26 = (bf16[5,2,24,768]{3,2,0,1:T(8,128)(2,1)S(1)}, bf16[5,2,24,768]{3,2,0,1:T(8,128)(2,1)S(1)}, u32[]{:S(2)}, u32[]{:S(2)}) collective-permute-start(bf16[5,2,24,768]{3,2,0,1:T(8,128)(2,1)S(1)} %fusion.9), channel_id=1, source_target_pairs={{0,1},{1,0},{2,3},{3,2},{4,5},{5,4},{6,7},{7,6},{8,9},{9,8},{10,11... | collective-permute-start | bytes 1105928 | tf_op jit(solution)/shard_map/swap_gmore_z1/ppermute | solution.py:446
  153.3 19.4 %collective-permute-start.27 = (bf16[4,256,128]{2,1,0:T(8,128)(2,1)S(1)}, bf16[4,256,128]{2,1,0:T(8,128)(2,1)S(1)}, u32[]{:S(2)}, u32[]{:S(2)}) collective-permute-start(bf16[4,256,128]{2,1,0:T(8,128)(2,1)S(1)} %get-tuple-element.227), channel_id=1, source_target_pairs={{0,8},{4,12},{8,0},{12,4},{16,24},{20,28},{24,16},{28,20},{1,9},{5... | collective-permute-start | bytes 786440 | tf_op jit(solution)/shard_map/swap_gkeyval0_x1/ppermute | solution.py:442
  158.5 18.7 %collective-permute-start.28 = (bf16[1,1,384,768]{3,2,1,0:T(8,128)(2,1)S(1)}, bf16[1,1,384,768]{3,2,1,0:T(8,128)(2,1)S(1)}, u32[]{:S(2)}, u32[]{:S(2)}) collective-permute-start(bf16[1,1,384,768]{3,2,1,0:T(8,128)(2,1)S(1)} %copy-done.44), channel_id=1, source_target_pairs={{0,8},{4,12},{8,0},{12,4},{16,24},{20,28},{24,16},{28,20},{1,9},{5... | collective-permute-start | bytes 1769480 | tf_op jit(solution)/shard_map/swap_gdown_x1/ppermute | solution.py:442
  177.2 7.5 %copy-start.21 = (bf16[4,2,256,768]{3,2,1,0:T(8,128)(2,1)S(1)}, bf16[4,2,256,768]{3,2,1,0:T(8,128)(2,1)}, u32[]{:S(2)}) copy-start(bf16[4,2,256,768]{3,2,1,0:T(8,128)(2,1)} %get-tuple-element.240.dnormed_ref) | copy-start | bytes 9437188
  177.4 7.3 %copy-start.24 = (bf16[768,384]{1,0:T(8,128)(2,1)S(1)}, bf16[768,384]{1,0:T(8,128)(2,1)}, u32[]{:S(2)}) copy-start(bf16[768,384]{1,0:T(8,128)(2,1)} %get-tuple-element.178.refs_4_.weight_ref) | copy-start | bytes 1769476
  177.4 7.3 %copy-start.5 = (bf16[1,256,768]{2,1,0:T(8,128)(2,1)S(1)}, bf16[1,256,768]{2,1,0:T(8,128)(2,1)}, u32[]{:S(2)}) copy-start(bf16[1,256,768]{2,1,0:T(8,128)(2,1)} %copy-done.4) | copy-start | bytes 1179652
  177.5 7.3 %copy-start.11 = (bf16[1,256,768]{2,1,0:T(8,128)(2,1)S(1)}, bf16[1,256,768]{2,1,0:T(8,128)(2,1)}, u32[]{:S(2)}) copy-start(bf16[1,256,768]{2,1,0:T(8,128)(2,1)} %copy-done.10) | copy-start | bytes 1179652
  177.6 13.2 %collective-permute-start.29 = (bf16[5,1,24,768]{3,2,0,1:T(8,128)(2,1)S(1)}, bf16[5,1,24,768]{3,2,0,1:T(8,128)(2,1)S(1)}, u32[]{:S(2)}, u32[]{:S(2)}) collective-permute-start(bf16[5,1,24,768]{3,2,0,1:T(8,128)(2,1)S(1)} %dynamic-slice_convert_fusion), channel_id=1, source_target_pairs={{0,2},{1,3},{2,0},{3,1},{4,6},{5,7},{6,4},{7,5},{8,10},{9,11},{10,... | collective-permute-start | bytes 552968 | tf_op jit(solution)/shard_map/swap_gmore_z2/ppermute | solution.py:446
  178.6 12.3 %collective-permute-start.30 = (bf16[4,256,128]{2,1,0:T(8,128)(2,1)S(1)}, bf16[4,256,128]{2,1,0:T(8,128)(2,1)S(1)}, u32[]{:S(2)}, u32[]{:S(2)}) collective-permute-start(bf16[4,256,128]{2,1,0:T(8,128)(2,1)S(1)} %get-tuple-element.251), channel_id=1, source_target_pairs={{0,8},{4,12},{8,0},{12,4},{16,24},{20,28},{24,16},{28,20},{1,9},{5... | collective-permute-start | bytes 786440 | tf_op jit(solution)/shard_map/swap_gkeyval1_x1/ppermute | solution.py:442
  182.7 15.8 %collective-permute-start.33 = (bf16[2,96,768]{2,1,0:T(8,128)(2,1)S(1)}, bf16[2,96,768]{2,1,0:T(8,128)(2,1)S(1)}, u32[]{:S(2)}, u32[]{:S(2)}) collective-permute-start(bf16[2,96,768]{2,1,0:T(8,128)(2,1)S(1)} %fusion.10), channel_id=1, source_target_pairs={{0,1},{1,0},{2,3},{3,2},{4,5},{5,4},{6,7},{7,6},{8,9},{9,8},{10,11... | collective-permute-start | bytes 884744 | tf_op jit(solution)/shard_map/swap_gdown_z1/ppermute | solution.py:446
  190.9 7.6 %collective-permute-start.31 = (bf16[2,256,768]{2,1,0:T(8,128)(2,1)S(1)}, bf16[2,256,768]{2,1,0:T(8,128)(2,1)S(1)}, u32[]{:S(2)}, u32[]{:S(2)}) collective-permute-start(bf16[2,256,768]{2,1,0:T(8,128)(2,1)S(1)} %get-tuple-element.262), channel_id=1, source_target_pairs={{0,4},{4,0},{8,12},{12,8},{16,20},{20,16},{24,28},{28,24},{1,5},{5... | collective-permute-start | bytes 2359304 | tf_op jit(solution)/shard_map/swap_dtokens0_c/ppermute | solution.py:442
  191.0 7.5 %collective-permute-start.32 = (bf16[2,24,768]{2,1,0:T(8,128)(2,1)S(1)}, bf16[2,24,768]{2,1,0:T(8,128)(2,1)S(1)}, u32[]{:S(2)}, u32[]{:S(2)}) collective-permute-start(bf16[2,24,768]{2,1,0:T(8,128)(2,1)S(1)} %fusion.14), channel_id=1, source_target_pairs={{0,4},{4,0},{8,12},{12,8},{16,20},{20,16},{24,28},{28,24},{1,5},{5... | collective-permute-start | bytes 221192 | tf_op jit(solution)/shard_map/swap_gup_c/ppermute | solution.py:442
  198.5 11.9 %collective-permute-start.34 = (bf16[1,4,96,384]{3,2,1,0:T(8,128)(2,1)S(1)}, bf16[1,4,96,384]{3,2,1,0:T(8,128)(2,1)S(1)}, u32[]{:S(2)}, u32[]{:S(2)}) collective-permute-start(bf16[1,4,96,384]{3,2,1,0:T(8,128)(2,1)S(1)} %get-tuple-element.269), channel_id=1, source_target_pairs={{0,8},{4,12},{8,0},{12,4},{16,24},{20,28},{24,16},{28,20},{1,9},{5... | collective-permute-start | bytes 884744 | tf_op jit(solution)/shard_map/swap_gfront_x1/ppermute | solution.py:442
  199.8 10.6 %collective-permute-start.35 = (bf16[2,256,768]{2,1,0:T(8,128)(2,1)S(1)}, bf16[2,256,768]{2,1,0:T(8,128)(2,1)S(1)}, u32[]{:S(2)}, u32[]{:S(2)}) collective-permute-start(bf16[2,256,768]{2,1,0:T(8,128)(2,1)S(1)} %get-tuple-element.270), channel_id=1, source_target_pairs={{0,4},{4,0},{8,12},{12,8},{16,20},{20,16},{24,28},{28,24},{1,5},{5... | collective-permute-start | bytes 2359304 | tf_op jit(solution)/shard_map/swap_dtokens1_c/ppermute | solution.py:442
  199.9 9.7 %collective-permute-start.42 = (bf16[1,96,768]{2,1,0:T(8,128)(2,1)S(1)}, bf16[1,96,768]{2,1,0:T(8,128)(2,1)S(1)}, u32[]{:S(2)}, u32[]{:S(2)}) collective-permute-start(bf16[1,96,768]{2,1,0:T(8,128)(2,1)S(1)} %dynamic-slice_convert_fusion.1), channel_id=1, source_target_pairs={{0,2},{1,3},{2,0},{3,1},{4,6},{5,7},{6,4},{7,5},{8,10},{9,11},{10,... | collective-permute-start | bytes 442376 | tf_op jit(solution)/shard_map/swap_gdown_z2/ppermute | solution.py:446
  200.3 13.2 %collective-permute-start.37 = (bf16[256,768]{1,0:T(8,128)(2,1)S(1)}, bf16[256,768]{1,0:T(8,128)(2,1)S(1)}, u32[]{:S(2)}, u32[]{:S(2)}) collective-permute-start(bf16[256,768]{1,0:T(8,128)(2,1)S(1)} %fusion.7), channel_id=1, source_target_pairs={{0,16},{4,20},{8,24},{12,28},{16,0},{20,4},{24,8},{28,12},{1,17},{... | collective-permute-start | bytes 1179656 | tf_op jit(solution)/shard_map/swap_dtokens0_y/ppermute | solution.py:442
  201.6 11.9 %collective-permute-start.38 = (bf16[24,1536]{1,0:T(8,128)(2,1)S(1)}, bf16[24,1536]{1,0:T(8,128)(2,1)S(1)}, u32[]{:S(2)}, u32[]{:S(2)}) collective-permute-start(bf16[24,1536]{1,0:T(8,128)(2,1)S(1)} %fusion.15), channel_id=1, source_target_pairs={{0,16},{4,20},{8,24},{12,28},{16,0},{20,4},{24,8},{28,12},{1,17},{... | collective-permute-start | bytes 221192 | tf_op jit(solution)/shard_map/swap_gup_y/ppermute | solution.py:442
  210.5 5.9 %collective-permute-start.36 = (bf16[4,2,24,384]{3,2,0,1:T(8,128)(2,1)S(1)}, bf16[4,2,24,384]{3,2,0,1:T(8,128)(2,1)S(1)}, u32[]{:S(2)}, u32[]{:S(2)}) collective-permute-start(bf16[4,2,24,384]{3,2,0,1:T(8,128)(2,1)S(1)} %fusion.11), channel_id=1, source_target_pairs={{0,1},{1,0},{2,3},{3,2},{4,5},{5,4},{6,7},{7,6},{8,9},{9,8},{10,11... | collective-permute-start | bytes 442376 | tf_op jit(solution)/shard_map/swap_gfront_z1/ppermute | solution.py:446
  210.8 2.0 collective-permute-start.41
  211.5 12.3 %collective-permute-start.40 = (bf16[256,768]{1,0:T(8,128)(2,1)S(1)}, bf16[256,768]{1,0:T(8,128)(2,1)S(1)}, u32[]{:S(2)}, u32[]{:S(2)}) collective-permute-start(bf16[256,768]{1,0:T(8,128)(2,1)S(1)} %fusion.8), channel_id=1, source_target_pairs={{0,16},{4,20},{8,24},{12,28},{16,0},{20,4},{24,8},{28,12},{1,17},{... | collective-permute-start | bytes 1179656 | tf_op jit(solution)/shard_map/swap_dtokens1_y/ppermute | solution.py:442
  216.4 7.4 %collective-permute-start.39 = (bf16[4,1,24,384]{3,2,0,1:T(8,128)(2,1)S(1)}, bf16[4,1,24,384]{3,2,0,1:T(8,128)(2,1)S(1)}, u32[]{:S(2)}, u32[]{:S(2)}) collective-permute-start(bf16[4,1,24,384]{3,2,0,1:T(8,128)(2,1)S(1)} %dynamic-slice_convert_fusion.2), channel_id=1, source_target_pairs={{0,2},{1,3},{2,0},{3,1},{4,6},{5,7},{6,4},{7,5},{8,10},{9,11},{10,... | collective-permute-start | bytes 221192 | tf_op jit(solution)/shard_map/swap_gfront_z2/ppermute | solution.py:446
  223.9 2.5 %collective-permute-start.43 = (bf16[2,24,384]{2,1,0:T(8,128)(2,1)S(1)}, bf16[2,24,384]{2,1,0:T(8,128)(2,1)S(1)}, u32[]{:S(2)}, u32[]{:S(2)}) collective-permute-start(bf16[2,24,384]{2,1,0:T(8,128)(2,1)S(1)} %fusion.16), channel_id=1, source_target_pairs={{0,4},{4,0},{8,12},{12,8},{16,20},{20,16},{24,28},{28,24},{1,5},{5... | collective-permute-start | bytes 110600 | tf_op jit(solution)/shard_map/swap_gfront_c/ppermute | solution.py:442
  226.6 4.0 %collective-permute-start.44 = (bf16[24,516]{1,0:T(8,128)(2,1)S(1)}, bf16[24,516]{1,0:T(8,128)(2,1)S(1)}, u32[]{:S(2)}, u32[]{:S(2)}) collective-permute-start(bf16[24,516]{1,0:T(8,128)(2,1)S(1)} %fusion.18), channel_id=1, source_target_pairs={{0,16},{4,20},{8,24},{12,28},{16,0},{20,4},{24,8},{28,12},{1,17},{... | collective-permute-start | bytes 74312 | tf_op jit(solution)/shard_map/swap_gfront_y/ppermute | solution.py:442
  (28 other events, 111.8 us)
